TPU v7x, 32 devices: a whole 2x2x4 slice. The times are simulated.
32 devices in a mesh: fsdp: 16 (over z, x, core), island: 2 (over y).
Axes of the slice: x: 2, y: 2, z: 4, core: 2. Of those that a mesh axis runs over, the one named last changes fastest.
Arguments:
- activations: bfloat16 [2, 2048, 4224], P('island', 'fsdp'), may hold values from -6 to 6
- out_grads: bfloat16 [2, 2048, 512], P('island', 'fsdp'), may hold values from -0.13183594 to 0.13183594
- projection: bfloat16 [4224, 256], P('fsdp'), may hold values from -0.09375 to 0.09375
- first_moment: float32 [2, 1, 256, 512], P('island'), may hold values from -1.8 to 1.8
- second_moment: float32 [2, 1, 256, 512], P('island'), may hold values from 0.01 to 1
- inner_weights: float32 [2, 4224, 512], P('island', 'fsdp'), may hold values from -6 to 6
- global_weights: float32 [4224, 512], P('fsdp'), may hold values from -6 to 6
- outer_momentum: float32 [4224, 512], P('fsdp'), may hold values from -6 to 6
Outputs:
- new_weights: bfloat16 [4224, 512], P('fsdp', 'island')
- new_momentum: float32 [4224, 512], P('fsdp')
- new_first: float32 [2, 1, 256, 512], P('island')
- new_second: float32 [2, 1, 256, 512], P('island')
All inputs are finite; a program needn't handle non-finite values.
Results may differ from a plain program's by a relative error of at most 0.001.
Values sent between devices are 32-bit elements; how exact they have to be, the bound alone decides.
No kernel may reach another device: no remote copies, remote signals or barrier semaphores. Data moves between devices by JAX's collectives and lax.ppermute only.
A program may use at most 64 MiB of HBM per device.

v0:
```python
import jax
import jax.numpy as jnp
from jax import lax
from jax.sharding import PartitionSpec as P

DW = 4224
RANK = 256
LAYERS = 1


first_decay = 0.9
second_decay = 0.999
first_fix = 1.0 - 0.9**10
second_fix = 1.0 - 0.999**10
epsilon = 1e-08
inner_rate = 1.0
outer_rate = 0.7
outer_beta = 0.9


def layer_select(first_row, row_count):
    layer_of = (first_row + lax.iota(jnp.int32, row_count)) // DW
    return (layer_of[:, None] == lax.iota(jnp.int32, LAYERS)[None, :]).astype(jnp.float32)


def outer_step(stepped_sum, global_part, momentum_part, island_count):
    pseudo_grad = global_part - stepped_sum / island_count
    momentum_next = outer_beta * momentum_part + pseudo_grad
    weights_next = (global_part - outer_rate * (pseudo_grad + outer_beta * momentum_next)).astype(
        jnp.bfloat16
    )
    return (weights_next, momentum_next)


def body(
    activations,
    out_grads,
    projection,
    first_moment,
    second_moment,
    inner_weights,
    global_weights,
    outer_momentum,
):
    inputs = activations[0]
    grads_out = out_grads[0]
    row_count = projection.shape[0]
    col_total = global_weights.shape[1]
    product = lax.dot_general(
        inputs, grads_out, (((0,), (0,)), ((), ())), preferred_element_type=jnp.float32
    )
    grad_rows = lax.psum_scatter(product, "fsdp", scatter_dimension=0, tiled=True)
    first_row = lax.axis_index("fsdp") * row_count
    select = layer_select(first_row, row_count)
    lifted = (projection.astype(jnp.float32)[:, None, :] * select[:, :, None]).reshape(
        row_count, LAYERS * RANK
    )
    partial_sum = lax.dot_general(
        lifted,
        grad_rows,
        (((0,), (0,)), ((), ())),
        precision=lax.Precision.HIGHEST,
        preferred_element_type=jnp.float32,
    )
    projected = lax.psum(partial_sum, "fsdp").reshape(LAYERS, RANK, col_total)
    new_first = first_decay * first_moment[0] + (1.0 - first_decay) * projected
    new_second = second_decay * second_moment[0] + (1.0 - second_decay) * projected * projected
    adapted = new_first / first_fix / (jnp.sqrt(new_second / second_fix) + epsilon)
    channel_scale = jnp.sqrt(jnp.mean(adapted * adapted, axis=1)) / jnp.sqrt(
        jnp.mean(projected * projected, axis=1) + 1e-06
    )
    row_scale = jnp.sum(select[:, :, None] * channel_scale[None, :, :], axis=1)
    stepped = inner_weights[0] - inner_rate * grad_rows * row_scale
    island_count = lax.axis_size("island")
    block_cols = col_total // island_count
    block_start = lax.axis_index("island") * block_cols
    share_total = lax.psum_scatter(stepped, "island", scatter_dimension=1, tiled=True)
    global_part = lax.dynamic_slice_in_dim(global_weights, block_start, block_cols, 1)
    momentum_part = lax.dynamic_slice_in_dim(outer_momentum, block_start, block_cols, 1)
    weights_block, momentum_block = outer_step(
        share_total, global_part, momentum_part, island_count
    )
    new_momentum = lax.all_gather(momentum_block, "island", axis=1, tiled=True)
    return (weights_block, new_momentum, new_first[None], new_second[None])


def solution(mesh):
    placed = (
        P("island", "fsdp", None),
        P("island", "fsdp", None),
        P("fsdp", None),
        P("island", None, None, None),
        P("island", None, None, None),
        P("island", "fsdp", None),
        P("fsdp", None),
        P("fsdp", None),
    )
    return jax.shard_map(
        body,
        mesh=mesh,
        in_specs=placed,
        out_specs=(
            P("fsdp", "island"),
            P("fsdp", None),
            P("island", None, None, None),
            P("island", None, None, None),
        ),
        check_vma=False,
    )
```

profile of v0, /device:TPU:0, one launch (start us, length us, event | category | flops | bytes accessed | tf_op | source)
XLA Modules:
  0.0 254.7 jit_solution(17458650715682141211)
XLA Ops:
  7.2 0.0 copy-start
  7.2 0.0 reduce-scatter.3.cloned.1.call-start
  7.2 1.2 copy-done
  8.4 5.5 %fusion = f32[4224,512]{1,0:T(8,128)} fusion(bf16[1,128,4224]{2,1,0:T(8,128)(2,1)S(1)} %copy-done, bf16[1,128,512]{2,1,0:T(8,128)(2,1)} %param.9), kind=kOutput, calls=%fused_computation | convolution fusion | flops 553648128 | bytes 9863168 | tf_op jit(solution)/shard_map/dot_general | solution.py:49
  13.9 0.0 copy-start.5
  13.9 0.0 reduce-scatter.3.cloned.1.call-update
  14.0 0.0 copy-start.3
  14.0 0.0 copy-start.4
  14.0 0.0 all-reduce.2.cloned.1.call-start
  14.1 109.9 %reduce-scatter.3.cloned.1.call-done = f32[264,512]{1,0:T(8,128)} async-done(((f32[4224,512]{1,0:T(8,128)}), f32[264,512]{1,0:T(8,128)}) %reduce-scatter.3.cloned.1.call-update) | async-done | bytes 540688 | tf_op jit(solution)/shard_map/reduce_scatter | solution.py:52
  124.0 0.0 copy-done.5
  124.0 3.0 %fusion.3 = f32[256,512]{1,0:T(8,128)} fusion(f32[264,512]{1,0:T(8,128)} %reduce-scatter.3.cloned.1.call-done, bf16[264,256]{1,0:T(8,128)(2,1)S(1)} %copy-done.5, f32[264]{0:T(512)S(1)} %fusion.11), kind=kOutput, calls=%fused_computation.11 | convolution fusion | flops 415371264 | bytes 1201184 | tf_op jit(solution)/shard_map/dot_general | solution.py:58
  127.1 0.0 all-reduce.2.cloned.1.call-update
  127.1 0.0 copy-start.1
  127.1 0.0 copy-start.2
  127.1 0.0 reduce-scatter.5.cloned.1.call-start
  127.2 90.7 %all-reduce.2.cloned.1.call-done = f32[256,512]{1,0:T(8,128)} async-done(((f32[256,512]{1,0:T(8,128)}), f32[256,512]{1,0:T(8,128)}) %all-reduce.2.cloned.1.call-update) | async-done | bytes 524304 | tf_op jit(solution)/shard_map/psum | solution.py:65
  217.9 0.0 copy-done.3
  217.9 0.0 copy-done.4
  217.9 2.4 multiply_reduce_fusion.1
  220.3 0.0 copy-done.1
  220.3 0.0 copy-done.2
  220.3 0.0 copy-start.6
  220.3 0.9 bitcast_subtract_fusion
  221.3 0.0 reduce-scatter.5.cloned.1.call-update
  221.3 15.4 %reduce-scatter.5.cloned.1.call-done = f32[264,256]{1,0:T(8,128)} async-done(((f32[264,512]{1,0:T(8,128)}), f32[264,256]{1,0:T(8,128)}) %reduce-scatter.5.cloned.1.call-update) | async-done | bytes 270352 | tf_op jit(solution)/shard_map/reduce_scatter | solution.py:77
  236.7 0.0 copy-done.6
  236.7 1.8 subtract_convert_fusion
  238.4 8.9 %all_gather.3 = f32[264,512]{1,0:T(8,128)S(1)} all-gather(f32[264,256]{1,0:T(8,128)S(1)} %get-tuple-element.7), channel_id=1, replica_groups=mesh['fsdp'=16,'island'=2] {'island'}, dimensions={1}, use_global_device_ids=true | all-gather | bytes 811008 | tf_op jit(solution)/shard_map/all_gather | solution.py:83
  247.3 0.8 copy.14
  (2 shorter events, 0.0 us)
Async XLA Ops:
  7.2 1.2 copy-start
  7.2 116.8 %reduce-scatter.3.cloned.1.call-start = ((), (), s32[]{:S(2)}) async-start(), calls=%async_computation.2 | async-start | bytes 9191424 | tf_op jit(solution)/shard_map/reduce_scatter | solution.py:52
  13.9 110.1 %copy-start.5 = (bf16[264,256]{1,0:T(8,128)(2,1)S(1)}, bf16[264,256]{1,0:T(8,128)(2,1)}, u32[]{:S(2)}) copy-start(bf16[264,256]{1,0:T(8,128)(2,1)} %param.10) | copy-start | bytes 405508
  14.0 203.9 %copy-start.3 = (f32[1,1,256,512]{3,2,1,0:T(8,128)S(1)}, f32[1,1,256,512]{3,2,1,0:T(8,128)}, u32[]{:S(2)}) copy-start(f32[1,1,256,512]{3,2,1,0:T(8,128)} %param.11) | copy-start | bytes 1572868
  14.0 203.9 %copy-start.4 = (f32[1,1,256,512]{3,2,1,0:T(8,128)S(1)}, f32[1,1,256,512]{3,2,1,0:T(8,128)}, u32[]{:S(2)}) copy-start(f32[1,1,256,512]{3,2,1,0:T(8,128)} %param.12) | copy-start | bytes 1572868
  14.0 203.9 %all-reduce.2.cloned.1.call-start = ((), (), s32[]{:S(2)}) async-start(), calls=%async_computation.3 | async-start | bytes 1048576 | tf_op jit(solution)/shard_map/psum | solution.py:65
  127.1 93.2 %copy-start.1 = (f32[264,512]{1,0:T(8,128)S(1)}, f32[264,512]{1,0:T(8,128)}, u32[]{:S(2)}) copy-start(f32[264,512]{1,0:T(8,128)} %reduce-scatter.3.cloned.1.call-done) | copy-start | bytes 1622020
  127.1 93.2 %copy-start.2 = (f32[1,264,512]{2,1,0:T(8,128)S(1)}, f32[1,264,512]{2,1,0:T(8,128)}, u32[]{:S(2)}) copy-start(f32[1,264,512]{2,1,0:T(8,128)} %param.13) | copy-start | bytes 1622020
  127.1 109.6 %reduce-scatter.5.cloned.1.call-start = ((), (), s32[]{:S(2)}) async-start(), calls=%async_computation.4 | async-start | bytes 811008 | tf_op jit(solution)/shard_map/reduce_scatter | solution.py:77
  220.3 16.4 %copy-start.6 = (f32[264,512]{1,0:T(8,128)S(1)}, f32[264,512]{1,0:T(8,128)}, u32[]{:S(2)}) copy-start(f32[264,512]{1,0:T(8,128)} %param.14) | copy-start | bytes 1622020
Sparse Core Ops, SparseCore 0:
  14.1 109.8 reduce-scatter.2
  128.0 89.8 all-reduce.1
  221.4 15.2 reduce-scatter.4
where the time goes:
time: 255 us
  waiting for transfers between devices  216 us (85%)
  between operations  13.8 us (5%)
  blocking collectives  8.9 us (3%)
  matrix products  8.57 us (3%)
  other arithmetic  5.12 us (2%)
    reduce_scatter x1, waiting for transfers between devices, body(): lax.psum_scatter(product, 'fsdp', scatter_dimension=0, tiled=True)  110 us
    psum x1, waiting for transfers between devices, body(): projected = lax.psum(partial_sum, 'fsdp').reshape(LAYERS, RANK, col_total)  90.7 us
    reduce_scatter x1, waiting for transfers between devices, body(): lax.psum_scatter(stepped, 'island', scatter_dimension=1, tiled=True)  15.4 us
    all_gather x1, blocking collectives, body(): new_momentum = lax.all_gather(momentum_block, 'island', axis=1, tiled=True)  8.9 us
    dot_general x1, matrix products, body(): lax.dot_general(inputs, grads_out, (((0,), (0,)), ((), ())), preferred_el...  5.53 us
  transfers between devices with their start and end apart: 3, of which 3 were waited for; matrix products, arithmetic and copies ran while one was open for 0% of the time, Pallas kernels for 0%

commit v1 on v0

v1 whole, which is shorter than its diff:
```python
import jax
import jax.numpy as jnp
from jax import lax
from jax.experimental import pallas as pl
from jax.experimental.pallas import tpu as pltpu
from jax.sharding import PartitionSpec as P

first_decay = 0.9
second_decay = 0.999
first_fix = 1.0 - 0.9**10
second_fix = 1.0 - 0.999**10
epsilon = 1e-08
inner_rate = 1.0
outer_rate = 0.7
outer_beta = 0.9


def outer_step(stepped_sum, global_part, momentum_part, island_count):
    pseudo_grad = global_part - stepped_sum / island_count
    momentum_next = outer_beta * momentum_part + pseudo_grad
    weights_next = (global_part - outer_rate * (pseudo_grad + outer_beta * momentum_next)).astype(
        jnp.bfloat16
    )
    return (weights_next, momentum_next)


def moments_and_scale(projected, first, second):
    new_first = first_decay * first + (1.0 - first_decay) * projected
    new_second = second_decay * second + (1.0 - second_decay) * projected * projected
    adapted = new_first / first_fix / (jnp.sqrt(new_second / second_fix) + epsilon)
    scale = jnp.sqrt(jnp.mean(adapted * adapted, axis=0, keepdims=True)) / jnp.sqrt(
        jnp.mean(projected * projected, axis=0, keepdims=True) + 1e-06
    )
    return new_first, new_second, scale


def plain_body(
    activations,
    out_grads,
    projection,
    first_moment,
    second_moment,
    inner_weights,
    global_weights,
    outer_momentum,
):
    col_total = global_weights.shape[1]
    product = lax.dot_general(
        activations[0],
        out_grads[0],
        (((0,), (0,)), ((), ())),
        preferred_element_type=jnp.float32,
    )
    grad_rows = lax.psum_scatter(product, "fsdp", scatter_dimension=0, tiled=True)
    partial_sum = lax.dot_general(
        projection.astype(jnp.float32),
        grad_rows,
        (((0,), (0,)), ((), ())),
        precision=lax.Precision.HIGHEST,
        preferred_element_type=jnp.float32,
    )
    projected = lax.psum(partial_sum, "fsdp")
    new_first, new_second, scale = moments_and_scale(
        projected, first_moment[0, 0], second_moment[0, 0]
    )
    stepped = inner_weights[0] - inner_rate * grad_rows * scale
    island_count = lax.axis_size("island")
    block_cols = col_total // island_count
    block_start = lax.axis_index("island") * block_cols
    share_total = lax.psum_scatter(stepped, "island", scatter_dimension=1, tiled=True)
    global_part = lax.dynamic_slice_in_dim(global_weights, block_start, block_cols, 1)
    momentum_part = lax.dynamic_slice_in_dim(outer_momentum, block_start, block_cols, 1)
    weights_block, momentum_block = outer_step(
        share_total, global_part, momentum_part, island_count
    )
    new_momentum = lax.all_gather(momentum_block, "island", axis=1, tiled=True)
    return (weights_block, new_momentum, new_first[None, None], new_second[None, None])


def product_kernel(
    at, own_a, core_a, crossed_a, own_g, core_g, side_g, far_g, out
):
    pieces = (
        (own_a[0, 0], own_g),
        (core_a[0, 0], core_g),
        (crossed_a[0], side_g),
        (crossed_a[1], far_g),
    )
    out[...] = sum(
        jnp.dot(
            a.astype(jnp.bfloat16),
            g[...].astype(jnp.bfloat16),
            preferred_element_type=jnp.float32,
        )
        for a, g in pieces
    )


def block_product(at, own_a, core_a, crossed_a, grads):
    rows, tokens = own_a.shape[2:]
    cols = grads[0].shape[1]
    picked = pl.BlockSpec((1, 1, rows, tokens), lambda i, at: (at[0], at[1], 0, 0))
    whole = pl.BlockSpec((tokens, cols), lambda i, at: (0, 0))
    return pl.pallas_call(
        product_kernel,
        out_shape=jax.ShapeDtypeStruct((rows, cols), jnp.float32),
        grid_spec=pltpu.PrefetchScalarGridSpec(
            num_scalar_prefetch=1,
            grid=(1,),
            in_specs=[
                picked,
                picked,
                pl.BlockSpec((2, rows, tokens), lambda i, at: (0, 0, 0)),
                whole,
                whole,
                whole,
                whole,
            ],
            out_specs=pl.BlockSpec((rows, cols), lambda i, at: (0, 0)),
        ),
        compiler_params=pltpu.CompilerParams(vmem_limit_bytes=24 * 1024 * 1024),
        cost_estimate=pl.CostEstimate(
            flops=8 * rows * tokens * cols,
            bytes_accessed=4 * (4 * tokens * (rows + cols) + rows * cols),
            transcendentals=0,
        ),
    )(at, own_a, core_a, crossed_a, *grads)


def line_body(
    activations,
    out_grads,
    projection,
    first_moment,
    second_moment,
    inner_weights,
    global_weights,
    outer_momentum,
):
    fsdp = lax.axis_size("fsdp")
    line = fsdp // 4
    me = lax.axis_index("fsdp")
    place, side, core = me // 4, (me // 2) % 2, me % 2
    at_end = (place == 0) | (place == line - 1)
    rows = projection.shape[0]
    tokens, features = activations.shape[1:]
    cols = global_weights.shape[1]
    rank = projection.shape[1]

    def move(value, target):
        pairs = []
        for f in range(fsdp):
            to = target(f // 4, (f // 2) % 2, f % 2)
            if to is not None:
                pairs.append((f, (to[0] * 2 + to[1]) * 2 + to[2]))
        return lax.ppermute(value, "fsdp", pairs)

    def to_core(value):
        return move(value, lambda l, x, c: (l, x, 1 - c))

    def to_side(value):
        return move(value, lambda l, x, c: (l, 1 - x, c))

    def to_place(value, mask):
        return move(value, lambda l, x, c: (l ^ mask, x, c))

    def inward(value, depth):
        def target(l, x, c):
            if l == depth:
                return (l + 1, x, c)
            if l == line - 1 - depth:
                return (l - 1, x, c)
            return None

        return move(value, target)

    def to_island(value):
        return lax.ppermute(value, "island", [(0, 1), (1, 0)])

    grads_own = out_grads[0].astype(jnp.float32)
    grads_side = to_side(grads_own)

    turned = lax.dot_general(
        activations[0],
        jnp.eye(tokens, dtype=activations.dtype),
        (((0,), (0,)), ((), ())),
        preferred_element_type=jnp.float32,
    ).reshape(line, 2, 2, rows, tokens)
    kept = lax.dynamic_index_in_dim(turned, core, 2, keepdims=False)
    from_core = to_core(lax.dynamic_index_in_dim(turned, 1 - core, 2, keepdims=False))
    grads_core = to_core(grads_own)
    grads_far = to_core(grads_side)

    table = []
    for l in range(line):
        needed = []
        for b in range(line):
            depth, hops = (l, b - l) if b > l else (line - 1 - l, l - b)
            needed.append((line - hops if hops else line + 1, depth, b))
        table.append([b for _, _, b in sorted(needed)])
    order = jnp.array(table, jnp.int32)[place]

    def block(stack, k, which):
        return lax.dynamic_slice(stack, (order[k], which, 0, 0), (1, 1, rows, tokens))[0, 0]

    proj_own = projection.astype(jnp.float32)
    proj_in = inward(proj_own, 0)
    proj_mid = inward(proj_own, 1)
    proj_mid2 = inward(proj_in, 1)
    proj_out = inward(jnp.stack([proj_own, proj_mid]), 2)
    proj_out2 = inward(proj_mid2, 2)
    proj_order = [
        jnp.where(at_end, proj_out2, proj_mid2),
        jnp.where(at_end, proj_out[1], proj_mid),
        jnp.where(at_end, proj_out[0], proj_in),
        proj_own,
    ]

    grads = (grads_own, grads_core, grads_side, grads_far)
    products = []
    for k in range(line):
        crossed = to_side(
            jnp.stack([block(kept, k, 1 - side), block(from_core, k, 1 - side)])
        )
        at = jnp.stack([order[k], side]).astype(jnp.int32)
        products.append(block_product(at, kept, from_core, crossed, grads))

    e1 = inward(products[0], 0)
    m1 = inward(products[0] + e1, 1)
    e2 = inward(products[1], 0)
    m2 = inward(products[1] + e2, 1)
    o1 = inward(products[2] + m1, 2)
    e3 = inward(products[2], 0)
    grad_rows = products[3] + e3 + m2 + o1

    partial = sum(
        lax.dot_general(
            products[k],
            proj_order[k],
            (((0,), (0,)), ((), ())),
            precision=lax.Precision.HIGH,
            preferred_element_type=jnp.float32,
        )
        for k in range(line)
    )

    def halve(value, bit, exchange):
        half = value.shape[0] // 2
        mine = lax.dynamic_slice_in_dim(value, bit * half, half, 0)
        other = lax.dynamic_slice_in_dim(value, (1 - bit) * half, half, 0)
        return mine + exchange(other)

    def double(value, bit, exchange):
        other = exchange(value)
        return jnp.where(
            bit == 0,
            jnp.concatenate([value, other]),
            jnp.concatenate([other, value]),
        )

    stages = (
        (core, to_core),
        (side, to_side),
        (place // 2, lambda v: to_place(v, 2)),
        (place % 2, lambda v: to_place(v, 1)),
    )
    for bit, exchange in stages:
        partial = halve(partial, bit, exchange)
    for bit, exchange in reversed(stages):
        partial = double(partial, bit, exchange)
    projected = partial.T

    new_first, new_second, scale = moments_and_scale(
        projected, first_moment[0, 0], second_moment[0, 0]
    )

    island = lax.axis_index("island")

    def ordered(own, other):
        return jnp.where(island == 0, own, other), jnp.where(island == 0, other, own)

    inner = inner_weights[0]
    inner0, inner1 = ordered(inner, to_island(inner))
    grad0, grad1 = ordered(grad_rows, to_island(grad_rows))
    scale0, scale1 = ordered(scale, to_island(scale))
    total = (inner0 - inner_rate * grad0 * scale0) + (inner1 - inner_rate * grad1 * scale1)
    weights, new_momentum = outer_step(total, global_weights, outer_momentum, 2)
    half_cols = cols // 2
    weights_block = lax.dynamic_slice_in_dim(weights, island * half_cols, half_cols, 1)
    return (weights_block, new_momentum, new_first[None, None], new_second[None, None])


def solution(mesh):
    placed = (
        P("island", "fsdp", None),
        P("island", "fsdp", None),
        P("fsdp", None),
        P("island", None, None, None),
        P("island", None, None, None),
        P("island", "fsdp", None),
        P("fsdp", None),
        P("fsdp", None),
    )
    lined = mesh.shape["fsdp"] == 4 * 4 and mesh.shape["island"] == 2
    return jax.shard_map(
        line_body if lined else plain_body,
        mesh=mesh,
        in_specs=placed,
        out_specs=(
            P("fsdp", "island"),
            P("fsdp", None),
            P("island", None, None, None),
            P("island", None, None, None),
        ),
        check_vma=False,
    )
```

time: 255 us -> 155 us (0.61)
  waiting for transfers between devices: 216 us -> 41.4 us
  starting transfers between devices: 0.12 us -> 55.6 us
  local copies, waits for them, and re-layouts: 2.02 us -> 16.9 us
  other arithmetic: 5.12 us -> 16.9 us
  blocking collectives: 8.9 us -> 0 us
  Pallas kernels: 0 us -> 8.47 us
  between operations: 13.8 us -> 8.87 us
  matrix products: 8.57 us -> 6 us
    reduce_scatter x2 -> x0, waiting for transfers between devices: 125 us -> none  [the longest x1 110 us: body(): lax.psum_scatter(product, 'fsdp', scatter_dimension=0, tiled=True)]
    psum x1 -> x0, waiting for transfers between devices: 90.7 us -> none  [body(): projected = lax.psum(partial_sum, 'fsdp').reshape(LAYERS, RANK, col_total)]
    ppermute x0 -> x30, starting transfers between devices: none -> 55.6 us  [the longest x27 51.9 us: move(): return lax.ppermute(value, 'fsdp', pairs)]
    ppermute x0 -> x30, waiting for transfers between devices: none -> 41.4 us  [the longest x27 29.3 us: move(): return lax.ppermute(value, 'fsdp', pairs)]
    all_gather x1 -> x0, blocking collectives: 8.9 us -> none  [body(): new_momentum = lax.all_gather(momentum_block, 'island', axis=1, tiled=True)]
    another operation x0 -> x10, other arithmetic: none -> 8.86 us  [the longest x4 3.42 us: line_body(): jnp.stack([block(kept, k, 1 - side), block(from_core, k, 1 - side)])]
    pallas_call x0 -> x4, Pallas kernels: none -> 8.47 us  [block_product(): pl.pallas_call(product_kernel, out_shape=jax.ShapeDtypeStruct((rows, cols...]
    add x0 -> x9, other arithmetic: none -> 6.52 us  [the longest x1 1.93 us: outer_step(): momentum_next = outer_beta * momentum_part + pseudo_grad]
  transfers between devices with their start and end apart: 3 -> 30, of which waited for: 3 -> 9; matrix products, arithmetic and copies ran while one was open for 0% -> 19% of each run, Pallas kernels for 0% -> 5%
where the time goes in v1:
time: 155 us; the launch traced here: 154 us
  starting transfers between devices  55.6 us (36%)
  waiting for transfers between devices  41.4 us (27%)
  local copies, waits for them, and re-layouts  16.9 us (11%)
  other arithmetic  16.9 us (11%)
  between operations  8.87 us (6%)
  Pallas kernels  8.47 us (5%)
  matrix products  6 us (4%)
    ppermute x27, starting transfers between devices, move(): return lax.ppermute(value, 'fsdp', pairs)  51.9 us
    ppermute x27, waiting for transfers between devices, move(): return lax.ppermute(value, 'fsdp', pairs)  29.3 us
    ppermute x3, waiting for transfers between devices, to_island(): return lax.ppermute(value, 'island', [(0, 1), (1, 0)])  12.1 us
    pallas_call x4, Pallas kernels, block_product(): pl.pallas_call(product_kernel, out_shape=jax.ShapeDtypeStruct((rows, cols...  8.47 us
    unnamed x40, local copies, waits for them, and re-layouts  7.47 us
    dot_general x4, matrix products, line_body(): lax.dot_general(products[k], proj_order[k], (((0,), (0,)), ((), ())), pre...  5.52 us
    ppermute x3, starting transfers between devices, to_island(): return lax.ppermute(value, 'island', [(0, 1), (1, 0)])  3.67 us
    another operation x4, other arithmetic, line_body(): jnp.stack([block(kept, k, 1 - side), block(from_core, k, 1 - side)])  3.42 us
  transfers between devices with their start and end apart: 30, of which 9 were waited for; matrix products, arithmetic and copies ran while one was open for 19% of the time, Pallas kernels for 5%

profile of v1, /device:TPU:0, one launch (start us, length us, event | category | flops | bytes accessed | tf_op | source)
XLA Modules:
  0.0 154.2 jit_solution(5748250553586105687)
XLA Ops:
  0.7 1.2 copy-done
  2.4 2.0 %copy.23 = f32[4224,128]{1,0:T(8,128)} copy(f32[4224,128]{0,1:T(8,128)S(1)} %convolution_bitcast_fusion) | data formatting | bytes 4325376 | tf_op jit(solution)/shard_map/dot_general | solution.py:183
  4.3 2.7 %dynamic-slice_bitcast_fusion = (f32[4,2,264,128]{3,2,1,0:T(8,128)}, f32[4,2,264,128]{3,2,1,0:T(8,128)S(1)}) fusion(f32[4,2,2,264,128]{4,3,2,1,0:T(8,128)} %bitcast.88, s32[]{:T(128)S(6)} %select_n.188, s32[]{:T(128)S(6)} %select_n.187), kind=kLoop, calls=%fused_computation.5 | loop fusion | bytes 4325384 | tf_op jit(solution)/shard_map/jit(dynamic_index_in_dim)/squeeze | solution.py:190
  7.5 2.6 %collective-permute-start.4 = (f32[128,512]{1,0:T(8,128)S(1)}, f32[128,512]{1,0:T(8,128)}, u32[]{:S(2)}, u32[]{:S(2)}) collective-permute-start(f32[128,512]{1,0:T(8,128)S(1)} %bitcast_convert_fusion.own_g), channel_id=1, source_target_pairs={{0,4},{2,6},{4,0},{6,2},{8,12},{10,14},{12,8},{14,10},{16,20},{18,... | collective-permute-start | bytes 786440 | tf_op jit(solution)/shard_map/ppermute | solution.py:156
  11.2 1.4 collective-permute-start.19
  12.5 6.3 %collective-permute-start.16 = (f32[264,256]{1,0:T(8,128)}, f32[264,256]{1,0:T(8,128)}, u32[]{:S(2)}, u32[]{:S(2)}) collective-permute-start(f32[264,256]{1,0:T(8,128)} %get-tuple-element.29), channel_id=1, source_target_pairs={{0,8},{2,10},{4,12},{6,14},{24,16},{26,18},{28,20},{30,22},{1,9},{... | collective-permute-start | bytes 811016 | tf_op jit(solution)/shard_map/ppermute | solution.py:156
  29.9 1.9 %dynamic-slice_bitcast_fusion.3 = (f32[1,264,128]{2,1,0:T(8,128)}, f32[1,264,128]{2,1,0:T(8,128)S(1)}, f32[1,264,128]{2,1,0:T(8,128)}, f32[1,264,128]{2,1,0:T(8,128)S(1)}) fusion(f32[4,2,2,264,128]{4,3,2,1,0:T(8,128)} %bitcast.89, s32[]{:T(128)S(6)} %select_n.199, s32[]{:T(128)S(6)} %select_n.192, s32[]{:T(128)S(6)} %select_n.193, s32[]{:T(128)S(6)} %select_n.197, ...), kind=kLoop, calls=%fused_computation.39 | loop fusion | bytes 1081368 | tf_op jit(solution)/shard_map/stack;squeeze | solution.py:223
  31.9 1.8 %pad_maximum_fusion = f32[2,264,256]{2,1,0:T(8,128)} fusion(f32[1,264,256]{2,1,0:T(8,128)} %bitcast.27, f32[1,264,256]{2,1,0:T(8,128)S(1)} %copy-done.12), kind=kLoop, calls=%fused_computation.8 | loop fusion | flops 135168 | bytes 1081344 | tf_op jit(solution)/shard_map/stack | solution.py:210
  33.7 1.3 collective-permute-start.20
  35.0 1.4 collective-permute-start.17
  39.1 1.5 collective-permute-start.2
  41.3 1.0 pad_maximum_fusion.4
  42.3 1.0 pad_maximum_fusion.2
  43.3 1.3 collective-permute-start.18
  45.2 2.2 %collective-permute-done.8.crossed_a = f32[2,264,128]{2,1,0:T(8,128)} collective-permute-done((f32[2,264,128]{2,1,0:T(8,128)}, f32[2,264,128]{2,1,0:T(8,128)}, u32[]{:S(2)}, u32[]{:S(2)}) %collective-permute-start.8) | collective-permute-done | bytes 270368 | tf_op jit(solution)/shard_map/ppermute | solution.py:156
  48.0 2.2 %shard_map.122 = f32[264,512]{1,0:T(8,128)S(1)} custom-call(s32[2]{0:T(128)S(1)} %pad_add_fusion.2.at, f32[4,2,264,128]{3,2,1,0:T(8,128)S(1)} %get-tuple-element.21.own_a, f32[4,2,264,128]{3,2,1,0:T(8,128)S(1)} %collective-permute-done.1.core_a, f32[2,264,128]{2,1,0:T(8,128)} %collective-permute-done.8.crossed_a, f32[128,512]{1,0:T(8,128)S(1)} %bitcast_convert_fusion.own_g, ...), custom_call_target="tpu_custom_call" | custom-call | flops 138412032 | bytes 2129920 | tf_op jit(solution)/shard_map/pallas_call | solution.py:104
  50.1 3.1 %collective-permute-done.2.crossed_a = f32[2,264,128]{2,1,0:T(8,128)} collective-permute-done((f32[2,264,128]{2,1,0:T(8,128)}, f32[2,264,128]{2,1,0:T(8,128)}, u32[]{:S(2)}, u32[]{:S(2)}) %collective-permute-start.2) | collective-permute-done | bytes 270368 | tf_op jit(solution)/shard_map/ppermute | solution.py:156
  53.2 2.2 %shard_map.120 = f32[264,512]{1,0:T(8,128)S(1)} custom-call(s32[2]{0:T(128)S(1)} %pad_add_fusion.at, f32[4,2,264,128]{3,2,1,0:T(8,128)S(1)} %get-tuple-element.21.own_a, f32[4,2,264,128]{3,2,1,0:T(8,128)S(1)} %collective-permute-done.1.core_a, f32[2,264,128]{2,1,0:T(8,128)} %collective-permute-done.2.crossed_a, f32[128,512]{1,0:T(8,128)S(1)} %bitcast_convert_fusion.own_g, ...), custom_call_target="tpu_custom_call" | custom-call | flops 138412032 | bytes 2129920 | tf_op jit(solution)/shard_map/pallas_call | solution.py:104
  56.2 2.7 %collective-permute-done.11.crossed_a = f32[2,264,128]{2,1,0:T(8,128)S(1)} collective-permute-done((f32[2,264,128]{2,1,0:T(8,128)S(1)}, f32[2,264,128]{2,1,0:T(8,128)S(1)}, u32[]{:S(2)}, u32[]{:S(2)}) %collective-permute-start.11) | collective-permute-done | bytes 270368 | tf_op jit(solution)/shard_map/ppermute | solution.py:156
  58.9 2.1 %shard_map.123 = f32[264,512]{1,0:T(8,128)S(1)} custom-call(s32[2]{0:T(128)S(1)} %pad_add_fusion.3.at, f32[4,2,264,128]{3,2,1,0:T(8,128)S(1)} %get-tuple-element.21.own_a, f32[4,2,264,128]{3,2,1,0:T(8,128)S(1)} %collective-permute-done.1.core_a, f32[2,264,128]{2,1,0:T(8,128)S(1)} %collective-permute-done.11.crossed_a, ...), custom_call_target="tpu_custom_call" | custom-call | flops 138412032 | bytes 2129920 | tf_op jit(solution)/shard_map/pallas_call | solution.py:104
  61.0 2.0 %fusion.11 = f32[512,256]{1,0:T(8,128)S(1)} fusion(f32[264,512]{1,0:T(8,128)S(1)} %shard_map.122, f32[264,256]{1,0:T(8,128)} %collective-permute-done.19, f32[2,264,256]{2,1,0:T(8,128)} %collective-permute-done.20, pred[]{:T(512)S(6)} %or.3), kind=kOutput, calls=%fused_computation.28 | convolution fusion | flops 207685632 | bytes 1605633 | tf_op jit(solution)/shard_map/dot_general | solution.py:237
  63.0 1.3 collective-permute-done.6.crossed_a
  64.3 2.1 %shard_map.121 = f32[264,512]{1,0:T(8,128)S(1)} custom-call(s32[2]{0:T(128)S(1)} %pad_add_fusion.1.at, f32[4,2,264,128]{3,2,1,0:T(8,128)S(1)} %get-tuple-element.21.own_a, f32[4,2,264,128]{3,2,1,0:T(8,128)S(1)} %collective-permute-done.1.core_a, f32[2,264,128]{2,1,0:T(8,128)S(1)} %collective-permute-done.6.crossed_a, ...), custom_call_target="tpu_custom_call" | custom-call | flops 138412032 | bytes 2129920 | tf_op jit(solution)/shard_map/pallas_call | solution.py:104
  66.4 2.0 %fusion.8 = f32[512,256]{1,0:T(8,128)S(1)} fusion(f32[264,512]{1,0:T(8,128)S(1)} %shard_map.121, f32[264,256]{1,0:T(8,128)} %collective-permute-done.16, f32[2,264,256]{2,1,0:T(8,128)} %collective-permute-done.20, pred[]{:T(512)S(6)} %or.3), kind=kOutput, calls=%fused_computation.25 | convolution fusion | flops 207685632 | bytes 1605633 | tf_op jit(solution)/shard_map/dot_general | solution.py:237
  69.5 1.5 collective-permute-done.21
  71.7 6.8 %collective-permute-start.12 = (f32[264,512]{1,0:T(8,128)S(1)}, f32[264,512]{1,0:T(8,128)S(1)}, u32[]{:S(2)}, u32[]{:S(2)}) collective-permute-start(f32[264,512]{1,0:T(8,128)S(1)} %copy-done.6), channel_id=1, source_target_pairs={{0,8},{2,10},{4,12},{6,14},{24,16},{26,18},{28,20},{30,22},{1,9},{... | collective-permute-start | bytes 1622024 | tf_op jit(solution)/shard_map/ppermute | solution.py:156
  79.9 4.0 %collective-permute-start.23 = (f32[64,256]{1,0:T(8,128)}, f32[64,256]{1,0:T(8,128)S(1)}, u32[]{:S(2)}, u32[]{:S(2)}) collective-permute-start(f32[64,256]{1,0:T(8,128)} %constant_dynamic-slice_fusion.1), channel_id=1, source_target_pairs={{0,16},{2,18},{4,20},{6,22},{8,24},{10,26},{12,28},{14,30},{16,0},... | collective-permute-start | bytes 196616 | tf_op jit(solution)/shard_map/ppermute | solution.py:156
  83.9 2.2 %collective-permute-start.9 = (f32[264,512]{1,0:T(8,128)S(1)}, f32[264,512]{1,0:T(8,128)}, u32[]{:S(2)}, u32[]{:S(2)}) collective-permute-start(f32[264,512]{1,0:T(8,128)S(1)} %copy-done.4), channel_id=1, source_target_pairs={{0,8},{2,10},{4,12},{6,14},{24,16},{26,18},{28,20},{30,22},{1,9},{... | collective-permute-start | bytes 1622024 | tf_op jit(solution)/shard_map/ppermute | solution.py:156
  86.2 5.0 %collective-permute-done.12 = f32[264,512]{1,0:T(8,128)S(1)} collective-permute-done((f32[264,512]{1,0:T(8,128)S(1)}, f32[264,512]{1,0:T(8,128)S(1)}, u32[]{:S(2)}, u32[]{:S(2)}) %collective-permute-start.12) | collective-permute-done | bytes 540704 | tf_op jit(solution)/shard_map/ppermute | solution.py:156
  92.8 5.3 %collective-permute-start.24 = (f32[32,256]{1,0:T(8,128)S(1)}, f32[32,256]{1,0:T(8,128)S(1)}, u32[]{:S(2)}, u32[]{:S(2)}) collective-permute-start(f32[32,256]{1,0:T(8,128)S(1)} %constant_dynamic-slice_fusion), channel_id=1, source_target_pairs={{0,8},{2,10},{4,12},{6,14},{8,0},{10,2},{12,4},{14,6},{16,24},{18,... | collective-permute-start | bytes 98312 | tf_op jit(solution)/shard_map/ppermute | solution.py:156
  98.1 5.6 %collective-permute-done.24 = f32[32,256]{1,0:T(8,128)S(1)} collective-permute-done((f32[32,256]{1,0:T(8,128)S(1)}, f32[32,256]{1,0:T(8,128)S(1)}, u32[]{:S(2)}, u32[]{:S(2)}) %collective-permute-start.24) | collective-permute-done | bytes 32800 | tf_op jit(solution)/shard_map/ppermute | solution.py:156
  103.7 2.5 %collective-permute-start.25 = (f32[32,256]{1,0:T(8,128)S(1)}, f32[32,256]{1,0:T(8,128)S(1)}, u32[]{:S(2)}, u32[]{:S(2)}) collective-permute-start(f32[32,256]{1,0:T(8,128)S(1)} %dynamic-slice_add_fusion.4), channel_id=1, source_target_pairs={{0,8},{2,10},{4,12},{6,14},{8,0},{10,2},{12,4},{14,6},{16,24},{18,... | collective-permute-start | bytes 98312 | tf_op jit(solution)/shard_map/ppermute | solution.py:156
  106.2 2.7 %collective-permute-start.7 = (f32[264,512]{1,0:T(8,128)S(1)}, f32[264,512]{1,0:T(8,128)}, u32[]{:S(2)}, u32[]{:S(2)}) collective-permute-start(f32[264,512]{1,0:T(8,128)S(1)} %copy-done.2), channel_id=1, source_target_pairs={{0,8},{2,10},{4,12},{6,14},{24,16},{26,18},{28,20},{30,22},{1,9},{... | collective-permute-start | bytes 1622024 | tf_op jit(solution)/shard_map/ppermute | solution.py:156
  108.9 1.1 add.183
  110.1 1.5 collective-permute-start.10
  112.5 1.3 collective-permute-start.14
  113.8 4.5 %collective-permute-start.26 = (f32[64,256]{1,0:T(8,128)S(1)}, f32[64,256]{1,0:T(8,128)S(1)}, u32[]{:S(2)}, u32[]{:S(2)}) collective-permute-start(f32[64,256]{1,0:T(8,128)S(1)} %maximum_select_fusion.3), channel_id=1, source_target_pairs={{0,16},{2,18},{4,20},{6,22},{8,24},{10,26},{12,28},{14,30},{16,0},... | collective-permute-start | bytes 196616 | tf_op jit(solution)/shard_map/ppermute | solution.py:156
  118.3 7.9 %collective-permute-done.26 = f32[64,256]{1,0:T(8,128)S(1)} collective-permute-done((f32[64,256]{1,0:T(8,128)S(1)}, f32[64,256]{1,0:T(8,128)S(1)}, u32[]{:S(2)}, u32[]{:S(2)}) %collective-permute-start.26) | collective-permute-done | bytes 65568 | tf_op jit(solution)/shard_map/ppermute | solution.py:156
  126.2 1.6 %collective-permute-start.27 = (f32[128,256]{1,0:T(8,128)S(1)}, f32[128,256]{1,0:T(8,128)S(1)}, u32[]{:S(2)}, u32[]{:S(2)}) collective-permute-start(f32[128,256]{1,0:T(8,128)S(1)} %maximum_select_fusion.2), channel_id=1, source_target_pairs={{0,4},{2,6},{4,0},{6,2},{8,12},{10,14},{12,8},{14,10},{16,20},{18,... | collective-permute-start | bytes 393224 | tf_op jit(solution)/shard_map/ppermute | solution.py:156
  127.8 1.5 collective-permute-start
  129.3 1.3 copy.24
  130.6 2.0 %copy.25 = f32[1,1,256,512]{2,3,1,0:T(8,128)} copy(f32[1,1,256,512]{3,2,1,0:T(8,128)} %param.13) | data formatting | bytes 1048576 | tf_op args[4]
  132.8 1.6 %add_add_fusion = f32[264,512]{1,0:T(8,128)S(1)} fusion(f32[264,512]{1,0:T(8,128)} %collective-permute-done.14, f32[264,512]{1,0:T(8,128)} %collective-permute-done.10, f32[264,512]{1,0:T(8,128)S(1)} %copy-done.8, f32[264,512]{1,0:T(8,128)} %collective-permute-done.7), kind=kLoop, calls=%fused_computation.11 | loop fusion | flops 405504 | bytes 2703360 | tf_op jit(solution)/shard_map/add | solution.py:234
  135.7 1.6 %collective-permute-start.29 = (f32[1,512]{1,0:T(1,128)S(1)}, f32[1,512]{1,0:T(1,128)S(1)}, u32[]{:S(2)}, u32[]{:S(2)}) collective-permute-start(f32[1,512]{1,0:T(1,128)S(1)} %bitcast.92), channel_id=1, source_target_pairs={{0,1},{1,0},{2,3},{3,2},{4,5},{5,4},{6,7},{7,6},{8,9},{9,8},{10,11... | collective-permute-start | bytes 6152 | tf_op jit(solution)/shard_map/ppermute | solution.py:178
  137.2 1.0 copy.26
  138.2 1.0 copy.27
  139.2 12.1 %collective-permute-done.29 = f32[1,512]{1,0:T(1,128)S(1)} collective-permute-done((f32[1,512]{1,0:T(1,128)S(1)}, f32[1,512]{1,0:T(1,128)S(1)}, u32[]{:S(2)}, u32[]{:S(2)}) %collective-permute-start.29) | collective-permute-done | bytes 2080 | tf_op jit(solution)/shard_map/ppermute | solution.py:178
  151.4 1.9 %multiply_add_fusion = (f32[264,512]{1,0:T(8,128)S(1)}, f32[264,512]{1,0:T(8,128)S(1)}) fusion(f32[264,512]{1,0:T(8,128)} %param.16, f32[264,512]{1,0:T(8,128)S(1)} %copy-done.10, f32[512]{0:T(512)S(1)} %bitcast.91, f32[264,512]{1,0:T(8,128)} %collective-permute-done.15, f32[264,512]{1,0:T(8,128)S(1)} %add_add_fusion, f32[264,512]{1,0:T(8,128)} %collective-permute-done, ...), kind=kLoop, calls=%fused_computation.9 | loop fusion | flops 1757184 | bytes 4329473 | tf_op jit(solution)/shard_map/add | solution.py:20
  (98 shorter events, 18.5 us)
Async XLA Ops:
  0.6 1.2 copy-start
  4.3 3.2 %copy-start.17 = (bf16[1,128,512]{2,1,0:T(8,128)(2,1)S(1)}, bf16[1,128,512]{2,1,0:T(8,128)(2,1)}, u32[]{:S(2)}) copy-start(bf16[1,128,512]{2,1,0:T(8,128)(2,1)} %param.10) | copy-start | bytes 393220
  4.3 6.0 %copy-start.13 = (bf16[264,256]{1,0:T(8,128)(2,1)S(1)}, bf16[264,256]{1,0:T(8,128)(2,1)}, u32[]{:S(2)}) copy-start(bf16[264,256]{1,0:T(8,128)(2,1)} %param.11) | copy-start | bytes 405508
  7.1 29.3 %collective-permute-start.1 = (f32[4,2,264,128]{3,2,1,0:T(8,128)}, f32[4,2,264,128]{3,2,1,0:T(8,128)S(1)}, u32[]{:S(2)}, u32[]{:S(2)}) collective-permute-start(f32[4,2,264,128]{3,2,1,0:T(8,128)} %get-tuple-element.20), channel_id=1, source_target_pairs={{0,2},{2,0},{4,6},{6,4},{8,10},{10,8},{12,14},{14,12},{16,18},{18,... | collective-permute-start | bytes 3244040 | tf_op jit(solution)/shard_map/ppermute | solution.py:156
  7.5 24.3 %collective-permute-start.4 = (f32[128,512]{1,0:T(8,128)S(1)}, f32[128,512]{1,0:T(8,128)}, u32[]{:S(2)}, u32[]{:S(2)}) collective-permute-start(f32[128,512]{1,0:T(8,128)S(1)} %bitcast_convert_fusion.own_g), channel_id=1, source_target_pairs={{0,4},{2,6},{4,0},{6,2},{8,12},{10,14},{12,8},{14,10},{16,20},{18,... | collective-permute-start | bytes 786440 | tf_op jit(solution)/shard_map/ppermute | solution.py:156
  10.1 29.0 %collective-permute-start.3 = (f32[128,512]{1,0:T(8,128)S(1)}, f32[128,512]{1,0:T(8,128)}, u32[]{:S(2)}, u32[]{:S(2)}) collective-permute-start(f32[128,512]{1,0:T(8,128)S(1)} %bitcast_convert_fusion.own_g), channel_id=1, source_target_pairs={{0,2},{2,0},{4,6},{6,4},{8,10},{10,8},{12,14},{14,12},{16,18},{18,... | collective-permute-start | bytes 786440 | tf_op jit(solution)/shard_map/ppermute | solution.py:156
  11.2 20.7 %collective-permute-start.19 = (f32[264,256]{1,0:T(8,128)}, f32[264,256]{1,0:T(8,128)}, u32[]{:S(2)}, u32[]{:S(2)}) collective-permute-start(f32[264,256]{1,0:T(8,128)} %get-tuple-element.29), channel_id=1, source_target_pairs={{8,16},{10,18},{12,20},{14,22},{16,8},{18,10},{20,12},{22,14},{9,1... | collective-permute-start | bytes 811016 | tf_op jit(solution)/shard_map/ppermute | solution.py:156
  12.5 22.4 %collective-permute-start.16 = (f32[264,256]{1,0:T(8,128)}, f32[264,256]{1,0:T(8,128)}, u32[]{:S(2)}, u32[]{:S(2)}) collective-permute-start(f32[264,256]{1,0:T(8,128)} %get-tuple-element.29), channel_id=1, source_target_pairs={{0,8},{2,10},{4,12},{6,14},{24,16},{26,18},{28,20},{30,22},{1,9},{... | collective-permute-start | bytes 811016 | tf_op jit(solution)/shard_map/ppermute | solution.py:156
  29.9 2.0 %copy-start.12 = (f32[1,264,256]{2,1,0:T(8,128)S(1)}, f32[1,264,256]{2,1,0:T(8,128)}, u32[]{:S(2)}) copy-start(f32[1,264,256]{2,1,0:T(8,128)} %get-tuple-element.28) | copy-start | bytes 811012
  31.9 12.7 %collective-permute-start.5 = (f32[128,512]{1,0:T(8,128)}, f32[128,512]{1,0:T(8,128)}, u32[]{:S(2)}, u32[]{:S(2)}) collective-permute-start(f32[128,512]{1,0:T(8,128)} %collective-permute-done.4.side_g), channel_id=1, source_target_pairs={{0,2},{2,0},{4,6},{6,4},{8,10},{10,8},{12,14},{14,12},{16,18},{18,... | collective-permute-start | bytes 786440 | tf_op jit(solution)/shard_map/ppermute | solution.py:156
  33.7 27.3 %collective-permute-start.20 = (f32[2,264,256]{2,1,0:T(8,128)}, f32[2,264,256]{2,1,0:T(8,128)}, u32[]{:S(2)}, u32[]{:S(2)}) collective-permute-start(f32[2,264,256]{2,1,0:T(8,128)} %pad_maximum_fusion), channel_id=1, source_target_pairs={{8,0},{10,2},{12,4},{14,6},{16,24},{18,26},{20,28},{22,30},{9,1},{... | collective-permute-start | bytes 1622024 | tf_op jit(solution)/shard_map/ppermute | solution.py:156
  35.0 8.3 %collective-permute-start.17 = (f32[264,256]{1,0:T(8,128)}, f32[264,256]{1,0:T(8,128)}, u32[]{:S(2)}, u32[]{:S(2)}) collective-permute-start(f32[264,256]{1,0:T(8,128)} %collective-permute-done.16), channel_id=1, source_target_pairs={{8,16},{10,18},{12,20},{14,22},{16,8},{18,10},{20,12},{22,14},{9,1... | collective-permute-start | bytes 811016 | tf_op jit(solution)/shard_map/ppermute | solution.py:156
  37.8 9.6 %collective-permute-start.8 = (f32[2,264,128]{2,1,0:T(8,128)}, f32[2,264,128]{2,1,0:T(8,128)}, u32[]{:S(2)}, u32[]{:S(2)}) collective-permute-start(f32[2,264,128]{2,1,0:T(8,128)} %pad_maximum_fusion.3), channel_id=1, source_target_pairs={{0,4},{2,6},{4,0},{6,2},{8,12},{10,14},{12,8},{14,10},{16,20},{18,... | collective-permute-start | bytes 811016 | tf_op jit(solution)/shard_map/ppermute | solution.py:156
  39.1 14.1 %collective-permute-start.2 = (f32[2,264,128]{2,1,0:T(8,128)}, f32[2,264,128]{2,1,0:T(8,128)}, u32[]{:S(2)}, u32[]{:S(2)}) collective-permute-start(f32[2,264,128]{2,1,0:T(8,128)} %pad_maximum_fusion.1), channel_id=1, source_target_pairs={{0,4},{2,6},{4,0},{6,2},{8,12},{10,14},{12,8},{14,10},{16,20},{18,... | collective-permute-start | bytes 811016 | tf_op jit(solution)/shard_map/ppermute | solution.py:156
  43.3 25.2 %collective-permute-start.18 = (f32[264,256]{1,0:T(8,128)}, f32[264,256]{1,0:T(8,128)S(1)}, u32[]{:S(2)}, u32[]{:S(2)}) collective-permute-start(f32[264,256]{1,0:T(8,128)} %collective-permute-done.17), channel_id=1, source_target_pairs={{8,0},{10,2},{12,4},{14,6},{16,24},{18,26},{20,28},{22,30},{9,1},{... | collective-permute-start | bytes 811016 | tf_op jit(solution)/shard_map/ppermute | solution.py:156
  44.6 14.3 %collective-permute-start.11 = (f32[2,264,128]{2,1,0:T(8,128)S(1)}, f32[2,264,128]{2,1,0:T(8,128)S(1)}, u32[]{:S(2)}, u32[]{:S(2)}) collective-permute-start(f32[2,264,128]{2,1,0:T(8,128)S(1)} %pad_maximum_fusion.4), channel_id=1, source_target_pairs={{0,4},{2,6},{4,0},{6,2},{8,12},{10,14},{12,8},{14,10},{16,20},{18,... | collective-permute-start | bytes 811016 | tf_op jit(solution)/shard_map/ppermute | solution.py:156
  47.4 16.9 %collective-permute-start.6 = (f32[2,264,128]{2,1,0:T(8,128)S(1)}, f32[2,264,128]{2,1,0:T(8,128)S(1)}, u32[]{:S(2)}, u32[]{:S(2)}) collective-permute-start(f32[2,264,128]{2,1,0:T(8,128)S(1)} %pad_maximum_fusion.2), channel_id=1, source_target_pairs={{0,4},{2,6},{4,0},{6,2},{8,12},{10,14},{12,8},{14,10},{16,20},{18,... | collective-permute-start | bytes 811016 | tf_op jit(solution)/shard_map/ppermute | solution.py:156
  50.1 10.9 %copy-start.3 = (f32[264,512]{1,0:T(8,128)}, f32[264,512]{1,0:T(8,128)S(1)}, u32[]{:S(2)}) copy-start(f32[264,512]{1,0:T(8,128)S(1)} %shard_map.122) | copy-start | bytes 1622020
  50.1 5.3 %copy-start.14 = (bf16[264,256]{1,0:T(8,128)(2,1)S(1)}, bf16[264,256]{1,0:T(8,128)(2,1)}, u32[]{:S(2)}) copy-start(bf16[264,256]{1,0:T(8,128)(2,1)} %param.11) | copy-start | bytes 405508
  55.4 0.8 copy-start.7
  61.0 7.5 %copy-start.5 = (f32[264,512]{1,0:T(8,128)}, f32[264,512]{1,0:T(8,128)S(1)}, u32[]{:S(2)}) copy-start(f32[264,512]{1,0:T(8,128)S(1)} %shard_map.123) | copy-start | bytes 1622020
  66.4 3.0 %copy-start.1 = (f32[264,512]{1,0:T(8,128)}, f32[264,512]{1,0:T(8,128)S(1)}, u32[]{:S(2)}) copy-start(f32[264,512]{1,0:T(8,128)S(1)} %shard_map.121) | copy-start | bytes 1622020
  69.4 2.3 %copy-start.6 = (f32[264,512]{1,0:T(8,128)S(1)}, f32[264,512]{1,0:T(8,128)}, u32[]{:S(2)}) copy-start(f32[264,512]{1,0:T(8,128)} %copy-done.5) | copy-start | bytes 1622020
  69.4 14.5 %copy-start.4 = (f32[264,512]{1,0:T(8,128)S(1)}, f32[264,512]{1,0:T(8,128)}, u32[]{:S(2)}) copy-start(f32[264,512]{1,0:T(8,128)} %copy-done.3) | copy-start | bytes 1622020
  69.4 1.6 %collective-permute-start.21 = (f32[256,256]{1,0:T(8,128)S(1)}, f32[256,256]{1,0:T(8,128)S(1)}, u32[]{:S(2)}, u32[]{:S(2)}) collective-permute-start(f32[256,256]{1,0:T(8,128)S(1)} %constant_dynamic-slice_fusion.3), channel_id=1, source_target_pairs={{0,2},{2,0},{4,6},{6,4},{8,10},{10,8},{12,14},{14,12},{16,18},{18,... | collective-permute-start | bytes 786440 | tf_op jit(solution)/shard_map/ppermute | solution.py:156
  71.1 7.5 %collective-permute-start.22 = (f32[128,256]{1,0:T(8,128)S(1)}, f32[128,256]{1,0:T(8,128)S(1)}, u32[]{:S(2)}, u32[]{:S(2)}) collective-permute-start(f32[128,256]{1,0:T(8,128)S(1)} %constant_dynamic-slice_fusion.2), channel_id=1, source_target_pairs={{0,4},{2,6},{4,0},{6,2},{8,12},{10,14},{12,8},{14,10},{16,20},{18,... | collective-permute-start | bytes 393224 | tf_op jit(solution)/shard_map/ppermute | solution.py:156
  71.7 19.5 %collective-permute-start.12 = (f32[264,512]{1,0:T(8,128)S(1)}, f32[264,512]{1,0:T(8,128)S(1)}, u32[]{:S(2)}, u32[]{:S(2)}) collective-permute-start(f32[264,512]{1,0:T(8,128)S(1)} %copy-done.6), channel_id=1, source_target_pairs={{0,8},{2,10},{4,12},{6,14},{24,16},{26,18},{28,20},{30,22},{1,9},{... | collective-permute-start | bytes 1622024 | tf_op jit(solution)/shard_map/ppermute | solution.py:156
  78.6 0.7 copy-start.15
  79.3 27.0 %copy-start.2 = (f32[264,512]{1,0:T(8,128)S(1)}, f32[264,512]{1,0:T(8,128)}, u32[]{:S(2)}) copy-start(f32[264,512]{1,0:T(8,128)} %copy-done.1) | copy-start | bytes 1622020
  79.9 12.8 %collective-permute-start.23 = (f32[64,256]{1,0:T(8,128)}, f32[64,256]{1,0:T(8,128)S(1)}, u32[]{:S(2)}, u32[]{:S(2)}) collective-permute-start(f32[64,256]{1,0:T(8,128)} %constant_dynamic-slice_fusion.1), channel_id=1, source_target_pairs={{0,16},{2,18},{4,20},{6,22},{8,24},{10,26},{12,28},{14,30},{16,0},... | collective-permute-start | bytes 196616 | tf_op jit(solution)/shard_map/ppermute | solution.py:156
  83.9 8.8 %copy-start.16 = (f32[128,256]{1,0:T(8,128)S(1)}, f32[128,256]{1,0:T(8,128)}, u32[]{:S(2)}) copy-start(f32[128,256]{1,0:T(8,128)} %copy-done.15) | copy-start | bytes 393220
  83.9 25.0 %collective-permute-start.9 = (f32[264,512]{1,0:T(8,128)S(1)}, f32[264,512]{1,0:T(8,128)}, u32[]{:S(2)}, u32[]{:S(2)}) collective-permute-start(f32[264,512]{1,0:T(8,128)S(1)} %copy-done.4), channel_id=1, source_target_pairs={{0,8},{2,10},{4,12},{6,14},{24,16},{26,18},{28,20},{30,22},{1,9},{... | collective-permute-start | bytes 1622024 | tf_op jit(solution)/shard_map/ppermute | solution.py:156
  92.0 19.6 %collective-permute-start.13 = (f32[264,512]{1,0:T(8,128)}, f32[264,512]{1,0:T(8,128)S(1)}, u32[]{:S(2)}, u32[]{:S(2)}) collective-permute-start(f32[264,512]{1,0:T(8,128)} %add.186), channel_id=1, source_target_pairs={{8,16},{10,18},{12,20},{14,22},{16,8},{18,10},{20,12},{22,14},{9,1... | collective-permute-start | bytes 1622024 | tf_op jit(solution)/shard_map/ppermute | solution.py:156
  92.8 10.9 %collective-permute-start.24 = (f32[32,256]{1,0:T(8,128)S(1)}, f32[32,256]{1,0:T(8,128)S(1)}, u32[]{:S(2)}, u32[]{:S(2)}) collective-permute-start(f32[32,256]{1,0:T(8,128)S(1)} %constant_dynamic-slice_fusion), channel_id=1, source_target_pairs={{0,8},{2,10},{4,12},{6,14},{8,0},{10,2},{12,4},{14,6},{16,24},{18,... | collective-permute-start | bytes 98312 | tf_op jit(solution)/shard_map/ppermute | solution.py:156
  103.7 10.0 %collective-permute-start.25 = (f32[32,256]{1,0:T(8,128)S(1)}, f32[32,256]{1,0:T(8,128)S(1)}, u32[]{:S(2)}, u32[]{:S(2)}) collective-permute-start(f32[32,256]{1,0:T(8,128)S(1)} %dynamic-slice_add_fusion.4), channel_id=1, source_target_pairs={{0,8},{2,10},{4,12},{6,14},{8,0},{10,2},{12,4},{14,6},{16,24},{18,... | collective-permute-start | bytes 98312 | tf_op jit(solution)/shard_map/ppermute | solution.py:156
  106.2 26.5 %collective-permute-start.7 = (f32[264,512]{1,0:T(8,128)S(1)}, f32[264,512]{1,0:T(8,128)}, u32[]{:S(2)}, u32[]{:S(2)}) collective-permute-start(f32[264,512]{1,0:T(8,128)S(1)} %copy-done.2), channel_id=1, source_target_pairs={{0,8},{2,10},{4,12},{6,14},{24,16},{26,18},{28,20},{30,22},{1,9},{... | collective-permute-start | bytes 1622024 | tf_op jit(solution)/shard_map/ppermute | solution.py:156
  110.1 22.7 %collective-permute-start.10 = (f32[264,512]{1,0:T(8,128)S(1)}, f32[264,512]{1,0:T(8,128)}, u32[]{:S(2)}, u32[]{:S(2)}) collective-permute-start(f32[264,512]{1,0:T(8,128)S(1)} %add.183), channel_id=1, source_target_pairs={{8,16},{10,18},{12,20},{14,22},{16,8},{18,10},{20,12},{22,14},{9,1... | collective-permute-start | bytes 1622024 | tf_op jit(solution)/shard_map/ppermute | solution.py:156
  112.5 20.3 %collective-permute-start.14 = (f32[264,512]{1,0:T(8,128)}, f32[264,512]{1,0:T(8,128)}, u32[]{:S(2)}, u32[]{:S(2)}) collective-permute-start(f32[264,512]{1,0:T(8,128)} %add.187), channel_id=1, source_target_pairs={{8,0},{10,2},{12,4},{14,6},{16,24},{18,26},{20,28},{22,30},{9,1},{... | collective-permute-start | bytes 1622024 | tf_op jit(solution)/shard_map/ppermute | solution.py:156
  113.8 12.4 %collective-permute-start.26 = (f32[64,256]{1,0:T(8,128)S(1)}, f32[64,256]{1,0:T(8,128)S(1)}, u32[]{:S(2)}, u32[]{:S(2)}) collective-permute-start(f32[64,256]{1,0:T(8,128)S(1)} %maximum_select_fusion.3), channel_id=1, source_target_pairs={{0,16},{2,18},{4,20},{6,22},{8,24},{10,26},{12,28},{14,30},{16,0},... | collective-permute-start | bytes 196616 | tf_op jit(solution)/shard_map/ppermute | solution.py:156
  126.2 6.4 %collective-permute-start.27 = (f32[128,256]{1,0:T(8,128)S(1)}, f32[128,256]{1,0:T(8,128)S(1)}, u32[]{:S(2)}, u32[]{:S(2)}) collective-permute-start(f32[128,256]{1,0:T(8,128)S(1)} %maximum_select_fusion.2), channel_id=1, source_target_pairs={{0,4},{2,6},{4,0},{6,2},{8,12},{10,14},{12,8},{14,10},{16,20},{18,... | collective-permute-start | bytes 393224 | tf_op jit(solution)/shard_map/ppermute | solution.py:156
  127.8 23.6 %collective-permute-start = (f32[264,512]{1,0:T(8,128)}, f32[264,512]{1,0:T(8,128)}, u32[]{:S(2)}, u32[]{:S(2)}) collective-permute-start(f32[264,512]{1,0:T(8,128)} %bitcast), channel_id=1, source_target_pairs={{0,1},{1,0},{2,3},{3,2},{4,5},{5,4},{6,7},{7,6},{8,9},{9,8},{10,11... | collective-permute-start | bytes 1622024 | tf_op jit(solution)/shard_map/ppermute | solution.py:178
  129.3 3.5 %copy-start.8 = (f32[264,512]{1,0:T(8,128)S(1)}, f32[264,512]{1,0:T(8,128)}, u32[]{:S(2)}) copy-start(f32[264,512]{1,0:T(8,128)} %copy-done.7) | copy-start | bytes 1622020
  132.6 2.3 %copy-start.9 = (f32[1,1,256,512]{2,3,1,0:T(8,128)S(1)}, f32[1,1,256,512]{2,3,1,0:T(8,128)}, u32[]{:S(2)}) copy-start(f32[1,1,256,512]{2,3,1,0:T(8,128)} %copy.25) | copy-start | bytes 1572868
  132.7 2.3 %collective-permute-start.28 = (f32[256,256]{1,0:T(8,128)S(1)}, f32[256,256]{1,0:T(8,128)S(1)}, u32[]{:S(2)}, u32[]{:S(2)}) collective-permute-start(f32[256,256]{1,0:T(8,128)S(1)} %maximum_select_fusion.1), channel_id=1, source_target_pairs={{0,2},{2,0},{4,6},{6,4},{8,10},{10,8},{12,14},{14,12},{16,18},{18,... | collective-permute-start | bytes 786440 | tf_op jit(solution)/shard_map/ppermute | solution.py:156
  134.4 16.9 %collective-permute-start.15 = (f32[264,512]{1,0:T(8,128)S(1)}, f32[264,512]{1,0:T(8,128)}, u32[]{:S(2)}, u32[]{:S(2)}) collective-permute-start(f32[264,512]{1,0:T(8,128)S(1)} %add_add_fusion), channel_id=1, source_target_pairs={{0,1},{1,0},{2,3},{3,2},{4,5},{5,4},{6,7},{7,6},{8,9},{9,8},{10,11... | collective-permute-start | bytes 1622024 | tf_op jit(solution)/shard_map/ppermute | solution.py:178
  135.6 15.7 %copy-start.10 = (f32[264,512]{1,0:T(8,128)S(1)}, f32[264,512]{1,0:T(8,128)}, u32[]{:S(2)}) copy-start(f32[264,512]{1,0:T(8,128)} %param.15) | copy-start | bytes 1622020
  135.7 15.7 %collective-permute-start.29 = (f32[1,512]{1,0:T(1,128)S(1)}, f32[1,512]{1,0:T(1,128)S(1)}, u32[]{:S(2)}, u32[]{:S(2)}) collective-permute-start(f32[1,512]{1,0:T(1,128)S(1)} %bitcast.92), channel_id=1, source_target_pairs={{0,1},{1,0},{2,3},{3,2},{4,5},{5,4},{6,7},{7,6},{8,9},{9,8},{10,11... | collective-permute-start | bytes 6152 | tf_op jit(solution)/shard_map/ppermute | solution.py:178
  153.3 0.8 copy-start.11

commit v2 on v0

v2 whole, which is shorter than its diff:
```python
import jax
import jax.numpy as jnp
from jax import lax
from jax.experimental import pallas as pl
from jax.experimental.pallas import tpu as pltpu
from jax.sharding import PartitionSpec as P

first_decay = 0.9
second_decay = 0.999
first_fix = 1.0 - 0.9**10
second_fix = 1.0 - 0.999**10
epsilon = 1e-08
inner_rate = 1.0
outer_rate = 0.7
outer_beta = 0.9


def outer_step(stepped_sum, global_part, momentum_part, island_count):
    pseudo_grad = global_part - stepped_sum / island_count
    momentum_next = outer_beta * momentum_part + pseudo_grad
    weights_next = (global_part - outer_rate * (pseudo_grad + outer_beta * momentum_next)).astype(
        jnp.bfloat16
    )
    return (weights_next, momentum_next)


def moments_and_scale(projected, first, second):
    new_first = first_decay * first + (1.0 - first_decay) * projected
    new_second = second_decay * second + (1.0 - second_decay) * projected * projected
    adapted = new_first / first_fix / (jnp.sqrt(new_second / second_fix) + epsilon)
    scale = jnp.sqrt(jnp.mean(adapted * adapted, axis=0, keepdims=True)) / jnp.sqrt(
        jnp.mean(projected * projected, axis=0, keepdims=True) + 1e-06
    )
    return new_first, new_second, scale


def plain_body(
    activations,
    out_grads,
    projection,
    first_moment,
    second_moment,
    inner_weights,
    global_weights,
    outer_momentum,
):
    col_total = global_weights.shape[1]
    product = lax.dot_general(
        activations[0],
        out_grads[0],
        (((0,), (0,)), ((), ())),
        preferred_element_type=jnp.float32,
    )
    grad_rows = lax.psum_scatter(product, "fsdp", scatter_dimension=0, tiled=True)
    partial_sum = lax.dot_general(
        projection.astype(jnp.float32),
        grad_rows,
        (((0,), (0,)), ((), ())),
        precision=lax.Precision.HIGHEST,
        preferred_element_type=jnp.float32,
    )
    projected = lax.psum(partial_sum, "fsdp")
    new_first, new_second, scale = moments_and_scale(
        projected, first_moment[0, 0], second_moment[0, 0]
    )
    stepped = inner_weights[0] - inner_rate * grad_rows * scale
    island_count = lax.axis_size("island")
    block_cols = col_total // island_count
    block_start = lax.axis_index("island") * block_cols
    share_total = lax.psum_scatter(stepped, "island", scatter_dimension=1, tiled=True)
    global_part = lax.dynamic_slice_in_dim(global_weights, block_start, block_cols, 1)
    momentum_part = lax.dynamic_slice_in_dim(outer_momentum, block_start, block_cols, 1)
    weights_block, momentum_block = outer_step(
        share_total, global_part, momentum_part, island_count
    )
    new_momentum = lax.all_gather(momentum_block, "island", axis=1, tiled=True)
    return (weights_block, new_momentum, new_first[None, None], new_second[None, None])


VMEM_BYTES = 32 * 1024 * 1024


def whole_block(shape):
    return pl.BlockSpec(shape, lambda *_: (0,) * len(shape))


def run(kernel, out_shapes, args, after=(), scalars=None, blocks=None, scratch=()):
    blocks = blocks or {}
    lead = 0 if scalars is None else 1
    ins = lead + len(args)

    def body(*refs):
        kernel(*refs[:ins], *refs[ins + len(after) :])

    return pl.pallas_call(
        body,
        out_shape=[jax.ShapeDtypeStruct(shape, kind) for shape, kind in out_shapes],
        grid_spec=pltpu.PrefetchScalarGridSpec(
            num_scalar_prefetch=lead,
            grid=(1,),
            in_specs=[blocks.get(i, whole_block(arg.shape)) for i, arg in enumerate(args)]
            + [pl.BlockSpec(memory_space=pl.ANY)] * len(after),
            out_specs=[whole_block(shape) for shape, _ in out_shapes],
            scratch_shapes=scratch,
        ),
        compiler_params=pltpu.CompilerParams(vmem_limit_bytes=VMEM_BYTES),
        cost_estimate=pl.CostEstimate(flops=0, bytes_accessed=0, transcendentals=0),
    )(*(() if scalars is None else (scalars,)), *args, *after)


F32 = jnp.float32
BF16 = jnp.bfloat16


def turn_kernel(at, a_ref, g_ref, first, far, rest, here, cores, turned):
    tokens, features = a_ref.shape[1:]
    cols = g_ref.shape[2]
    line, rows = here.shape[:2]
    for at_col in range(0, features, tokens):
        turned[at_col : at_col + tokens, :] = (
            a_ref[0, :, at_col : at_col + tokens].astype(F32).T
        )
    for at_col in range(0, cols, tokens):
        first[at_col : at_col + tokens, :] = g_ref[0, :, at_col : at_col + tokens].astype(F32)
    side, core = at[line], at[line + 1]

    def block(k, toward, which):
        start = pl.multiple_of(((at[k] * 2 + toward) * 2 + which) * rows, 8)
        return turned[pl.ds(start, rows), :]

    first[cols:, :] = block(0, 1 - side, core)
    far[...] = block(0, 1 - side, 1 - core)
    for k in range(line):
        here[k] = block(k, side, core)
        cores[k] = block(k, side, 1 - core)
        if k:
            rest[k - 1] = block(k, 1 - side, core)
            cores[line + k - 1] = block(k, 1 - side, 1 - core)


def pair_kernel(*refs):
    out = refs[-1]
    for i, ref in enumerate(refs[:-1]):
        out[i % 2, i // 2] = ref[...]


def stack_kernel(*refs):
    for i, ref in enumerate(refs[:-1]):
        refs[-1][i] = ref[...]


def gather_kernel(near, away, out):
    out[0] = near[...]
    out[1:] = away[...]


def half_kernel(flag, value, out):
    half = out.shape[1]
    out[...] = jnp.where(
        flag[:, :half] == 0, value[:, :half].astype(F32), value[:, half:].astype(F32)
    )


def two_kernel(g_ref, crossed, out):
    tokens = g_ref.shape[1]
    cols = g_ref.shape[2]
    for at_col in range(0, cols, tokens):
        out[0, at_col : at_col + tokens, :] = g_ref[0, :, at_col : at_col + tokens].astype(F32)
    out[1] = crossed[:cols, :]


def first_product_kernel(here, core_a, crossed, far, g_ref, core_g, out, grads):
    tokens = g_ref.shape[1]
    cols = g_ref.shape[2]
    grads[:tokens, :] = g_ref[0]
    for at_col in range(0, cols, tokens):
        span = slice(at_col, at_col + tokens)
        grads[tokens : 2 * tokens, span] = core_g[0, span, :].astype(BF16)
        grads[2 * tokens : 3 * tokens, span] = crossed[span, :].astype(BF16)
        grads[3 * tokens :, span] = core_g[1, span, :].astype(BF16)
    pieces = (here[0], core_a[0], crossed[cols:, :], far[...])
    a = jnp.concatenate([piece.astype(BF16) for piece in pieces], axis=1)
    out[...] = jnp.dot(a, grads[...], preferred_element_type=F32)


def product_kernel(here, core_a, grads, *refs):
    outs = refs[len(refs) - (here.shape[0] - 1) :]
    crossed = [(ref, i) for ref in refs[: -len(outs)] for i in range(ref.shape[1])]
    for k, (out, (ref, i)) in enumerate(zip(outs, crossed)):
        pieces = (here[k + 1], core_a[k + 1], ref[0, i], ref[1, i])
        a = jnp.concatenate([piece.astype(BF16) for piece in pieces], axis=1)
        out[...] = jnp.dot(a, grads[...], preferred_element_type=F32)


def sum_kernel(*refs):
    total = refs[0][...]
    for ref in refs[1:-1]:
        total = total + ref[...]
    refs[-1][...] = total


def lift_kernel(flag, p0, p1, p2, p3, own, received, others, out):
    half = others.shape[2]
    first = flag[:, :half] == 0
    low, high = own[:, :half].astype(F32), own[:, half:].astype(F32)
    mine = (received[2], received[0], received[1], jnp.where(first, low, high))
    theirs = (others[2], others[0], others[1], jnp.where(first, high, low))
    splits = []
    for product in (p0, p1, p2, p3):
        value = product[...]
        top = value.astype(BF16)
        splits.append((top, (value - top.astype(F32)).astype(BF16)))
    totals = []
    for rows in (mine, theirs):
        total = None
        for row, parts in zip(rows, splits):
            turned = row.T.astype(BF16)
            for part in parts:
                term = jnp.dot(turned, part, preferred_element_type=F32)
                total = term if total is None else total + term
        totals.append(total)
    first = flag[...] == 0
    out[:half, :] = jnp.where(first, totals[0], totals[1])
    out[half:, :] = jnp.where(first, totals[1], totals[0])


def outer_kernel(
    flag, inner_sum, grad, grad_other, scale, scale_other, weights, momentum, out, momentum_out
):
    first_island = flag[...] == 0
    own, other = grad[...] * scale[...], grad_other[...] * scale_other[...]
    first, second = jnp.where(first_island, own, other), jnp.where(first_island, other, own)
    total = (inner_sum[...] - inner_rate * first) - inner_rate * second
    weights_next, momentum_next = outer_step(total, weights[...], momentum[...], 2)
    half = out.shape[1]
    out[...] = jnp.where(
        flag[:, :half] == 0,
        weights_next[:, :half].astype(F32),
        weights_next[:, half:].astype(F32),
    ).astype(BF16)
    momentum_out[...] = momentum_next


def line_body(
    activations,
    out_grads,
    projection,
    first_moment,
    second_moment,
    inner_weights,
    global_weights,
    outer_momentum,
):
    fsdp = lax.axis_size("fsdp")
    line = fsdp // 4
    me = lax.axis_index("fsdp")
    place, side, core = me // 4, (me // 2) % 2, me % 2
    rows = projection.shape[0]
    tokens, features = activations.shape[1:]
    cols = global_weights.shape[1]
    rank = projection.shape[1]

    def move(value, target):
        pairs = []
        for f in range(fsdp):
            to = target(f // 4, (f // 2) % 2, f % 2)
            if to is not None:
                pairs.append((f, (to[0] * 2 + to[1]) * 2 + to[2]))
        return lax.ppermute(value, "fsdp", pairs)

    def to_core(value):
        return move(value, lambda l, x, c: (l, x, 1 - c))

    def to_side(value):
        return move(value, lambda l, x, c: (l, 1 - x, c))

    def to_far(value):
        return move(value, lambda l, x, c: (l, 1 - x, 1 - c))

    def to_place(value, mask):
        return move(value, lambda l, x, c: (l ^ mask, x, c))

    def to_island(value):
        return lax.ppermute(value, "island", [(0, 1), (1, 0)])

    island = lax.axis_index("island")
    at = jnp.stack([place ^ 3, place ^ 1, place ^ 2, place, side, core]).astype(jnp.int32)
    flag = jnp.full((1, cols), island, F32)

    block_shape = (rows, tokens)
    first, far, rest, here, cores = run(
        turn_kernel,
        [
            ((cols + rows, tokens), F32),
            (block_shape, F32),
            ((line - 1, *block_shape), F32),
            ((line, *block_shape), F32),
            ((2 * line - 1, *block_shape), F32),
        ],
        [activations, out_grads],
        scalars=at,
        scratch=[pltpu.VMEM((features, tokens), F32)],
    )
    first = to_side(first)
    far = to_far(far)
    from_core = to_core(cores)

    def blocks_of(start, count):
        return pl.BlockSpec((count, *block_shape), lambda *_: (start // count, 0, 0))

    def cross(k, count, after):
        parts = []
        for i in range(count):
            parts += [rest[k - 1 + i], from_core[line + k - 1 + i]]
        (paired,) = run(
            pair_kernel, [((2, count, *block_shape), F32)], parts, after=after
        )
        return to_side(paired)

    def total(*terms, after=()):
        return run(sum_kernel, [(terms[0].shape, F32)], terms, after=after)[0]

    half_rank = (rows, rank // 2)
    (proj_half,) = run(half_kernel, [(half_rank, F32)], [flag, projection])
    proj_near = to_place(proj_half, 1)
    (proj_two,) = run(stack_kernel, [((2, *half_rank), F32)], [proj_half, proj_near])
    proj_away = to_place(proj_two, 2)
    (grads_two,) = run(
        two_kernel, [((2, cols, tokens), F32)], [out_grads, first], after=[far]
    )
    grads_core = to_core(grads_two)
    (proj_stack,) = run(
        gather_kernel, [((3, *half_rank), F32)], [proj_near, proj_away], after=[grads_two]
    )
    proj_others = to_island(proj_stack)
    crossed = [cross(1, 1, [grads_two]), cross(2, line - 2, [grads_two])]
    product0, grads = run(
        first_product_kernel,
        [((rows, cols), F32), ((4 * tokens, cols), BF16)],
        [here, from_core, first, far, out_grads, grads_core],
        after=[proj_stack],
        blocks={0: blocks_of(0, 1), 1: blocks_of(0, 1)},
    )
    got0 = to_place(product0, 1)
    product1, product2, product3 = run(
        product_kernel,
        [((rows, cols), F32)] * (line - 1),
        [here, from_core, grads, *crossed],
    )
    got1 = to_place(product1, 1)

    (partial,) = run(
        lift_kernel,
        [((rank, cols), F32)],
        [flag, product0, product1, product2, product3, projection, proj_stack, proj_others],
    )

    def halve(value, bit, exchange, after=()):
        half = value.shape[0] // 2
        mine = jnp.where(bit == 0, value[:half], value[half:])
        other = jnp.where(bit == 0, value[half:], value[:half])
        return total(mine, exchange(other), after=after)

    def double(value, bit, exchange):
        other = exchange(value)
        return jnp.where(
            bit == 0,
            jnp.concatenate([value, other]),
            jnp.concatenate([other, value]),
        )

    got2 = to_place(total(product2, got0, after=[partial]), 2)
    partial = halve(partial, core, to_core)
    inner_sum = total(inner_weights[0], to_island(inner_weights[0]), after=[partial])
    partial = halve(partial, side, to_side, after=[inner_sum])
    partial_next = to_place(partial, 1)
    grad_rows = total(product3, got1, got2, after=[partial])
    grad_other = to_island(grad_rows)
    partial = total(partial, partial_next, after=[grad_rows])
    partial_next = to_place(partial, 2)
    partial = total(partial, partial_next, after=[grad_other])
    partial = double(partial, side, to_side)
    projected = double(partial, core, to_core)

    new_first, new_second, scale = moments_and_scale(
        projected, first_moment[0, 0], second_moment[0, 0]
    )
    scale_other = to_island(scale)
    weights_block, new_momentum = run(
        outer_kernel,
        [((rows, cols // 2), BF16), ((rows, cols), F32)],
        [flag, inner_sum, grad_rows, grad_other, scale, scale_other, global_weights, outer_momentum],
    )
    return (weights_block, new_momentum, new_first[None, None], new_second[None, None])


def solution(mesh):
    placed = (
        P("island", "fsdp", None),
        P("island", "fsdp", None),
        P("fsdp", None),
        P("island", None, None, None),
        P("island", None, None, None),
        P("island", "fsdp", None),
        P("fsdp", None),
        P("fsdp", None),
    )
    lined = mesh.shape["fsdp"] == 4 * 4 and mesh.shape["island"] == 2
    return jax.shard_map(
        line_body if lined else plain_body,
        mesh=mesh,
        in_specs=placed,
        out_specs=(
            P("fsdp", "island"),
            P("fsdp", None),
            P("island", None, None, None),
            P("island", None, None, None),
        ),
        check_vma=False,
    )
```

time: 255 us -> 105 us (0.41)
  waiting for transfers between devices: 216 us -> 56.4 us
  starting transfers between devices: 0.12 us -> 28.3 us
  between operations: 13.8 us -> 0.84 us
  Pallas kernels: 0 us -> 12.1 us
  blocking collectives: 8.9 us -> 0 us
  matrix products: 8.57 us -> 0 us
  other arithmetic: 5.12 us -> 2.42 us
    reduce_scatter x2 -> x0, waiting for transfers between devices: 125 us -> none  [the longest x1 110 us: body(): lax.psum_scatter(product, 'fsdp', scatter_dimension=0, tiled=True)]
    psum x1 -> x0, waiting for transfers between devices: 90.7 us -> none  [body(): projected = lax.psum(partial_sum, 'fsdp').reshape(LAYERS, RANK, col_total)]
    ppermute x0 -> x21, waiting for transfers between devices: none -> 56.4 us  [the longest x17 50.3 us: move(): return lax.ppermute(value, 'fsdp', pairs)]
    ppermute x0 -> x21, starting transfers between devices: none -> 28.3 us  [the longest x17 23 us: move(): return lax.ppermute(value, 'fsdp', pairs)]
    pallas_call x0 -> x18, Pallas kernels: none -> 12.1 us  [run(): pl.pallas_call(body, out_shape=[jax.ShapeDtypeStruct(shape, kind) for sha...]
    all_gather x1 -> x0, blocking collectives: 8.9 us -> none  [body(): new_momentum = lax.all_gather(momentum_block, 'island', axis=1, tiled=True)]
    dot_general x2 -> x0, matrix products: 8.57 us -> none  [the longest x1 5.53 us: body(): lax.dot_general(inputs, grads_out, (((0,), (0,)), ((), ())), preferred_el...]
  transfers between devices with their start and end apart: 3 -> 21, of which waited for: 3 -> 12; matrix products, arithmetic and copies ran while one was open for 0% -> 2% of each run, Pallas kernels for 0% -> 7%
where the time goes in v2:
time: 105 us; the launch traced here: 104 us
  waiting for transfers between devices  56.4 us (54%)
  starting transfers between devices  28.3 us (27%)
  Pallas kernels  12.1 us (12%)
  local copies, waits for them, and re-layouts  4.15 us (4%)
  other arithmetic  2.42 us (2%)
    ppermute x17, waiting for transfers between devices, move(): return lax.ppermute(value, 'fsdp', pairs)  50.3 us
    ppermute x17, starting transfers between devices, move(): return lax.ppermute(value, 'fsdp', pairs)  23 us
    pallas_call x18, Pallas kernels, run(): pl.pallas_call(body, out_shape=[jax.ShapeDtypeStruct(shape, kind) for sha...  12.1 us
    ppermute x4, waiting for transfers between devices, to_island(): return lax.ppermute(value, 'island', [(0, 1), (1, 0)])  6.08 us
    ppermute x4, starting transfers between devices, to_island(): return lax.ppermute(value, 'island', [(0, 1), (1, 0)])  5.32 us
    unnamed x22, local copies, waits for them, and re-layouts  4.01 us
  transfers between devices with their start and end apart: 21, of which 12 were waited for; matrix products, arithmetic and copies ran while one was open for 2% of the time, Pallas kernels for 7%

profile of v2, /device:TPU:0, one launch (start us, length us, event | category | flops | bytes accessed | tf_op | source)
XLA Modules:
  0.0 104.2 jit_solution(3864015978783498561)
XLA Ops:
  0.7 0.1 stack.27.refs_0_
  0.8 0.9 copy-done
  1.7 1.2 %copy-done.2 = bf16[1,128,4224]{2,1,0:T(8,128)(2,1)S(1)} copy-done((bf16[1,128,4224]{2,1,0:T(8,128)(2,1)S(1)}, bf16[1,128,4224]{2,1,0:T(8,128)(2,1)}, u32[]{:S(2)}) %copy-start.2) | copy-done | bytes 1081368
  2.9 2.1 %shard_map.111 = (f32[776,128]{1,0:T(8,128)}, f32[264,128]{1,0:T(8,128)S(1)}, f32[3,264,128]{2,1,0:T(8,128)S(1)}, f32[4,264,128]{2,1,0:T(8,128)S(1)}, f32[7,264,128]{2,1,0:T(8,128)}) custom-call(s32[6]{0:T(128)S(1)} %stack.27.refs_0_, bf16[1,128,4224]{2,1,0:T(8,128)(2,1)S(1)} %copy-done.2, bf16[1,128,512]{2,1,0:T(8,128)(2,1)S(1)} %copy-done), custom_call_target="tpu_custom_call" | custom-call | tf_op jit(solution)/shard_map/pallas_call | solution.py:95
  5.0 0.5 collective-permute-start.1
  5.4 2.5 %collective-permute-start.2 = (f32[776,128]{1,0:T(8,128)}, f32[776,128]{1,0:T(8,128)S(1)}, u32[]{:S(2)}, u32[]{:S(2)}) collective-permute-start(f32[776,128]{1,0:T(8,128)} %get-tuple-element.18), channel_id=1, source_target_pairs={{0,4},{2,6},{4,0},{6,2},{8,12},{10,14},{12,8},{14,10},{16,20},{18,... | collective-permute-start | bytes 1191944 | tf_op jit(solution)/shard_map/ppermute | solution.py:269
  7.9 0.1 collective-permute-start.3
  8.1 1.9 %collective-permute-start.5 = (f32[264,128]{1,0:T(8,128)S(1)}, f32[264,128]{1,0:T(8,128)S(1)}, u32[]{:S(2)}, u32[]{:S(2)}) collective-permute-start(f32[264,128]{1,0:T(8,128)S(1)} %shard_map.113.refs_0_), channel_id=1, source_target_pairs={{0,8},{2,10},{4,12},{6,14},{8,0},{10,2},{12,4},{14,6},{16,24},{18,... | collective-permute-start | bytes 405512 | tf_op jit(solution)/shard_map/ppermute | solution.py:269
  10.0 4.0 %collective-permute-done.5.refs_1_.refs_0_ = f32[264,128]{1,0:T(8,128)S(1)} collective-permute-done((f32[264,128]{1,0:T(8,128)S(1)}, f32[264,128]{1,0:T(8,128)S(1)}, u32[]{:S(2)}, u32[]{:S(2)}) %collective-permute-start.5) | collective-permute-done | bytes 135200 | tf_op jit(solution)/shard_map/ppermute | solution.py:269
  14.0 2.8 %collective-permute-start.6 = (f32[2,264,128]{2,1,0:T(8,128)S(1)}, f32[2,264,128]{2,1,0:T(8,128)S(1)}, u32[]{:S(2)}, u32[]{:S(2)}) collective-permute-start(f32[2,264,128]{2,1,0:T(8,128)S(1)} %shard_map.114), channel_id=1, source_target_pairs={{0,16},{2,18},{4,20},{6,22},{8,24},{10,26},{12,28},{14,30},{16,0},... | collective-permute-start | bytes 811016 | tf_op jit(solution)/shard_map/ppermute | solution.py:269
  16.8 3.9 %collective-permute-done.3.refs_2_.refs_3_ = f32[264,128]{1,0:T(8,128)S(1)} collective-permute-done((f32[264,128]{1,0:T(8,128)S(1)}, f32[264,128]{1,0:T(8,128)S(1)}, u32[]{:S(2)}, u32[]{:S(2)}) %collective-permute-start.3) | collective-permute-done | bytes 135200 | tf_op jit(solution)/shard_map/ppermute | solution.py:269
  20.8 0.2 collective-permute-start.4
  21.0 1.7 %collective-permute-start.8 = (f32[2,2,264,128]{3,2,1,0:T(8,128)S(1)}, f32[2,2,264,128]{3,2,1,0:T(8,128)}, u32[]{:S(2)}, u32[]{:S(2)}) collective-permute-start(f32[2,2,264,128]{3,2,1,0:T(8,128)S(1)} %shard_map.118), channel_id=1, source_target_pairs={{0,4},{2,6},{4,0},{6,2},{8,12},{10,14},{12,8},{14,10},{16,20},{18,... | collective-permute-start | bytes 1622024 | tf_op jit(solution)/shard_map/ppermute | solution.py:269
  22.7 6.0 %collective-permute-done.6.refs_1_ = f32[2,264,128]{2,1,0:T(8,128)S(1)} collective-permute-done((f32[2,264,128]{2,1,0:T(8,128)S(1)}, f32[2,264,128]{2,1,0:T(8,128)S(1)}, u32[]{:S(2)}, u32[]{:S(2)}) %collective-permute-start.6) | collective-permute-done | bytes 270368 | tf_op jit(solution)/shard_map/ppermute | solution.py:269
  28.8 1.6 %collective-permute-start.9 = (f32[3,264,128]{2,1,0:T(8,128)S(1)}, f32[3,264,128]{2,1,0:T(8,128)}, u32[]{:S(2)}, u32[]{:S(2)}) collective-permute-start(f32[3,264,128]{2,1,0:T(8,128)S(1)} %shard_map.115.refs_6_), channel_id=1, source_target_pairs={{0,1},{1,0},{2,3},{3,2},{4,5},{5,4},{6,7},{7,6},{8,9},{9,8},{10,11... | collective-permute-start | bytes 1216520 | tf_op jit(solution)/shard_map/ppermute | solution.py:284
  30.4 1.6 %collective-permute-start.7 = (f32[2,1,264,128]{3,2,1,0:T(8,128)S(1)}, f32[2,1,264,128]{3,2,1,0:T(8,128)}, u32[]{:S(2)}, u32[]{:S(2)}) collective-permute-start(f32[2,1,264,128]{3,2,1,0:T(8,128)S(1)} %shard_map.117), channel_id=1, source_target_pairs={{0,4},{2,6},{4,0},{6,2},{8,12},{10,14},{12,8},{14,10},{16,20},{18,... | collective-permute-start | bytes 811016 | tf_op jit(solution)/shard_map/ppermute | solution.py:269
  32.0 1.1 %shard_map.116 = (f32[264,512]{1,0:T(8,128)}, bf16[512,512]{1,0:T(8,128)(2,1)S(1)}) custom-call(f32[4,264,128]{2,1,0:T(8,128)S(1)} %get-tuple-element.16.refs_0_, f32[7,264,128]{2,1,0:T(8,128)S(1)} %collective-permute-done.1.refs_1_, f32[776,128]{1,0:T(8,128)S(1)} %collective-permute-done.2.refs_1_.refs_2_, ...), custom_call_target="tpu_custom_call" | custom-call | tf_op jit(solution)/shard_map/pallas_call | solution.py:95
  33.1 0.8 copy-done.7
  33.9 0.7 collective-permute-start.12
  34.6 7.0 %collective-permute-done.7.refs_3_ = f32[2,1,264,128]{3,2,1,0:T(8,128)} collective-permute-done((f32[2,1,264,128]{3,2,1,0:T(8,128)S(1)}, f32[2,1,264,128]{3,2,1,0:T(8,128)}, u32[]{:S(2)}, u32[]{:S(2)}) %collective-permute-start.7) | collective-permute-done | bytes 270368 | tf_op jit(solution)/shard_map/ppermute | solution.py:269
  41.6 1.0 copy-done.8
  42.6 1.7 %shard_map.119 = (f32[264,512]{1,0:T(8,128)S(1)}, f32[264,512]{1,0:T(8,128)S(1)}, f32[264,512]{1,0:T(8,128)S(1)}) custom-call(f32[4,264,128]{2,1,0:T(8,128)S(1)} %get-tuple-element.16.refs_0_, f32[7,264,128]{2,1,0:T(8,128)S(1)} %collective-permute-done.1.refs_1_, bf16[512,512]{1,0:T(8,128)(2,1)S(1)} %copy-done.8, ...), custom_call_target="tpu_custom_call" | custom-call | tf_op jit(solution)/shard_map/pallas_call | solution.py:95
  44.4 2.5 %shard_map.120.refs_2_ = f32[256,512]{1,0:T(8,128)S(1)} custom-call(f32[1,512]{1,0:T(1,128)S(1)} %broadcast_in_dim.2.refs_0_, f32[264,512]{1,0:T(8,128)} %get-tuple-element.20.refs_1_, f32[264,512]{1,0:T(8,128)S(1)} %get-tuple-element.23.refs_2_, f32[264,512]{1,0:T(8,128)S(1)} %get-tuple-element.24.refs_3_.refs_0_, ...), custom_call_target="tpu_custom_call" | custom-call | tf_op jit(solution)/shard_map/pallas_call | solution.py:95
  46.9 0.8 slice_select_fusion
  47.7 1.6 %collective-permute-start = (f32[264,512]{1,0:T(8,128)S(1)}, f32[264,512]{1,0:T(8,128)S(1)}, u32[]{:S(2)}, u32[]{:S(2)}) collective-permute-start(f32[264,512]{1,0:T(8,128)S(1)} %bitcast.34), channel_id=1, source_target_pairs={{0,1},{1,0},{2,3},{3,2},{4,5},{5,4},{6,7},{7,6},{8,9},{9,8},{10,11... | collective-permute-start | bytes 1622024 | tf_op jit(solution)/shard_map/ppermute | solution.py:284
  49.2 1.1 %shard_map.123 = f32[264,512]{1,0:T(8,128)S(1)} custom-call(f32[264,512]{1,0:T(8,128)S(1)} %get-tuple-element.24.refs_3_.refs_0_, f32[264,512]{1,0:T(8,128)} %collective-permute-done.12.refs_1_, f32[256,512]{1,0:T(8,128)S(1)} %shard_map.120.refs_2_), custom_call_target="tpu_custom_call" | custom-call | tf_op jit(solution)/shard_map/pallas_call | solution.py:95
  50.4 2.7 %collective-permute-start.13 = (f32[264,512]{1,0:T(8,128)S(1)}, f32[264,512]{1,0:T(8,128)S(1)}, u32[]{:S(2)}, u32[]{:S(2)}) collective-permute-start(f32[264,512]{1,0:T(8,128)S(1)} %shard_map.123), channel_id=1, source_target_pairs={{0,16},{2,18},{4,20},{6,22},{8,24},{10,26},{12,28},{14,30},{16,0},... | collective-permute-start | bytes 1622024 | tf_op jit(solution)/shard_map/ppermute | solution.py:269
  53.0 1.6 %collective-permute-start.11 = (f32[264,512]{1,0:T(8,128)S(1)}, f32[264,512]{1,0:T(8,128)}, u32[]{:S(2)}, u32[]{:S(2)}) collective-permute-start(f32[264,512]{1,0:T(8,128)S(1)} %get-tuple-element.23.refs_2_), channel_id=1, source_target_pairs={{0,8},{2,10},{4,12},{6,14},{8,0},{10,2},{12,4},{14,6},{16,24},{18,... | collective-permute-start | bytes 1622024 | tf_op jit(solution)/shard_map/ppermute | solution.py:269
  54.6 1.0 shard_map.121.refs_2_
  55.6 1.6 %collective-permute-start.14 = (f32[64,512]{1,0:T(8,128)S(1)}, f32[64,512]{1,0:T(8,128)S(1)}, u32[]{:S(2)}, u32[]{:S(2)}) collective-permute-start(f32[64,512]{1,0:T(8,128)S(1)} %get-tuple-element.40), channel_id=1, source_target_pairs={{0,4},{2,6},{4,0},{6,2},{8,12},{10,14},{12,8},{14,10},{16,20},{18,... | collective-permute-start | bytes 393224 | tf_op jit(solution)/shard_map/ppermute | solution.py:269
  57.2 5.2 %collective-permute-done.refs_1_ = f32[264,512]{1,0:T(8,128)S(1)} collective-permute-done((f32[264,512]{1,0:T(8,128)S(1)}, f32[264,512]{1,0:T(8,128)S(1)}, u32[]{:S(2)}, u32[]{:S(2)}) %collective-permute-start) | collective-permute-done | bytes 540704 | tf_op jit(solution)/shard_map/ppermute | solution.py:284
  62.4 0.1 shard_map.122.refs_2_.refs_1_
  62.5 15.0 %collective-permute-done.13.refs_2_ = f32[264,512]{1,0:T(8,128)S(1)} collective-permute-done((f32[264,512]{1,0:T(8,128)S(1)}, f32[264,512]{1,0:T(8,128)S(1)}, u32[]{:S(2)}, u32[]{:S(2)}) %collective-permute-start.13) | collective-permute-done | bytes 540704 | tf_op jit(solution)/shard_map/ppermute | solution.py:269
  77.4 0.3 collective-permute-done.11.refs_1_
  77.7 1.1 %shard_map.125.refs_2_ = f32[264,512]{1,0:T(8,128)S(1)} custom-call(f32[264,512]{1,0:T(8,128)S(1)} %get-tuple-element.25.refs_4_.refs_0_, f32[264,512]{1,0:T(8,128)} %collective-permute-done.11.refs_1_, f32[264,512]{1,0:T(8,128)S(1)} %collective-permute-done.13.refs_2_, f32[64,512]{1,0:T(8,128)S(1)} %shard_map.124.refs_3_.refs_0_), custom_call_target="tpu_custom_call" | custom-call | tf_op jit(solution)/shard_map/pallas_call | solution.py:95
  78.9 0.5 collective-permute-start.15
  79.4 1.5 %collective-permute-start.16 = (f32[64,512]{1,0:T(8,128)S(1)}, f32[64,512]{1,0:T(8,128)S(1)}, u32[]{:S(2)}, u32[]{:S(2)}) collective-permute-start(f32[64,512]{1,0:T(8,128)S(1)} %shard_map.124.refs_3_.refs_0_), channel_id=1, source_target_pairs={{0,8},{2,10},{4,12},{6,14},{8,0},{10,2},{12,4},{14,6},{16,24},{18,... | collective-permute-start | bytes 393224 | tf_op jit(solution)/shard_map/ppermute | solution.py:269
  80.9 3.5 %collective-permute-done.16.refs_1_ = f32[64,512]{1,0:T(8,128)S(1)} collective-permute-done((f32[64,512]{1,0:T(8,128)S(1)}, f32[64,512]{1,0:T(8,128)S(1)}, u32[]{:S(2)}, u32[]{:S(2)}) %collective-permute-start.16) | collective-permute-done | bytes 131104 | tf_op jit(solution)/shard_map/ppermute | solution.py:269
  84.4 2.2 %collective-permute-start.17 = (f32[64,512]{1,0:T(8,128)S(1)}, f32[64,512]{1,0:T(8,128)S(1)}, u32[]{:S(2)}, u32[]{:S(2)}) collective-permute-start(f32[64,512]{1,0:T(8,128)S(1)} %shard_map.126.refs_0_), channel_id=1, source_target_pairs={{0,16},{2,18},{4,20},{6,22},{8,24},{10,26},{12,28},{14,30},{16,0},... | collective-permute-start | bytes 393224 | tf_op jit(solution)/shard_map/ppermute | solution.py:269
  86.6 5.7 %collective-permute-done.17.refs_1_ = f32[64,512]{1,0:T(8,128)S(1)} collective-permute-done((f32[64,512]{1,0:T(8,128)S(1)}, f32[64,512]{1,0:T(8,128)S(1)}, u32[]{:S(2)}, u32[]{:S(2)}) %collective-permute-start.17) | collective-permute-done | bytes 131104 | tf_op jit(solution)/shard_map/ppermute | solution.py:269
  92.3 1.6 %collective-permute-start.18 = (f32[64,512]{1,0:T(8,128)S(1)}, f32[64,512]{1,0:T(8,128)S(1)}, u32[]{:S(2)}, u32[]{:S(2)}) collective-permute-start(f32[64,512]{1,0:T(8,128)S(1)} %shard_map.127), channel_id=1, source_target_pairs={{0,4},{2,6},{4,0},{6,2},{8,12},{10,14},{12,8},{14,10},{16,20},{18,... | collective-permute-start | bytes 393224 | tf_op jit(solution)/shard_map/ppermute | solution.py:269
  93.9 3.5 %collective-permute-done.18 = f32[64,512]{1,0:T(8,128)S(1)} collective-permute-done((f32[64,512]{1,0:T(8,128)S(1)}, f32[64,512]{1,0:T(8,128)S(1)}, u32[]{:S(2)}, u32[]{:S(2)}) %collective-permute-start.18) | collective-permute-done | bytes 131104 | tf_op jit(solution)/shard_map/ppermute | solution.py:269
  97.5 1.5 %collective-permute-done.19 = f32[128,512]{1,0:T(8,128)S(1)} collective-permute-done((f32[128,512]{1,0:T(8,128)S(1)}, f32[128,512]{1,0:T(8,128)S(1)}, u32[]{:S(2)}, u32[]{:S(2)}) %collective-permute-start.19) | collective-permute-done | bytes 262176 | tf_op jit(solution)/shard_map/ppermute | solution.py:269
  99.0 0.4 fusion.8
  99.4 1.6 %collective-permute-start.20 = (f32[1,512]{1,0:T(1,128)S(1)}, f32[1,512]{1,0:T(1,128)S(1)}, u32[]{:S(2)}, u32[]{:S(2)}) collective-permute-start(f32[1,512]{1,0:T(1,128)S(1)} %bitcast.36), channel_id=1, source_target_pairs={{0,1},{1,0},{2,3},{3,2},{4,5},{5,4},{6,7},{7,6},{8,9},{9,8},{10,11... | collective-permute-start | bytes 6152 | tf_op jit(solution)/shard_map/ppermute | solution.py:284
  101.0 1.2 %fusion.6 = (f32[1,1,256,512]{3,2,1,0:T(8,128)}, f32[1,1,256,512]{3,2,1,0:T(8,128)}) fusion(f32[1,1,256,512]{3,2,1,0:T(8,128)S(1)} %copy-done.9, f32[1,1,128,512]{3,2,1,0:T(8,128)S(1)} %bitcast.38, f32[1,1,128,512]{3,2,1,0:T(8,128)S(1)} %bitcast.39, pred[]{:T(512)S(6)} %eq.7, f32[1,1,256,512]{3,2,1,0:T(8,128)S(1)} %copy-done.10), kind=kLoop, calls=%fused_computation.8 | loop fusion | flops 1310720 | bytes 2621441 | tf_op jit(solution)/shard_map/add | solution.py:29
  102.2 0.9 collective-permute-done.20.refs_5_
  103.1 1.1 %shard_map.128 = (bf16[264,256]{1,0:T(8,128)(2,1)}, f32[264,512]{1,0:T(8,128)}) custom-call(f32[1,512]{1,0:T(1,128)S(1)} %broadcast_in_dim.2.refs_0_, f32[264,512]{1,0:T(8,128)S(1)} %shard_map.122.refs_2_.refs_1_, f32[264,512]{1,0:T(8,128)S(1)} %shard_map.125.refs_2_, f32[264,512]{1,0:T(8,128)S(1)} %collective-permute-done.15.refs_2_.refs_3_, ...), custom_call_target="tpu_custom_call" | custom-call | tf_op jit(solution)/shard_map/pallas_call | solution.py:95
  (44 shorter events, 0.5 us)
Async XLA Ops:
  0.8 0.9 copy-start
  1.7 1.2 %copy-start.2 = (bf16[1,128,4224]{2,1,0:T(8,128)(2,1)S(1)}, bf16[1,128,4224]{2,1,0:T(8,128)(2,1)}, u32[]{:S(2)}) copy-start(bf16[1,128,4224]{2,1,0:T(8,128)(2,1)} %refs_1_.2) | copy-start | bytes 3244036
  2.9 5.2 %copy-start.6 = (bf16[264,256]{1,0:T(8,128)(2,1)S(1)}, bf16[264,256]{1,0:T(8,128)(2,1)}, u32[]{:S(2)}) copy-start(bf16[264,256]{1,0:T(8,128)(2,1)} %refs_5_.1) | copy-start | bytes 405508
  5.0 15.7 %copy-start.1 = (bf16[1,128,512]{2,1,0:T(8,128)(2,1)S(1)}, bf16[1,128,512]{2,1,0:T(8,128)(2,1)}, u32[]{:S(2)}) copy-start(bf16[1,128,512]{2,1,0:T(8,128)(2,1)} %refs_4_.1) | copy-start | bytes 393220
  5.0 16.0 %collective-permute-start.1 = (f32[7,264,128]{2,1,0:T(8,128)}, f32[7,264,128]{2,1,0:T(8,128)S(1)}, u32[]{:S(2)}, u32[]{:S(2)}) collective-permute-start(f32[7,264,128]{2,1,0:T(8,128)} %get-tuple-element.17), channel_id=1, source_target_pairs={{0,2},{2,0},{4,6},{6,4},{8,10},{10,8},{12,14},{14,12},{16,18},{18,... | collective-permute-start | bytes 2838536 | tf_op jit(solution)/shard_map/ppermute | solution.py:269
  5.4 15.3 %collective-permute-start.2 = (f32[776,128]{1,0:T(8,128)}, f32[776,128]{1,0:T(8,128)S(1)}, u32[]{:S(2)}, u32[]{:S(2)}) collective-permute-start(f32[776,128]{1,0:T(8,128)} %get-tuple-element.18), channel_id=1, source_target_pairs={{0,4},{2,6},{4,0},{6,2},{8,12},{10,14},{12,8},{14,10},{16,20},{18,... | collective-permute-start | bytes 1191944 | tf_op jit(solution)/shard_map/ppermute | solution.py:269
  7.9 12.8 %collective-permute-start.3 = (f32[264,128]{1,0:T(8,128)S(1)}, f32[264,128]{1,0:T(8,128)S(1)}, u32[]{:S(2)}, u32[]{:S(2)}) collective-permute-start(f32[264,128]{1,0:T(8,128)S(1)} %get-tuple-element.19), channel_id=1, source_target_pairs={{0,6},{2,4},{4,2},{6,0},{8,14},{10,12},{12,10},{14,8},{16,22},{18,... | collective-permute-start | bytes 405512 | tf_op jit(solution)/shard_map/ppermute | solution.py:269
  8.1 5.9 %collective-permute-start.5 = (f32[264,128]{1,0:T(8,128)S(1)}, f32[264,128]{1,0:T(8,128)S(1)}, u32[]{:S(2)}, u32[]{:S(2)}) collective-permute-start(f32[264,128]{1,0:T(8,128)S(1)} %shard_map.113.refs_0_), channel_id=1, source_target_pairs={{0,8},{2,10},{4,12},{6,14},{8,0},{10,2},{12,4},{14,6},{16,24},{18,... | collective-permute-start | bytes 405512 | tf_op jit(solution)/shard_map/ppermute | solution.py:269
  14.0 14.7 %collective-permute-start.6 = (f32[2,264,128]{2,1,0:T(8,128)S(1)}, f32[2,264,128]{2,1,0:T(8,128)S(1)}, u32[]{:S(2)}, u32[]{:S(2)}) collective-permute-start(f32[2,264,128]{2,1,0:T(8,128)S(1)} %shard_map.114), channel_id=1, source_target_pairs={{0,16},{2,18},{4,20},{6,22},{8,24},{10,26},{12,28},{14,30},{16,0},... | collective-permute-start | bytes 811016 | tf_op jit(solution)/shard_map/ppermute | solution.py:269
  20.8 11.2 %collective-permute-start.4 = (f32[2,512,128]{2,1,0:T(8,128)S(1)}, f32[2,512,128]{2,1,0:T(8,128)S(1)}, u32[]{:S(2)}, u32[]{:S(2)}) collective-permute-start(f32[2,512,128]{2,1,0:T(8,128)S(1)} %shard_map.112.refs_2_.refs_4_), channel_id=1, source_target_pairs={{0,2},{2,0},{4,6},{6,4},{8,10},{10,8},{12,14},{14,12},{16,18},{18,... | collective-permute-start | bytes 1572872 | tf_op jit(solution)/shard_map/ppermute | solution.py:269
  21.0 20.5 %collective-permute-start.8 = (f32[2,2,264,128]{3,2,1,0:T(8,128)S(1)}, f32[2,2,264,128]{3,2,1,0:T(8,128)}, u32[]{:S(2)}, u32[]{:S(2)}) collective-permute-start(f32[2,2,264,128]{3,2,1,0:T(8,128)S(1)} %shard_map.118), channel_id=1, source_target_pairs={{0,4},{2,6},{4,0},{6,2},{8,12},{10,14},{12,8},{14,10},{16,20},{18,... | collective-permute-start | bytes 1622024 | tf_op jit(solution)/shard_map/ppermute | solution.py:269
  28.8 15.6 %collective-permute-start.9 = (f32[3,264,128]{2,1,0:T(8,128)S(1)}, f32[3,264,128]{2,1,0:T(8,128)}, u32[]{:S(2)}, u32[]{:S(2)}) collective-permute-start(f32[3,264,128]{2,1,0:T(8,128)S(1)} %shard_map.115.refs_6_), channel_id=1, source_target_pairs={{0,1},{1,0},{2,3},{3,2},{4,5},{5,4},{6,7},{7,6},{8,9},{9,8},{10,11... | collective-permute-start | bytes 1216520 | tf_op jit(solution)/shard_map/ppermute | solution.py:284
  30.4 11.1 %collective-permute-start.7 = (f32[2,1,264,128]{3,2,1,0:T(8,128)S(1)}, f32[2,1,264,128]{3,2,1,0:T(8,128)}, u32[]{:S(2)}, u32[]{:S(2)}) collective-permute-start(f32[2,1,264,128]{3,2,1,0:T(8,128)S(1)} %shard_map.117), channel_id=1, source_target_pairs={{0,4},{2,6},{4,0},{6,2},{8,12},{10,14},{12,8},{14,10},{16,20},{18,... | collective-permute-start | bytes 811016 | tf_op jit(solution)/shard_map/ppermute | solution.py:269
  33.1 0.8 copy-start.7
  33.9 15.3 %collective-permute-start.12 = (f32[264,512]{1,0:T(8,128)}, f32[264,512]{1,0:T(8,128)}, u32[]{:S(2)}, u32[]{:S(2)}) collective-permute-start(f32[264,512]{1,0:T(8,128)} %get-tuple-element.20.refs_1_), channel_id=1, source_target_pairs={{0,8},{2,10},{4,12},{6,14},{8,0},{10,2},{12,4},{14,6},{16,24},{18,... | collective-permute-start | bytes 1622024 | tf_op jit(solution)/shard_map/ppermute | solution.py:269
  41.6 1.0 %copy-start.8 = (bf16[512,512]{1,0:T(8,128)(2,1)S(1)}, bf16[512,512]{1,0:T(8,128)(2,1)}, u32[]{:S(2)}) copy-start(bf16[512,512]{1,0:T(8,128)(2,1)} %copy-done.7) | copy-start | bytes 1572868
  44.4 3.3 %copy-start.3 = (f32[1,264,512]{2,1,0:T(8,128)S(1)}, f32[1,264,512]{2,1,0:T(8,128)}, u32[]{:S(2)}) copy-start(f32[1,264,512]{2,1,0:T(8,128)} %param.13) | copy-start | bytes 1622020
  47.7 6.9 %collective-permute-start.10 = (f32[128,512]{1,0:T(8,128)}, f32[128,512]{1,0:T(8,128)}, u32[]{:S(2)}, u32[]{:S(2)}) collective-permute-start(f32[128,512]{1,0:T(8,128)} %get-tuple-element.35), channel_id=1, source_target_pairs={{0,2},{2,0},{4,6},{6,4},{8,10},{10,8},{12,14},{14,12},{16,18},{18,... | collective-permute-start | bytes 786440 | tf_op jit(solution)/shard_map/ppermute | solution.py:269
  47.7 14.7 %collective-permute-start = (f32[264,512]{1,0:T(8,128)S(1)}, f32[264,512]{1,0:T(8,128)S(1)}, u32[]{:S(2)}, u32[]{:S(2)}) collective-permute-start(f32[264,512]{1,0:T(8,128)S(1)} %bitcast.34), channel_id=1, source_target_pairs={{0,1},{1,0},{2,3},{3,2},{4,5},{5,4},{6,7},{7,6},{8,9},{9,8},{10,11... | collective-permute-start | bytes 1622024 | tf_op jit(solution)/shard_map/ppermute | solution.py:284
  50.4 27.1 %collective-permute-start.13 = (f32[264,512]{1,0:T(8,128)S(1)}, f32[264,512]{1,0:T(8,128)S(1)}, u32[]{:S(2)}, u32[]{:S(2)}) collective-permute-start(f32[264,512]{1,0:T(8,128)S(1)} %shard_map.123), channel_id=1, source_target_pairs={{0,16},{2,18},{4,20},{6,22},{8,24},{10,26},{12,28},{14,30},{16,0},... | collective-permute-start | bytes 1622024 | tf_op jit(solution)/shard_map/ppermute | solution.py:269
  53.0 24.7 %collective-permute-start.11 = (f32[264,512]{1,0:T(8,128)S(1)}, f32[264,512]{1,0:T(8,128)}, u32[]{:S(2)}, u32[]{:S(2)}) collective-permute-start(f32[264,512]{1,0:T(8,128)S(1)} %get-tuple-element.23.refs_2_), channel_id=1, source_target_pairs={{0,8},{2,10},{4,12},{6,14},{8,0},{10,2},{12,4},{14,6},{16,24},{18,... | collective-permute-start | bytes 1622024 | tf_op jit(solution)/shard_map/ppermute | solution.py:269
  55.6 6.8 %collective-permute-start.14 = (f32[64,512]{1,0:T(8,128)S(1)}, f32[64,512]{1,0:T(8,128)S(1)}, u32[]{:S(2)}, u32[]{:S(2)}) collective-permute-start(f32[64,512]{1,0:T(8,128)S(1)} %get-tuple-element.40), channel_id=1, source_target_pairs={{0,4},{2,6},{4,0},{6,2},{8,12},{10,14},{12,8},{14,10},{16,20},{18,... | collective-permute-start | bytes 393224 | tf_op jit(solution)/shard_map/ppermute | solution.py:269
  78.9 20.1 %copy-start.9 = (f32[1,1,256,512]{3,2,1,0:T(8,128)S(1)}, f32[1,1,256,512]{3,2,1,0:T(8,128)}, u32[]{:S(2)}) copy-start(f32[1,1,256,512]{3,2,1,0:T(8,128)} %param.12) | copy-start | bytes 1572868
  78.9 20.1 %copy-start.10 = (f32[1,1,256,512]{3,2,1,0:T(8,128)S(1)}, f32[1,1,256,512]{3,2,1,0:T(8,128)}, u32[]{:S(2)}) copy-start(f32[1,1,256,512]{3,2,1,0:T(8,128)} %param.11) | copy-start | bytes 1572868
  78.9 13.4 %collective-permute-start.15 = (f32[264,512]{1,0:T(8,128)S(1)}, f32[264,512]{1,0:T(8,128)S(1)}, u32[]{:S(2)}, u32[]{:S(2)}) collective-permute-start(f32[264,512]{1,0:T(8,128)S(1)} %shard_map.125.refs_2_), channel_id=1, source_target_pairs={{0,1},{1,0},{2,3},{3,2},{4,5},{5,4},{6,7},{7,6},{8,9},{9,8},{10,11... | collective-permute-start | bytes 1622024 | tf_op jit(solution)/shard_map/ppermute | solution.py:284
  79.4 5.0 %collective-permute-start.16 = (f32[64,512]{1,0:T(8,128)S(1)}, f32[64,512]{1,0:T(8,128)S(1)}, u32[]{:S(2)}, u32[]{:S(2)}) collective-permute-start(f32[64,512]{1,0:T(8,128)S(1)} %shard_map.124.refs_3_.refs_0_), channel_id=1, source_target_pairs={{0,8},{2,10},{4,12},{6,14},{8,0},{10,2},{12,4},{14,6},{16,24},{18,... | collective-permute-start | bytes 393224 | tf_op jit(solution)/shard_map/ppermute | solution.py:269
  84.4 7.9 %collective-permute-start.17 = (f32[64,512]{1,0:T(8,128)S(1)}, f32[64,512]{1,0:T(8,128)S(1)}, u32[]{:S(2)}, u32[]{:S(2)}) collective-permute-start(f32[64,512]{1,0:T(8,128)S(1)} %shard_map.126.refs_0_), channel_id=1, source_target_pairs={{0,16},{2,18},{4,20},{6,22},{8,24},{10,26},{12,28},{14,30},{16,0},... | collective-permute-start | bytes 393224 | tf_op jit(solution)/shard_map/ppermute | solution.py:269
  92.3 5.0 %collective-permute-start.18 = (f32[64,512]{1,0:T(8,128)S(1)}, f32[64,512]{1,0:T(8,128)S(1)}, u32[]{:S(2)}, u32[]{:S(2)}) collective-permute-start(f32[64,512]{1,0:T(8,128)S(1)} %shard_map.127), channel_id=1, source_target_pairs={{0,4},{2,6},{4,0},{6,2},{8,12},{10,14},{12,8},{14,10},{16,20},{18,... | collective-permute-start | bytes 393224 | tf_op jit(solution)/shard_map/ppermute | solution.py:269
  97.4 1.6 %collective-permute-start.19 = (f32[128,512]{1,0:T(8,128)S(1)}, f32[128,512]{1,0:T(8,128)S(1)}, u32[]{:S(2)}, u32[]{:S(2)}) collective-permute-start(f32[128,512]{1,0:T(8,128)S(1)} %maximum_select_fusion.2), channel_id=1, source_target_pairs={{0,2},{2,0},{4,6},{6,4},{8,10},{10,8},{12,14},{14,12},{16,18},{18,... | collective-permute-start | bytes 786440 | tf_op jit(solution)/shard_map/ppermute | solution.py:269
  99.4 3.6 %collective-permute-start.20 = (f32[1,512]{1,0:T(1,128)S(1)}, f32[1,512]{1,0:T(1,128)S(1)}, u32[]{:S(2)}, u32[]{:S(2)}) collective-permute-start(f32[1,512]{1,0:T(1,128)S(1)} %bitcast.36), channel_id=1, source_target_pairs={{0,1},{1,0},{2,3},{3,2},{4,5},{5,4},{6,7},{7,6},{8,9},{9,8},{10,11... | collective-permute-start | bytes 6152 | tf_op jit(solution)/shard_map/ppermute | solution.py:284
  101.0 2.1 %copy-start.4 = (f32[264,512]{1,0:T(8,128)S(1)}, f32[264,512]{1,0:T(8,128)}, u32[]{:S(2)}) copy-start(f32[264,512]{1,0:T(8,128)} %refs_6_.1) | copy-start | bytes 1622020
  101.0 2.1 %copy-start.5 = (f32[264,512]{1,0:T(8,128)S(1)}, f32[264,512]{1,0:T(8,128)}, u32[]{:S(2)}) copy-start(f32[264,512]{1,0:T(8,128)} %refs_7_.1) | copy-start | bytes 1622020

commit v3 on v2

--- a/solution.py
+++ b/solution.py
@@ -1,3 +1,5 @@
+import functools
+
 import jax
 import jax.numpy as jnp
 from jax import lax
@@ -112,7 +114,7 @@
 BF16 = jnp.bfloat16
 
 
-def turn_kernel(at, a_ref, g_ref, first, far, rest, here, cores, turned):
+def turn_kernel(at, a_ref, g_ref, first, far, rest, here, cores, passed, turned):
     tokens, features = a_ref.shape[1:]
     cols = g_ref.shape[2]
     line, rows = here.shape[:2]
@@ -135,7 +137,7 @@
         cores[k] = block(k, side, 1 - core)
         if k:
             rest[k - 1] = block(k, 1 - side, core)
-            cores[line + k - 1] = block(k, 1 - side, 1 - core)
+            passed[k - 1] = block(k, 1 - side, 1 - core)
 
 
 def pair_kernel(*refs):
@@ -149,9 +151,10 @@
         refs[-1][i] = ref[...]
 
 
-def gather_kernel(near, away, out):
-    out[0] = near[...]
-    out[1:] = away[...]
+def gather_kernel(mid, odd, out):
+    out[0] = odd[0]
+    out[1] = mid[...]
+    out[2] = odd[1]
 
 
 def half_kernel(flag, value, out):
@@ -183,11 +186,9 @@
     out[...] = jnp.dot(a, grads[...], preferred_element_type=F32)
 
 
-def product_kernel(here, core_a, grads, *refs):
-    outs = refs[len(refs) - (here.shape[0] - 1) :]
-    crossed = [(ref, i) for ref in refs[: -len(outs)] for i in range(ref.shape[1])]
-    for k, (out, (ref, i)) in enumerate(zip(outs, crossed)):
-        pieces = (here[k + 1], core_a[k + 1], ref[0, i], ref[1, i])
+def product_kernel(k, here, core_a, crossed, grads, *outs):
+    for i, out in enumerate(outs):
+        pieces = (here[k + i], core_a[k + i], crossed[0, i], crossed[1, i])
         a = jnp.concatenate([piece.astype(BF16) for piece in pieces], axis=1)
         out[...] = jnp.dot(a, grads[...], preferred_element_type=F32)
 
@@ -288,14 +289,15 @@
     flag = jnp.full((1, cols), island, F32)
 
     block_shape = (rows, tokens)
-    first, far, rest, here, cores = run(
+    first, far, rest, here, cores, passed = run(
         turn_kernel,
         [
             ((cols + rows, tokens), F32),
             (block_shape, F32),
             ((line - 1, *block_shape), F32),
             ((line, *block_shape), F32),
-            ((2 * line - 1, *block_shape), F32),
+            ((line, *block_shape), F32),
+            ((line - 1, *block_shape), F32),
         ],
         [activations, out_grads],
         scalars=at,
@@ -304,6 +306,7 @@
     first = to_side(first)
     far = to_far(far)
     from_core = to_core(cores)
+    passed = to_core(passed)
 
     def blocks_of(start, count):
         return pl.BlockSpec((count, *block_shape), lambda *_: (start // count, 0, 0))
@@ -311,7 +314,7 @@
     def cross(k, count, after):
         parts = []
         for i in range(count):
-            parts += [rest[k - 1 + i], from_core[line + k - 1 + i]]
+            parts += [rest[k - 1 + i], passed[k - 1 + i]]
         (paired,) = run(
             pair_kernel, [((2, count, *block_shape), F32)], parts, after=after
         )
@@ -322,44 +325,47 @@
 
     half_rank = (rows, rank // 2)
     (proj_half,) = run(half_kernel, [(half_rank, F32)], [flag, projection])
-    proj_near = to_place(proj_half, 1)
-    (proj_two,) = run(stack_kernel, [((2, *half_rank), F32)], [proj_half, proj_near])
-    proj_away = to_place(proj_two, 2)
+    proj_mid = to_place(proj_half, 2)
+    (proj_two,) = run(stack_kernel, [((2, *half_rank), F32)], [proj_half, proj_mid])
+    proj_odd = to_place(proj_two, 1)
     (grads_two,) = run(
-        two_kernel, [((2, cols, tokens), F32)], [out_grads, first], after=[far]
+        two_kernel, [((2, cols, tokens), F32)], [out_grads, first], after=[far, proj_odd]
     )
     grads_core = to_core(grads_two)
-    (proj_stack,) = run(
-        gather_kernel, [((3, *half_rank), F32)], [proj_near, proj_away], after=[grads_two]
-    )
-    proj_others = to_island(proj_stack)
-    crossed = [cross(1, 1, [grads_two]), cross(2, line - 2, [grads_two])]
     product0, grads = run(
         first_product_kernel,
         [((rows, cols), F32), ((4 * tokens, cols), BF16)],
         [here, from_core, first, far, out_grads, grads_core],
-        after=[proj_stack],
         blocks={0: blocks_of(0, 1), 1: blocks_of(0, 1)},
     )
     got0 = to_place(product0, 1)
-    product1, product2, product3 = run(
-        product_kernel,
-        [((rows, cols), F32)] * (line - 1),
-        [here, from_core, grads, *crossed],
-    )
+    crossed12 = cross(1, 2, [grads_two])
+    crossed3 = cross(3, 1, [product0])
+    (proj_stack,) = run(
+        gather_kernel, [((3, *half_rank), F32)], [proj_mid, proj_odd], after=[product0]
+    )
+    proj_others = to_island(proj_stack)
+
+    def multiply(k, count, crossed, after):
+        return run(
+            functools.partial(product_kernel, k),
+            [((rows, cols), F32)] * count,
+            [here, from_core, crossed, grads],
+            after=after,
+        )
+
+    inner_sum = total(inner_weights[0], to_island(inner_weights[0]), after=[proj_stack])
+    product1, product2 = multiply(1, 2, crossed12, [inner_sum])
     got1 = to_place(product1, 1)
+    sum2 = total(product2, got0, after=[product1])
+    got2 = to_place(sum2, 2)
+    (product3,) = multiply(3, 1, crossed3, [sum2])
 
     (partial,) = run(
         lift_kernel,
         [((rank, cols), F32)],
         [flag, product0, product1, product2, product3, projection, proj_stack, proj_others],
     )
-
-    def halve(value, bit, exchange, after=()):
-        half = value.shape[0] // 2
-        mine = jnp.where(bit == 0, value[:half], value[half:])
-        other = jnp.where(bit == 0, value[half:], value[:half])
-        return total(mine, exchange(other), after=after)
 
     def double(value, bit, exchange):
         other = exchange(value)
@@ -369,14 +375,22 @@
             jnp.concatenate([other, value]),
         )
 
-    got2 = to_place(total(product2, got0, after=[partial]), 2)
-    partial = halve(partial, core, to_core)
-    inner_sum = total(inner_weights[0], to_island(inner_weights[0]), after=[partial])
-    partial = halve(partial, side, to_side, after=[inner_sum])
+    def halves(value, bit):
+        half = value.shape[0] // 2
+        low, high = value[:half], value[half:]
+        return jnp.where(bit == 0, low, high), jnp.where(bit == 0, high, low)
+
+    quarters = partial.reshape(2, 2, rank // 4, cols)
+    mine = jnp.where(side == 0, quarters[:, 0], quarters[:, 1]).reshape(rank // 2, cols)
+    theirs = jnp.where(side == 0, quarters[:, 1], quarters[:, 0]).reshape(rank // 2, cols)
+    theirs = to_side(theirs)
+    grad_rows = total(product3, got1, got2, after=[partial])
+    partial = total(mine, theirs, after=[grad_rows])
+    mine, theirs = halves(partial, core)
+    partial = total(mine, to_core(theirs))
     partial_next = to_place(partial, 1)
-    grad_rows = total(product3, got1, got2, after=[partial])
     grad_other = to_island(grad_rows)
-    partial = total(partial, partial_next, after=[grad_rows])
+    partial = total(partial, partial_next)
     partial_next = to_place(partial, 2)
     partial = total(partial, partial_next, after=[grad_other])
     partial = double(partial, side, to_side)

time: 105 us -> 97.7 us (0.930)
  starting transfers between devices: 28.3 us -> 23.4 us
  Pallas kernels: 12.1 us -> 10.4 us
    ppermute x17 -> x18, starting transfers between devices: 23 us -> 19.1 us  [move(): return lax.ppermute(value, 'fsdp', pairs)]
    ppermute x4, waiting for transfers between devices: 6.08 us -> 8.64 us  [to_island(): return lax.ppermute(value, 'island', [(0, 1), (1, 0)])]
    ppermute x17 -> x18, waiting for transfers between devices: 50.3 us -> 48 us  [move(): return lax.ppermute(value, 'fsdp', pairs)]
    pallas_call x18 -> x19, Pallas kernels: 12.1 us -> 10.4 us  [run(): pl.pallas_call(body, out_shape=[jax.ShapeDtypeStruct(shape, kind) for sha...]
    ppermute x4, starting transfers between devices: 5.32 us -> 4.24 us  [to_island(): return lax.ppermute(value, 'island', [(0, 1), (1, 0)])]
    unnamed x22 -> x28, local copies, waits for them, and re-layouts: 4.01 us -> 4.13 us
  transfers between devices with their start and end apart: 21 -> 22, of which waited for: 12 -> 13; matrix products, arithmetic and copies ran while one was open for 2% -> 1% of each run, Pallas kernels for 7% -> 10%
where the time goes in v3:
time: 97.7 us; the launch traced here: 97.3 us
  waiting for transfers between devices  56.7 us (58%)
  starting transfers between devices  23.4 us (24%)
  Pallas kernels  10.4 us (11%)
  local copies, waits for them, and re-layouts  4.27 us (4%)
  other arithmetic  1.71 us (2%)
    ppermute x18, waiting for transfers between devices, move(): return lax.ppermute(value, 'fsdp', pairs)  48 us
    ppermute x18, starting transfers between devices, move(): return lax.ppermute(value, 'fsdp', pairs)  19.1 us
    pallas_call x19, Pallas kernels, run(): pl.pallas_call(body, out_shape=[jax.ShapeDtypeStruct(shape, kind) for sha...  10.4 us
    ppermute x4, waiting for transfers between devices, to_island(): return lax.ppermute(value, 'island', [(0, 1), (1, 0)])  8.64 us
    ppermute x4, starting transfers between devices, to_island(): return lax.ppermute(value, 'island', [(0, 1), (1, 0)])  4.24 us
    unnamed x28, local copies, waits for them, and re-layouts  4.13 us
  transfers between devices with their start and end apart: 22, of which 13 were waited for; matrix products, arithmetic and copies ran while one was open for 1% of the time, Pallas kernels for 10%

profile of v3, /device:TPU:0, one launch (start us, length us, event | category | flops | bytes accessed | tf_op | source)
XLA Modules:
  0.0 97.3 jit_solution(7512739364709508608)
XLA Ops:
  0.7 0.9 copy-done.10
  1.6 4.1 %collective-permute-start.1 = (f32[264,128]{1,0:T(8,128)S(1)}, f32[264,128]{1,0:T(8,128)S(1)}, u32[]{:S(2)}, u32[]{:S(2)}) collective-permute-start(f32[264,128]{1,0:T(8,128)S(1)} %shard_map.111.refs_0_), channel_id=1, source_target_pairs={{0,16},{2,18},{4,20},{6,22},{8,24},{10,26},{12,28},{14,30},{16,0},... | collective-permute-start | bytes 405512 | tf_op jit(solution)/shard_map/ppermute | solution.py:270
  5.7 0.1 stack.27.refs_0_
  5.8 0.9 copy-done.4
  6.7 1.2 %copy-done.6 = bf16[1,128,4224]{2,1,0:T(8,128)(2,1)S(1)} copy-done((bf16[1,128,4224]{2,1,0:T(8,128)(2,1)S(1)}, bf16[1,128,4224]{2,1,0:T(8,128)(2,1)}, u32[]{:S(2)}) %copy-start.6) | copy-done | bytes 1081368
  7.9 1.1 %shard_map.113 = (f32[776,128]{1,0:T(8,128)S(1)}, f32[264,128]{1,0:T(8,128)S(1)}, f32[3,264,128]{2,1,0:T(8,128)S(1)}, f32[4,264,128]{2,1,0:T(8,128)S(1)}, f32[4,...) custom-call(s32[6]{0:T(128)S(1)} %stack.27.refs_0_, bf16[1,128,4224]{2,1,0:T(8,128)(2,1)S(1)} %copy-done.6, ...), custom_call_target="tpu_custom_call" | custom-call | tf_op jit(solution)/shard_map/pallas_call | solution.py:97
  9.0 1.6 %collective-permute-start.4 = (f32[776,128]{1,0:T(8,128)S(1)}, f32[776,128]{1,0:T(8,128)S(1)}, u32[]{:S(2)}, u32[]{:S(2)}) collective-permute-start(f32[776,128]{1,0:T(8,128)S(1)} %get-tuple-element.18), channel_id=1, source_target_pairs={{0,4},{2,6},{4,0},{6,2},{8,12},{10,14},{12,8},{14,10},{16,20},{18,... | collective-permute-start | bytes 1191944 | tf_op jit(solution)/shard_map/ppermute | solution.py:270
  10.5 1.6 %collective-permute-done.1.refs_1_.refs_0_ = f32[264,128]{1,0:T(8,128)S(1)} collective-permute-done((f32[264,128]{1,0:T(8,128)S(1)}, f32[264,128]{1,0:T(8,128)S(1)}, u32[]{:S(2)}, u32[]{:S(2)}) %collective-permute-start.1) | collective-permute-done | bytes 135200 | tf_op jit(solution)/shard_map/ppermute | solution.py:270
  12.2 0.8 collective-permute-start.2
  13.0 0.8 collective-permute-start.5
  13.8 0.8 collective-permute-start.7
  14.6 7.0 %collective-permute-done.5.refs_2_.refs_3_ = f32[264,128]{1,0:T(8,128)S(1)} collective-permute-done((f32[264,128]{1,0:T(8,128)S(1)}, f32[264,128]{1,0:T(8,128)S(1)}, u32[]{:S(2)}, u32[]{:S(2)}) %collective-permute-start.5) | collective-permute-done | bytes 135200 | tf_op jit(solution)/shard_map/ppermute | solution.py:270
  21.7 0.9 collective-permute-start.6
  22.6 1.5 %collective-permute-start = (f32[264,512]{1,0:T(8,128)S(1)}, f32[264,512]{1,0:T(8,128)S(1)}, u32[]{:S(2)}, u32[]{:S(2)}) collective-permute-start(f32[264,512]{1,0:T(8,128)S(1)} %bitcast.51), channel_id=1, source_target_pairs={{0,1},{1,0},{2,3},{3,2},{4,5},{5,4},{6,7},{7,6},{8,9},{9,8},{10,11... | collective-permute-start | bytes 1622024 | tf_op jit(solution)/shard_map/ppermute | solution.py:285
  24.2 1.6 %collective-permute-start.9 = (f32[2,2,264,128]{3,2,1,0:T(8,128)S(1)}, f32[2,2,264,128]{3,2,1,0:T(8,128)S(1)}, u32[]{:S(2)}, u32[]{:S(2)}) collective-permute-start(f32[2,2,264,128]{3,2,1,0:T(8,128)S(1)} %shard_map.119), channel_id=1, source_target_pairs={{0,4},{2,6},{4,0},{6,2},{8,12},{10,14},{12,8},{14,10},{16,20},{18,... | collective-permute-start | bytes 1622024 | tf_op jit(solution)/shard_map/ppermute | solution.py:270
  25.8 0.3 shard_map.115
  26.1 1.6 %collective-permute-start.10 = (f32[264,512]{1,0:T(8,128)S(1)}, f32[264,512]{1,0:T(8,128)S(1)}, u32[]{:S(2)}, u32[]{:S(2)}) collective-permute-start(f32[264,512]{1,0:T(8,128)S(1)} %get-tuple-element.20.refs_2_.refs_1_), channel_id=1, source_target_pairs={{0,8},{2,10},{4,12},{6,14},{8,0},{10,2},{12,4},{14,6},{16,24},{18,... | collective-permute-start | bytes 1622024 | tf_op jit(solution)/shard_map/ppermute | solution.py:270
  27.8 0.6 collective-permute-start.13
  28.4 0.7 shard_map.118
  29.1 0.8 collective-permute-start.8
  29.9 7.7 %collective-permute-done.refs_1_ = f32[264,512]{1,0:T(8,128)S(1)} collective-permute-done((f32[264,512]{1,0:T(8,128)S(1)}, f32[264,512]{1,0:T(8,128)S(1)}, u32[]{:S(2)}, u32[]{:S(2)}) %collective-permute-start) | collective-permute-done | bytes 540704 | tf_op jit(solution)/shard_map/ppermute | solution.py:285
  37.7 1.7 %collective-permute-done.9.refs_2_ = f32[2,2,264,128]{3,2,1,0:T(8,128)S(1)} collective-permute-done((f32[2,2,264,128]{3,2,1,0:T(8,128)S(1)}, f32[2,2,264,128]{3,2,1,0:T(8,128)S(1)}, u32[]{:S(2)}, u32[]{:S(2)}) %collective-permute-start.9) | collective-permute-done | bytes 540704 | tf_op jit(solution)/shard_map/ppermute | solution.py:270
  39.4 1.1 %shard_map.120 = (f32[264,512]{1,0:T(8,128)}, f32[264,512]{1,0:T(8,128)S(1)}) custom-call(f32[4,264,128]{2,1,0:T(8,128)S(1)} %get-tuple-element.16.refs_0_, f32[4,264,128]{2,1,0:T(8,128)S(1)} %collective-permute-done.3.refs_1_, f32[2,2,264,128]{3,2,1,0:T(8,128)S(1)} %collective-permute-done.9.refs_2_, bf16[512,512]{1,0:T(8,128)(2,1)S(1)} %get-tuple-element.23.refs_3_, ...), custom_call_target="tpu_custom_call" | custom-call | tf_op jit(solution)/shard_map/pallas_call | solution.py:97
  40.6 1.6 %collective-permute-start.11 = (f32[264,512]{1,0:T(8,128)}, f32[264,512]{1,0:T(8,128)}, u32[]{:S(2)}, u32[]{:S(2)}) collective-permute-start(f32[264,512]{1,0:T(8,128)} %get-tuple-element.25.refs_2_), channel_id=1, source_target_pairs={{0,8},{2,10},{4,12},{6,14},{8,0},{10,2},{12,4},{14,6},{16,24},{18,... | collective-permute-start | bytes 1622024 | tf_op jit(solution)/shard_map/ppermute | solution.py:270
  42.2 0.9 shard_map.121.refs_4_
  43.0 0.8 collective-permute-start.12
  43.8 0.4 collective-permute-done.8.refs_2_
  44.2 1.0 %copy-done.3 = bf16[512,512]{1,0:T(8,128)(2,1)S(1)} copy-done((bf16[512,512]{1,0:T(8,128)(2,1)S(1)}, bf16[512,512]{1,0:T(8,128)(2,1)}, u32[]{:S(2)}) %copy-start.3) | copy-done | bytes 524312
  45.2 1.3 %shard_map.122.refs_4_.refs_0_ = f32[264,512]{1,0:T(8,128)S(1)} custom-call(f32[4,264,128]{2,1,0:T(8,128)S(1)} %get-tuple-element.16.refs_0_, f32[4,264,128]{2,1,0:T(8,128)S(1)} %collective-permute-done.3.refs_1_, f32[2,1,264,128]{3,2,1,0:T(8,128)} %collective-permute-done.8.refs_2_, bf16[512,512]{1,0:T(8,128)(2,1)S(1)} %copy-done.3, ...), custom_call_target="tpu_custom_call" | custom-call | tf_op jit(solution)/shard_map/pallas_call | solution.py:97
  46.5 2.4 %shard_map.123.refs_3_ = f32[256,512]{1,0:T(8,128)S(1)} custom-call(f32[1,512]{1,0:T(1,128)S(1)} %broadcast_in_dim.2.refs_0_, f32[264,512]{1,0:T(8,128)S(1)} %get-tuple-element.20.refs_2_.refs_1_, f32[264,512]{1,0:T(8,128)} %get-tuple-element.25.refs_2_, f32[264,512]{1,0:T(8,128)S(1)} %copy-done.1, f32[264,512]{1,0:T(8,128)S(1)} %shard_map.122.refs_4_.refs_0_, ...), custom_call_target="tpu_custom_call" | custom-call | tf_op jit(solution)/shard_map/pallas_call | solution.py:97
  49.0 1.6 %collective-permute-start.15 = (f32[128,512]{1,0:T(8,128)S(1)}, f32[128,512]{1,0:T(8,128)S(1)}, u32[]{:S(2)}, u32[]{:S(2)}) collective-permute-start(f32[128,512]{1,0:T(8,128)S(1)} %bitcast.57), channel_id=1, source_target_pairs={{0,4},{2,6},{4,0},{6,2},{8,12},{10,14},{12,8},{14,10},{16,20},{18,... | collective-permute-start | bytes 786440 | tf_op jit(solution)/shard_map/ppermute | solution.py:270
  50.5 11.7 %collective-permute-done.11.refs_1_ = f32[264,512]{1,0:T(8,128)} collective-permute-done((f32[264,512]{1,0:T(8,128)}, f32[264,512]{1,0:T(8,128)}, u32[]{:S(2)}, u32[]{:S(2)}) %collective-permute-start.11) | collective-permute-done | bytes 540704 | tf_op jit(solution)/shard_map/ppermute | solution.py:270
  62.2 5.3 %collective-permute-done.12.refs_2_ = f32[264,512]{1,0:T(8,128)} collective-permute-done((f32[264,512]{1,0:T(8,128)}, f32[264,512]{1,0:T(8,128)}, u32[]{:S(2)}, u32[]{:S(2)}) %collective-permute-start.12) | collective-permute-done | bytes 540704 | tf_op jit(solution)/shard_map/ppermute | solution.py:270
  67.5 1.3 %shard_map.124.refs_2_ = f32[264,512]{1,0:T(8,128)S(1)} custom-call(f32[264,512]{1,0:T(8,128)S(1)} %shard_map.122.refs_4_.refs_0_, f32[264,512]{1,0:T(8,128)} %collective-permute-done.11.refs_1_, f32[264,512]{1,0:T(8,128)} %collective-permute-done.12.refs_2_, f32[256,512]{1,0:T(8,128)S(1)} %shard_map.123.refs_3_), custom_call_target="tpu_custom_call" | custom-call | tf_op jit(solution)/shard_map/pallas_call | solution.py:97
  68.8 0.6 collective-permute-start.14
  69.5 1.3 %collective-permute-done.16.refs_1_ = f32[64,512]{1,0:T(8,128)S(1)} collective-permute-done((f32[64,512]{1,0:T(8,128)S(1)}, f32[64,512]{1,0:T(8,128)S(1)}, u32[]{:S(2)}, u32[]{:S(2)}) %collective-permute-start.16) | collective-permute-done | bytes 131104 | tf_op jit(solution)/shard_map/ppermute | solution.py:270
  70.9 0.1 collective-permute-start.17
  71.0 5.5 %collective-permute-done.17.refs_1_ = f32[64,512]{1,0:T(8,128)S(1)} collective-permute-done((f32[64,512]{1,0:T(8,128)S(1)}, f32[64,512]{1,0:T(8,128)S(1)}, u32[]{:S(2)}, u32[]{:S(2)}) %collective-permute-start.17) | collective-permute-done | bytes 131104 | tf_op jit(solution)/shard_map/ppermute | solution.py:270
  76.5 0.4 collective-permute-start.18
  76.9 8.1 %collective-permute-done.18.refs_1_ = f32[64,512]{1,0:T(8,128)S(1)} collective-permute-done((f32[64,512]{1,0:T(8,128)S(1)}, f32[64,512]{1,0:T(8,128)S(1)}, u32[]{:S(2)}, u32[]{:S(2)}) %collective-permute-start.18) | collective-permute-done | bytes 131104 | tf_op jit(solution)/shard_map/ppermute | solution.py:270
  85.0 1.7 %collective-permute-start.19 = (f32[64,512]{1,0:T(8,128)S(1)}, f32[64,512]{1,0:T(8,128)S(1)}, u32[]{:S(2)}, u32[]{:S(2)}) collective-permute-start(f32[64,512]{1,0:T(8,128)S(1)} %shard_map.128), channel_id=1, source_target_pairs={{0,4},{2,6},{4,0},{6,2},{8,12},{10,14},{12,8},{14,10},{16,20},{18,... | collective-permute-start | bytes 393224 | tf_op jit(solution)/shard_map/ppermute | solution.py:270
  86.7 3.8 %collective-permute-done.19 = f32[64,512]{1,0:T(8,128)S(1)} collective-permute-done((f32[64,512]{1,0:T(8,128)S(1)}, f32[64,512]{1,0:T(8,128)S(1)}, u32[]{:S(2)}, u32[]{:S(2)}) %collective-permute-start.19) | collective-permute-done | bytes 131104 | tf_op jit(solution)/shard_map/ppermute | solution.py:270
  90.6 1.5 %collective-permute-done.20 = f32[128,512]{1,0:T(8,128)S(1)} collective-permute-done((f32[128,512]{1,0:T(8,128)S(1)}, f32[128,512]{1,0:T(8,128)S(1)}, u32[]{:S(2)}, u32[]{:S(2)}) %collective-permute-start.20) | collective-permute-done | bytes 262176 | tf_op jit(solution)/shard_map/ppermute | solution.py:270
  92.1 0.4 fusion.8
  92.6 1.6 %collective-permute-start.21 = (f32[1,512]{1,0:T(1,128)S(1)}, f32[1,512]{1,0:T(1,128)S(1)}, u32[]{:S(2)}, u32[]{:S(2)}) collective-permute-start(f32[1,512]{1,0:T(1,128)S(1)} %bitcast.53), channel_id=1, source_target_pairs={{0,1},{1,0},{2,3},{3,2},{4,5},{5,4},{6,7},{7,6},{8,9},{9,8},{10,11... | collective-permute-start | bytes 6152 | tf_op jit(solution)/shard_map/ppermute | solution.py:285
  94.2 1.2 %fusion.6 = (f32[1,1,256,512]{3,2,1,0:T(8,128)}, f32[1,1,256,512]{3,2,1,0:T(8,128)}) fusion(f32[1,1,256,512]{3,2,1,0:T(8,128)S(1)} %copy-done.12, f32[1,1,128,512]{3,2,1,0:T(8,128)S(1)} %bitcast.55, f32[1,1,128,512]{3,2,1,0:T(8,128)S(1)} %bitcast.56, pred[]{:T(512)S(6)} %eq.7, f32[1,1,256,512]{3,2,1,0:T(8,128)S(1)} %copy-done.13), kind=kLoop, calls=%fused_computation.8 | loop fusion | flops 1310720 | bytes 2621441 | tf_op jit(solution)/shard_map/add | solution.py:31
  95.3 0.9 collective-permute-done.21.refs_5_
  96.2 1.1 %shard_map.129 = (bf16[264,256]{1,0:T(8,128)(2,1)}, f32[264,512]{1,0:T(8,128)}) custom-call(f32[1,512]{1,0:T(1,128)S(1)} %broadcast_in_dim.2.refs_0_, f32[264,512]{1,0:T(8,128)S(1)} %shard_map.117.refs_4_.refs_1_, f32[264,512]{1,0:T(8,128)S(1)} %shard_map.124.refs_2_, f32[264,512]{1,0:T(8,128)S(1)} %collective-permute-done.14.refs_2_.refs_3_, ...), custom_call_target="tpu_custom_call" | custom-call | tf_op jit(solution)/shard_map/pallas_call | solution.py:97
  (53 shorter events, 0.6 us)
Async XLA Ops:
  0.6 0.9 copy-start.10
  1.6 10.6 %collective-permute-start.1 = (f32[264,128]{1,0:T(8,128)S(1)}, f32[264,128]{1,0:T(8,128)S(1)}, u32[]{:S(2)}, u32[]{:S(2)}) collective-permute-start(f32[264,128]{1,0:T(8,128)S(1)} %shard_map.111.refs_0_), channel_id=1, source_target_pairs={{0,16},{2,18},{4,20},{6,22},{8,24},{10,26},{12,28},{14,30},{16,0},... | collective-permute-start | bytes 405512 | tf_op jit(solution)/shard_map/ppermute | solution.py:270
  5.8 0.9 copy-start.4
  6.7 1.2 %copy-start.6 = (bf16[1,128,4224]{2,1,0:T(8,128)(2,1)S(1)}, bf16[1,128,4224]{2,1,0:T(8,128)(2,1)}, u32[]{:S(2)}) copy-start(bf16[1,128,4224]{2,1,0:T(8,128)(2,1)} %refs_1_.3) | copy-start | bytes 3244036
  9.0 13.6 %copy-start.7 = (f32[1,264,512]{2,1,0:T(8,128)S(1)}, f32[1,264,512]{2,1,0:T(8,128)}, u32[]{:S(2)}) copy-start(f32[1,264,512]{2,1,0:T(8,128)} %param.13) | copy-start | bytes 1622020
  9.0 12.6 %collective-permute-start.4 = (f32[776,128]{1,0:T(8,128)S(1)}, f32[776,128]{1,0:T(8,128)S(1)}, u32[]{:S(2)}, u32[]{:S(2)}) collective-permute-start(f32[776,128]{1,0:T(8,128)S(1)} %get-tuple-element.18), channel_id=1, source_target_pairs={{0,4},{2,6},{4,0},{6,2},{8,12},{10,14},{12,8},{14,10},{16,20},{18,... | collective-permute-start | bytes 1191944 | tf_op jit(solution)/shard_map/ppermute | solution.py:270
  12.2 9.5 %collective-permute-start.2 = (f32[2,264,128]{2,1,0:T(8,128)S(1)}, f32[2,264,128]{2,1,0:T(8,128)S(1)}, u32[]{:S(2)}, u32[]{:S(2)}) collective-permute-start(f32[2,264,128]{2,1,0:T(8,128)S(1)} %shard_map.112), channel_id=1, source_target_pairs={{0,8},{2,10},{4,12},{6,14},{8,0},{10,2},{12,4},{14,6},{16,24},{18,... | collective-permute-start | bytes 811016 | tf_op jit(solution)/shard_map/ppermute | solution.py:270
  13.0 8.7 %collective-permute-start.5 = (f32[264,128]{1,0:T(8,128)S(1)}, f32[264,128]{1,0:T(8,128)S(1)}, u32[]{:S(2)}, u32[]{:S(2)}) collective-permute-start(f32[264,128]{1,0:T(8,128)S(1)} %get-tuple-element.19), channel_id=1, source_target_pairs={{0,6},{2,4},{4,2},{6,0},{8,14},{10,12},{12,10},{14,8},{16,22},{18,... | collective-permute-start | bytes 405512 | tf_op jit(solution)/shard_map/ppermute | solution.py:270
  13.8 10.3 %collective-permute-start.7 = (f32[3,264,128]{2,1,0:T(8,128)S(1)}, f32[3,264,128]{2,1,0:T(8,128)S(1)}, u32[]{:S(2)}, u32[]{:S(2)}) collective-permute-start(f32[3,264,128]{2,1,0:T(8,128)S(1)} %get-tuple-element.22), channel_id=1, source_target_pairs={{0,2},{2,0},{4,6},{6,4},{8,10},{10,8},{12,14},{14,12},{16,18},{18,... | collective-permute-start | bytes 1216520 | tf_op jit(solution)/shard_map/ppermute | solution.py:270
  14.6 11.2 %collective-permute-start.3 = (f32[4,264,128]{2,1,0:T(8,128)S(1)}, f32[4,264,128]{2,1,0:T(8,128)S(1)}, u32[]{:S(2)}, u32[]{:S(2)}) collective-permute-start(f32[4,264,128]{2,1,0:T(8,128)S(1)} %get-tuple-element.17), channel_id=1, source_target_pairs={{0,2},{2,0},{4,6},{6,4},{8,10},{10,8},{12,14},{14,12},{16,18},{18,... | collective-permute-start | bytes 1622024 | tf_op jit(solution)/shard_map/ppermute | solution.py:270
  21.7 4.1 %collective-permute-start.6 = (f32[2,512,128]{2,1,0:T(8,128)S(1)}, f32[2,512,128]{2,1,0:T(8,128)S(1)}, u32[]{:S(2)}, u32[]{:S(2)}) collective-permute-start(f32[2,512,128]{2,1,0:T(8,128)S(1)} %shard_map.114.refs_4_), channel_id=1, source_target_pairs={{0,2},{2,0},{4,6},{6,4},{8,10},{10,8},{12,14},{14,12},{16,18},{18,... | collective-permute-start | bytes 1572872 | tf_op jit(solution)/shard_map/ppermute | solution.py:270
  22.6 15.1 %collective-permute-start = (f32[264,512]{1,0:T(8,128)S(1)}, f32[264,512]{1,0:T(8,128)S(1)}, u32[]{:S(2)}, u32[]{:S(2)}) collective-permute-start(f32[264,512]{1,0:T(8,128)S(1)} %bitcast.51), channel_id=1, source_target_pairs={{0,1},{1,0},{2,3},{3,2},{4,5},{5,4},{6,7},{7,6},{8,9},{9,8},{10,11... | collective-permute-start | bytes 1622024 | tf_op jit(solution)/shard_map/ppermute | solution.py:285
  24.1 1.7 %copy-start.5 = (bf16[1,128,512]{2,1,0:T(8,128)(2,1)S(1)}, bf16[1,128,512]{2,1,0:T(8,128)(2,1)}, u32[]{:S(2)}) copy-start(bf16[1,128,512]{2,1,0:T(8,128)(2,1)} %refs_4_.1) | copy-start | bytes 393220
  24.2 15.2 %collective-permute-start.9 = (f32[2,2,264,128]{3,2,1,0:T(8,128)S(1)}, f32[2,2,264,128]{3,2,1,0:T(8,128)S(1)}, u32[]{:S(2)}, u32[]{:S(2)}) collective-permute-start(f32[2,2,264,128]{3,2,1,0:T(8,128)S(1)} %shard_map.119), channel_id=1, source_target_pairs={{0,4},{2,6},{4,0},{6,2},{8,12},{10,14},{12,8},{14,10},{16,20},{18,... | collective-permute-start | bytes 1622024 | tf_op jit(solution)/shard_map/ppermute | solution.py:270
  26.1 13.3 %copy-start.2 = (bf16[512,512]{1,0:T(8,128)(2,1)}, bf16[512,512]{1,0:T(8,128)(2,1)S(1)}, u32[]{:S(2)}) copy-start(bf16[512,512]{1,0:T(8,128)(2,1)S(1)} %get-tuple-element.23.refs_3_) | copy-start | bytes 1572868
  26.1 16.0 %collective-permute-start.10 = (f32[264,512]{1,0:T(8,128)S(1)}, f32[264,512]{1,0:T(8,128)S(1)}, u32[]{:S(2)}, u32[]{:S(2)}) collective-permute-start(f32[264,512]{1,0:T(8,128)S(1)} %get-tuple-element.20.refs_2_.refs_1_), channel_id=1, source_target_pairs={{0,8},{2,10},{4,12},{6,14},{8,0},{10,2},{12,4},{14,6},{16,24},{18,... | collective-permute-start | bytes 1622024 | tf_op jit(solution)/shard_map/ppermute | solution.py:270
  27.8 18.7 %collective-permute-start.13 = (f32[3,264,128]{2,1,0:T(8,128)S(1)}, f32[3,264,128]{2,1,0:T(8,128)S(1)}, u32[]{:S(2)}, u32[]{:S(2)}) collective-permute-start(f32[3,264,128]{2,1,0:T(8,128)S(1)} %shard_map.116.refs_2_.refs_6_), channel_id=1, source_target_pairs={{0,1},{1,0},{2,3},{3,2},{4,5},{5,4},{6,7},{7,6},{8,9},{9,8},{10,11... | collective-permute-start | bytes 1216520 | tf_op jit(solution)/shard_map/ppermute | solution.py:285
  29.1 15.1 %collective-permute-start.8 = (f32[2,1,264,128]{3,2,1,0:T(8,128)}, f32[2,1,264,128]{3,2,1,0:T(8,128)}, u32[]{:S(2)}, u32[]{:S(2)}) collective-permute-start(f32[2,1,264,128]{3,2,1,0:T(8,128)} %shard_map.118), channel_id=1, source_target_pairs={{0,4},{2,6},{4,0},{6,2},{8,12},{10,14},{12,8},{14,10},{16,20},{18,... | collective-permute-start | bytes 811016 | tf_op jit(solution)/shard_map/ppermute | solution.py:270
  40.6 2.5 %copy-start = (f32[264,512]{1,0:T(8,128)}, f32[264,512]{1,0:T(8,128)S(1)}, u32[]{:S(2)}) copy-start(f32[264,512]{1,0:T(8,128)S(1)} %get-tuple-element.24.refs_0_.refs_3_) | copy-start | bytes 1622020
  40.6 21.6 %collective-permute-start.11 = (f32[264,512]{1,0:T(8,128)}, f32[264,512]{1,0:T(8,128)}, u32[]{:S(2)}, u32[]{:S(2)}) collective-permute-start(f32[264,512]{1,0:T(8,128)} %get-tuple-element.25.refs_2_), channel_id=1, source_target_pairs={{0,8},{2,10},{4,12},{6,14},{8,0},{10,2},{12,4},{14,6},{16,24},{18,... | collective-permute-start | bytes 1622024 | tf_op jit(solution)/shard_map/ppermute | solution.py:270
  43.0 24.5 %collective-permute-start.12 = (f32[264,512]{1,0:T(8,128)}, f32[264,512]{1,0:T(8,128)}, u32[]{:S(2)}, u32[]{:S(2)}) collective-permute-start(f32[264,512]{1,0:T(8,128)} %shard_map.121.refs_4_), channel_id=1, source_target_pairs={{0,16},{2,18},{4,20},{6,22},{8,24},{10,26},{12,28},{14,30},{16,0},... | collective-permute-start | bytes 1622024 | tf_op jit(solution)/shard_map/ppermute | solution.py:270
  43.8 2.7 %copy-start.1 = (f32[264,512]{1,0:T(8,128)S(1)}, f32[264,512]{1,0:T(8,128)}, u32[]{:S(2)}) copy-start(f32[264,512]{1,0:T(8,128)} %copy-done) | copy-start | bytes 1622020
  44.2 1.0 %copy-start.3 = (bf16[512,512]{1,0:T(8,128)(2,1)S(1)}, bf16[512,512]{1,0:T(8,128)(2,1)}, u32[]{:S(2)}) copy-start(bf16[512,512]{1,0:T(8,128)(2,1)} %copy-done.2) | copy-start | bytes 1572868
  45.2 1.3 %copy-start.11 = (bf16[264,256]{1,0:T(8,128)(2,1)S(1)}, bf16[264,256]{1,0:T(8,128)(2,1)}, u32[]{:S(2)}) copy-start(bf16[264,256]{1,0:T(8,128)(2,1)} %refs_5_.1) | copy-start | bytes 405508
  49.0 20.4 %collective-permute-start.15 = (f32[128,512]{1,0:T(8,128)S(1)}, f32[128,512]{1,0:T(8,128)S(1)}, u32[]{:S(2)}, u32[]{:S(2)}) collective-permute-start(f32[128,512]{1,0:T(8,128)S(1)} %bitcast.57), channel_id=1, source_target_pairs={{0,4},{2,6},{4,0},{6,2},{8,12},{10,14},{12,8},{14,10},{16,20},{18,... | collective-permute-start | bytes 786440 | tf_op jit(solution)/shard_map/ppermute | solution.py:270
  68.8 16.2 %collective-permute-start.14 = (f32[264,512]{1,0:T(8,128)S(1)}, f32[264,512]{1,0:T(8,128)S(1)}, u32[]{:S(2)}, u32[]{:S(2)}) collective-permute-start(f32[264,512]{1,0:T(8,128)S(1)} %shard_map.124.refs_2_), channel_id=1, source_target_pairs={{0,1},{1,0},{2,3},{3,2},{4,5},{5,4},{6,7},{7,6},{8,9},{9,8},{10,11... | collective-permute-start | bytes 1622024 | tf_op jit(solution)/shard_map/ppermute | solution.py:285
  69.5 1.4 %collective-permute-start.16 = (f32[64,512]{1,0:T(8,128)S(1)}, f32[64,512]{1,0:T(8,128)S(1)}, u32[]{:S(2)}, u32[]{:S(2)}) collective-permute-start(f32[64,512]{1,0:T(8,128)S(1)} %get-tuple-element.40), channel_id=1, source_target_pairs={{0,2},{2,0},{4,6},{6,4},{8,10},{10,8},{12,14},{14,12},{16,18},{18,... | collective-permute-start | bytes 393224 | tf_op jit(solution)/shard_map/ppermute | solution.py:270
  70.9 21.2 %copy-start.12 = (f32[1,1,256,512]{3,2,1,0:T(8,128)S(1)}, f32[1,1,256,512]{3,2,1,0:T(8,128)}, u32[]{:S(2)}) copy-start(f32[1,1,256,512]{3,2,1,0:T(8,128)} %param.12) | copy-start | bytes 1572868
  70.9 21.2 %copy-start.13 = (f32[1,1,256,512]{3,2,1,0:T(8,128)S(1)}, f32[1,1,256,512]{3,2,1,0:T(8,128)}, u32[]{:S(2)}) copy-start(f32[1,1,256,512]{3,2,1,0:T(8,128)} %param.11) | copy-start | bytes 1572868
  70.9 5.6 %collective-permute-start.17 = (f32[64,512]{1,0:T(8,128)S(1)}, f32[64,512]{1,0:T(8,128)S(1)}, u32[]{:S(2)}, u32[]{:S(2)}) collective-permute-start(f32[64,512]{1,0:T(8,128)S(1)} %shard_map.126.refs_0_), channel_id=1, source_target_pairs={{0,8},{2,10},{4,12},{6,14},{8,0},{10,2},{12,4},{14,6},{16,24},{18,... | collective-permute-start | bytes 393224 | tf_op jit(solution)/shard_map/ppermute | solution.py:270
  76.5 8.5 %collective-permute-start.18 = (f32[64,512]{1,0:T(8,128)S(1)}, f32[64,512]{1,0:T(8,128)S(1)}, u32[]{:S(2)}, u32[]{:S(2)}) collective-permute-start(f32[64,512]{1,0:T(8,128)S(1)} %shard_map.127.refs_0_), channel_id=1, source_target_pairs={{0,16},{2,18},{4,20},{6,22},{8,24},{10,26},{12,28},{14,30},{16,0},... | collective-permute-start | bytes 393224 | tf_op jit(solution)/shard_map/ppermute | solution.py:270
  85.0 5.4 %collective-permute-start.19 = (f32[64,512]{1,0:T(8,128)S(1)}, f32[64,512]{1,0:T(8,128)S(1)}, u32[]{:S(2)}, u32[]{:S(2)}) collective-permute-start(f32[64,512]{1,0:T(8,128)S(1)} %shard_map.128), channel_id=1, source_target_pairs={{0,4},{2,6},{4,0},{6,2},{8,12},{10,14},{12,8},{14,10},{16,20},{18,... | collective-permute-start | bytes 393224 | tf_op jit(solution)/shard_map/ppermute | solution.py:270
  90.5 1.6 %collective-permute-start.20 = (f32[128,512]{1,0:T(8,128)S(1)}, f32[128,512]{1,0:T(8,128)S(1)}, u32[]{:S(2)}, u32[]{:S(2)}) collective-permute-start(f32[128,512]{1,0:T(8,128)S(1)} %maximum_select_fusion.2), channel_id=1, source_target_pairs={{0,2},{2,0},{4,6},{6,4},{8,10},{10,8},{12,14},{14,12},{16,18},{18,... | collective-permute-start | bytes 786440 | tf_op jit(solution)/shard_map/ppermute | solution.py:270
  92.6 3.6 %collective-permute-start.21 = (f32[1,512]{1,0:T(1,128)S(1)}, f32[1,512]{1,0:T(1,128)S(1)}, u32[]{:S(2)}, u32[]{:S(2)}) collective-permute-start(f32[1,512]{1,0:T(1,128)S(1)} %bitcast.53), channel_id=1, source_target_pairs={{0,1},{1,0},{2,3},{3,2},{4,5},{5,4},{6,7},{7,6},{8,9},{9,8},{10,11... | collective-permute-start | bytes 6152 | tf_op jit(solution)/shard_map/ppermute | solution.py:285
  94.2 2.1 %copy-start.8 = (f32[264,512]{1,0:T(8,128)S(1)}, f32[264,512]{1,0:T(8,128)}, u32[]{:S(2)}) copy-start(f32[264,512]{1,0:T(8,128)} %refs_6_.1) | copy-start | bytes 1622020
  94.2 2.1 %copy-start.9 = (f32[264,512]{1,0:T(8,128)S(1)}, f32[264,512]{1,0:T(8,128)}, u32[]{:S(2)}) copy-start(f32[264,512]{1,0:T(8,128)} %refs_7_.1) | copy-start | bytes 1622020

commit v4 on v3

--- a/solution.py
+++ b/solution.py
@@ -354,12 +354,12 @@
             after=after,
         )
 
-    inner_sum = total(inner_weights[0], to_island(inner_weights[0]), after=[proj_stack])
-    product1, product2 = multiply(1, 2, crossed12, [inner_sum])
+    product1, product2 = multiply(1, 2, crossed12, [proj_stack])
     got1 = to_place(product1, 1)
     sum2 = total(product2, got0, after=[product1])
     got2 = to_place(sum2, 2)
-    (product3,) = multiply(3, 1, crossed3, [sum2])
+    inner_sum = total(inner_weights[0], to_island(inner_weights[0]), after=[sum2])
+    (product3,) = multiply(3, 1, crossed3, [inner_sum])
 
     (partial,) = run(
         lift_kernel,
@@ -380,20 +380,29 @@
         low, high = value[:half], value[half:]
         return jnp.where(bit == 0, low, high), jnp.where(bit == 0, high, low)
 
-    quarters = partial.reshape(2, 2, rank // 4, cols)
-    mine = jnp.where(side == 0, quarters[:, 0], quarters[:, 1]).reshape(rank // 2, cols)
-    theirs = jnp.where(side == 0, quarters[:, 1], quarters[:, 0]).reshape(rank // 2, cols)
-    theirs = to_side(theirs)
+    quarter_rows = rank // 4
+    number = 2 * core + side
+
+    def quarter_of(which):
+        return lax.select_n(
+            which,
+            *(partial[q * quarter_rows : (q + 1) * quarter_rows] for q in range(4)),
+        )
+
+    terms = [
+        quarter_of(number),
+        to_far(quarter_of(number ^ 3)),
+        to_side(quarter_of(number ^ 1)),
+        to_core(quarter_of(number ^ 2)),
+    ]
     grad_rows = total(product3, got1, got2, after=[partial])
-    partial = total(mine, theirs, after=[grad_rows])
-    mine, theirs = halves(partial, core)
-    partial = total(mine, to_core(theirs))
+    partial = total(*terms, after=[got1, got2])
     partial_next = to_place(partial, 1)
     grad_other = to_island(grad_rows)
     partial = total(partial, partial_next)
     partial_next = to_place(partial, 2)
-    partial = total(partial, partial_next, after=[grad_other])
-    partial = double(partial, side, to_side)
+    partial = total(partial, partial_next)
+    partial = total(double(partial, side, to_side), after=[grad_other])
     projected = double(partial, core, to_core)
 
     new_first, new_second, scale = moments_and_scale(

time: 97.7 us -> 94.5 us (0.967)
  waiting for transfers between devices: 56.7 us -> 53.4 us
  local copies, waits for them, and re-layouts: 4.27 us -> 3.22 us
    ppermute x4, waiting for transfers between devices: 8.64 us -> 4.31 us  [to_island(): return lax.ppermute(value, 'island', [(0, 1), (1, 0)])]
    ppermute x18 -> x19, waiting for transfers between devices: 48 us -> 49.1 us  [move(): return lax.ppermute(value, 'fsdp', pairs)]
    unnamed x28 -> x18, local copies, waits for them, and re-layouts: 4.13 us -> 3.08 us
    ppermute x18 -> x19, starting transfers between devices: 19.1 us -> 19.3 us  [move(): return lax.ppermute(value, 'fsdp', pairs)]
  transfers between devices with their start and end apart: 22 -> 23, of which waited for: 13 -> 11; matrix products, arithmetic and copies ran while one was open for 1% -> 2% of each run, Pallas kernels for 10% -> 10%
where the time goes in v4:
time: 94.5 us; the launch traced here: 94.2 us
  waiting for transfers between devices  53.4 us (57%)
  starting transfers between devices  24.1 us (26%)
  Pallas kernels  10.8 us (11%)
  local copies, waits for them, and re-layouts  3.22 us (3%)
  other arithmetic  1.72 us (2%)
    ppermute x19, waiting for transfers between devices, move(): return lax.ppermute(value, 'fsdp', pairs)  49.1 us
    ppermute x19, starting transfers between devices, move(): return lax.ppermute(value, 'fsdp', pairs)  19.3 us
    pallas_call x19, Pallas kernels, run(): pl.pallas_call(body, out_shape=[jax.ShapeDtypeStruct(shape, kind) for sha...  10.8 us
    ppermute x4, starting transfers between devices, to_island(): return lax.ppermute(value, 'island', [(0, 1), (1, 0)])  4.81 us
    ppermute x4, waiting for transfers between devices, to_island(): return lax.ppermute(value, 'island', [(0, 1), (1, 0)])  4.31 us
    unnamed x18, local copies, waits for them, and re-layouts  3.08 us
  transfers between devices with their start and end apart: 23, of which 11 were waited for; matrix products, arithmetic and copies ran while one was open for 2% of the time, Pallas kernels for 10%

profile of v4, /device:TPU:0, one launch (start us, length us, event | category | flops | bytes accessed | tf_op | source)
XLA Modules:
  0.0 94.2 jit_solution(9754024092619140696)
XLA Ops:
  0.7 0.9 copy-done.5
  1.6 4.1 %collective-permute-start.5 = (f32[264,128]{1,0:T(8,128)S(1)}, f32[264,128]{1,0:T(8,128)S(1)}, u32[]{:S(2)}, u32[]{:S(2)}) collective-permute-start(f32[264,128]{1,0:T(8,128)S(1)} %shard_map.112.refs_0_), channel_id=1, source_target_pairs={{0,16},{2,18},{4,20},{6,22},{8,24},{10,26},{12,28},{14,30},{16,0},... | collective-permute-start | bytes 405512 | tf_op jit(solution)/shard_map/ppermute | solution.py:270
  5.7 0.1 stack.27.refs_0_
  5.8 0.9 copy-done
  6.7 1.2 %copy-done.2 = bf16[1,128,4224]{2,1,0:T(8,128)(2,1)S(1)} copy-done((bf16[1,128,4224]{2,1,0:T(8,128)(2,1)S(1)}, bf16[1,128,4224]{2,1,0:T(8,128)(2,1)}, u32[]{:S(2)}) %copy-start.2) | copy-done | bytes 1081368
  7.9 1.1 %shard_map.111 = (f32[776,128]{1,0:T(8,128)S(1)}, f32[264,128]{1,0:T(8,128)S(1)}, f32[3,264,128]{2,1,0:T(8,128)S(1)}, f32[4,264,128]{2,1,0:T(8,128)S(1)}, f32[4,...) custom-call(s32[6]{0:T(128)S(1)} %stack.27.refs_0_, bf16[1,128,4224]{2,1,0:T(8,128)(2,1)S(1)} %copy-done.2, ...), custom_call_target="tpu_custom_call" | custom-call | tf_op jit(solution)/shard_map/pallas_call | solution.py:97
  9.0 1.6 %collective-permute-start.3 = (f32[776,128]{1,0:T(8,128)S(1)}, f32[776,128]{1,0:T(8,128)S(1)}, u32[]{:S(2)}, u32[]{:S(2)}) collective-permute-start(f32[776,128]{1,0:T(8,128)S(1)} %get-tuple-element.20), channel_id=1, source_target_pairs={{0,4},{2,6},{4,0},{6,2},{8,12},{10,14},{12,8},{14,10},{16,20},{18,... | collective-permute-start | bytes 1191944 | tf_op jit(solution)/shard_map/ppermute | solution.py:270
  10.5 1.6 %collective-permute-done.5.refs_1_.refs_0_ = f32[264,128]{1,0:T(8,128)S(1)} collective-permute-done((f32[264,128]{1,0:T(8,128)S(1)}, f32[264,128]{1,0:T(8,128)S(1)}, u32[]{:S(2)}, u32[]{:S(2)}) %collective-permute-start.5) | collective-permute-done | bytes 135200 | tf_op jit(solution)/shard_map/ppermute | solution.py:270
  12.2 0.8 collective-permute-start.6
  13.0 0.8 collective-permute-start.4
  13.8 0.8 collective-permute-start.2
  14.6 7.0 %collective-permute-done.4.refs_2_.refs_3_ = f32[264,128]{1,0:T(8,128)S(1)} collective-permute-done((f32[264,128]{1,0:T(8,128)S(1)}, f32[264,128]{1,0:T(8,128)S(1)}, u32[]{:S(2)}, u32[]{:S(2)}) %collective-permute-start.4) | collective-permute-done | bytes 135200 | tf_op jit(solution)/shard_map/ppermute | solution.py:270
  21.7 0.9 collective-permute-start.8
  22.6 0.8 shard_map.115
  23.5 1.5 %collective-permute-start.7 = (f32[2,2,264,128]{3,2,1,0:T(8,128)}, f32[2,2,264,128]{3,2,1,0:T(8,128)}, u32[]{:S(2)}, u32[]{:S(2)}) collective-permute-start(f32[2,2,264,128]{3,2,1,0:T(8,128)} %shard_map.115), channel_id=1, source_target_pairs={{0,4},{2,6},{4,0},{6,2},{8,12},{10,14},{12,8},{14,10},{16,20},{18,... | collective-permute-start | bytes 1622024 | tf_op jit(solution)/shard_map/ppermute | solution.py:270
  25.0 0.3 shard_map.116
  25.3 1.6 %collective-permute-start.9 = (f32[264,512]{1,0:T(8,128)S(1)}, f32[264,512]{1,0:T(8,128)}, u32[]{:S(2)}, u32[]{:S(2)}) collective-permute-start(f32[264,512]{1,0:T(8,128)S(1)} %get-tuple-element.23.refs_2_.refs_1_), channel_id=1, source_target_pairs={{0,8},{2,10},{4,12},{6,14},{8,0},{10,2},{12,4},{14,6},{16,24},{18,... | collective-permute-start | bytes 1622024 | tf_op jit(solution)/shard_map/ppermute | solution.py:270
  27.0 1.5 %collective-permute-start = (f32[264,512]{1,0:T(8,128)}, f32[264,512]{1,0:T(8,128)}, u32[]{:S(2)}, u32[]{:S(2)}) collective-permute-start(f32[264,512]{1,0:T(8,128)} %bitcast.refs_0_), channel_id=1, source_target_pairs={{0,1},{1,0},{2,3},{3,2},{4,5},{5,4},{6,7},{7,6},{8,9},{9,8},{10,11... | collective-permute-start | bytes 1622024 | tf_op jit(solution)/shard_map/ppermute | solution.py:285
  28.5 0.6 collective-permute-start.13
  29.1 0.7 shard_map.121
  29.8 0.6 collective-permute-start.10
  30.4 8.5 %collective-permute-done.7.refs_2_ = f32[2,2,264,128]{3,2,1,0:T(8,128)} collective-permute-done((f32[2,2,264,128]{3,2,1,0:T(8,128)}, f32[2,2,264,128]{3,2,1,0:T(8,128)}, u32[]{:S(2)}, u32[]{:S(2)}) %collective-permute-start.7) | collective-permute-done | bytes 540704 | tf_op jit(solution)/shard_map/ppermute | solution.py:270
  38.9 1.5 %shard_map.118 = (f32[264,512]{1,0:T(8,128)S(1)}, f32[264,512]{1,0:T(8,128)S(1)}) custom-call(f32[4,264,128]{2,1,0:T(8,128)S(1)} %get-tuple-element.16.refs_0_, f32[4,264,128]{2,1,0:T(8,128)S(1)} %collective-permute-done.1.refs_1_, f32[2,2,264,128]{3,2,1,0:T(8,128)} %collective-permute-done.7.refs_2_, bf16[512,512]{1,0:T(8,128)(2,1)S(1)} %get-tuple-element.22.refs_3_, ...), custom_call_target="tpu_custom_call" | custom-call | tf_op jit(solution)/shard_map/pallas_call | solution.py:97
  40.4 1.6 %collective-permute-start.11 = (f32[264,512]{1,0:T(8,128)S(1)}, f32[264,512]{1,0:T(8,128)S(1)}, u32[]{:S(2)}, u32[]{:S(2)}) collective-permute-start(f32[264,512]{1,0:T(8,128)S(1)} %get-tuple-element.25.refs_2_), channel_id=1, source_target_pairs={{0,8},{2,10},{4,12},{6,14},{8,0},{10,2},{12,4},{14,6},{16,24},{18,... | collective-permute-start | bytes 1622024 | tf_op jit(solution)/shard_map/ppermute | solution.py:270
  42.1 1.1 %shard_map.119.refs_2_ = f32[264,512]{1,0:T(8,128)S(1)} custom-call(f32[264,512]{1,0:T(8,128)S(1)} %get-tuple-element.24.refs_0_.refs_3_, f32[264,512]{1,0:T(8,128)} %collective-permute-done.9.refs_1_, f32[264,512]{1,0:T(8,128)S(1)} %get-tuple-element.25.refs_2_), custom_call_target="tpu_custom_call" | custom-call | tf_op jit(solution)/shard_map/pallas_call | solution.py:97
  43.2 0.8 collective-permute-start.12
  43.9 1.3 %shard_map.120.refs_4_.refs_1_ = f32[264,512]{1,0:T(8,128)S(1)} custom-call(f32[264,512]{1,0:T(8,128)} %bitcast.refs_0_, f32[264,512]{1,0:T(8,128)} %collective-permute-done.refs_1_, f32[264,512]{1,0:T(8,128)S(1)} %shard_map.119.refs_2_), custom_call_target="tpu_custom_call" | custom-call | tf_op jit(solution)/shard_map/pallas_call | solution.py:97
  45.2 1.3 %shard_map.122.refs_4_.refs_0_ = f32[264,512]{1,0:T(8,128)S(1)} custom-call(f32[4,264,128]{2,1,0:T(8,128)S(1)} %get-tuple-element.16.refs_0_, f32[4,264,128]{2,1,0:T(8,128)S(1)} %collective-permute-done.1.refs_1_, f32[2,1,264,128]{3,2,1,0:T(8,128)} %collective-permute-done.10.refs_2_, bf16[512,512]{1,0:T(8,128)(2,1)S(1)} %get-tuple-element.22.refs_3_, ...), custom_call_target="tpu_custom_call" | custom-call | tf_op jit(solution)/shard_map/pallas_call | solution.py:97
  46.5 3.0 %collective-permute-done.13.refs_7_ = f32[3,264,128]{2,1,0:T(8,128)S(1)} collective-permute-done((f32[3,264,128]{2,1,0:T(8,128)S(1)}, f32[3,264,128]{2,1,0:T(8,128)S(1)}, u32[]{:S(2)}, u32[]{:S(2)}) %collective-permute-start.13) | collective-permute-done | bytes 405536 | tf_op jit(solution)/shard_map/ppermute | solution.py:285
  49.5 1.3 %shard_map.123.refs_3_ = f32[256,512]{1,0:T(8,128)S(1)} custom-call(f32[1,512]{1,0:T(1,128)S(1)} %broadcast_in_dim.2.refs_0_, f32[264,512]{1,0:T(8,128)S(1)} %get-tuple-element.23.refs_2_.refs_1_, f32[264,512]{1,0:T(8,128)S(1)} %get-tuple-element.25.refs_2_, f32[264,512]{1,0:T(8,128)S(1)} %get-tuple-element.24.refs_0_.refs_3_, ...), custom_call_target="tpu_custom_call" | custom-call | tf_op jit(solution)/shard_map/pallas_call | solution.py:97
  50.9 0.1 collective-permute-start.15
  51.0 1.2 %collective-permute-start.16 = (f32[64,512]{1,0:T(8,128)S(1)}, f32[64,512]{1,0:T(8,128)S(1)}, u32[]{:S(2)}, u32[]{:S(2)}) collective-permute-start(f32[64,512]{1,0:T(8,128)S(1)} %get-tuple-element.34), channel_id=1, source_target_pairs={{0,4},{2,6},{4,0},{6,2},{8,12},{10,14},{12,8},{14,10},{16,20},{18,... | collective-permute-start | bytes 393224 | tf_op jit(solution)/shard_map/ppermute | solution.py:270
  52.3 0.6 collective-permute-start.17
  52.9 9.3 %collective-permute-done.11.refs_1_.refs_4_ = f32[264,512]{1,0:T(8,128)S(1)} collective-permute-done((f32[264,512]{1,0:T(8,128)S(1)}, f32[264,512]{1,0:T(8,128)S(1)}, u32[]{:S(2)}, u32[]{:S(2)}) %collective-permute-start.11) | collective-permute-done | bytes 540704 | tf_op jit(solution)/shard_map/ppermute | solution.py:270
  62.2 5.8 %collective-permute-done.12.refs_2_.refs_5_ = f32[264,512]{1,0:T(8,128)S(1)} collective-permute-done((f32[264,512]{1,0:T(8,128)S(1)}, f32[264,512]{1,0:T(8,128)S(1)}, u32[]{:S(2)}, u32[]{:S(2)}) %collective-permute-start.12) | collective-permute-done | bytes 540704 | tf_op jit(solution)/shard_map/ppermute | solution.py:270
  68.0 0.1 shard_map.124.refs_2_
  68.1 1.6 %collective-permute-start.14 = (f32[264,512]{1,0:T(8,128)S(1)}, f32[264,512]{1,0:T(8,128)S(1)}, u32[]{:S(2)}, u32[]{:S(2)}) collective-permute-start(f32[264,512]{1,0:T(8,128)S(1)} %shard_map.124.refs_2_), channel_id=1, source_target_pairs={{0,1},{1,0},{2,3},{3,2},{4,5},{5,4},{6,7},{7,6},{8,9},{9,8},{10,11... | collective-permute-start | bytes 1622024 | tf_op jit(solution)/shard_map/ppermute | solution.py:285
  69.8 6.0 %collective-permute-done.18.refs_1_ = f32[64,512]{1,0:T(8,128)S(1)} collective-permute-done((f32[64,512]{1,0:T(8,128)S(1)}, f32[64,512]{1,0:T(8,128)S(1)}, u32[]{:S(2)}, u32[]{:S(2)}) %collective-permute-start.18) | collective-permute-done | bytes 131104 | tf_op jit(solution)/shard_map/ppermute | solution.py:270
  75.8 0.5 collective-permute-start.19
  76.3 5.9 %collective-permute-done.19.refs_1_ = f32[64,512]{1,0:T(8,128)S(1)} collective-permute-done((f32[64,512]{1,0:T(8,128)S(1)}, f32[64,512]{1,0:T(8,128)S(1)}, u32[]{:S(2)}, u32[]{:S(2)}) %collective-permute-start.19) | collective-permute-done | bytes 131104 | tf_op jit(solution)/shard_map/ppermute | solution.py:270
  82.2 1.6 %collective-permute-start.20 = (f32[64,512]{1,0:T(8,128)S(1)}, f32[64,512]{1,0:T(8,128)S(1)}, u32[]{:S(2)}, u32[]{:S(2)}) collective-permute-start(f32[64,512]{1,0:T(8,128)S(1)} %shard_map.127), channel_id=1, source_target_pairs={{0,4},{2,6},{4,0},{6,2},{8,12},{10,14},{12,8},{14,10},{16,20},{18,... | collective-permute-start | bytes 393224 | tf_op jit(solution)/shard_map/ppermute | solution.py:270
  83.8 3.5 %collective-permute-done.20 = f32[64,512]{1,0:T(8,128)S(1)} collective-permute-done((f32[64,512]{1,0:T(8,128)S(1)}, f32[64,512]{1,0:T(8,128)S(1)}, u32[]{:S(2)}, u32[]{:S(2)}) %collective-permute-start.20) | collective-permute-done | bytes 131104 | tf_op jit(solution)/shard_map/ppermute | solution.py:270
  87.4 1.5 %collective-permute-done.21 = f32[128,512]{1,0:T(8,128)S(1)} collective-permute-done((f32[128,512]{1,0:T(8,128)S(1)}, f32[128,512]{1,0:T(8,128)S(1)}, u32[]{:S(2)}, u32[]{:S(2)}) %collective-permute-start.21) | collective-permute-done | bytes 262176 | tf_op jit(solution)/shard_map/ppermute | solution.py:270
  88.9 0.4 fusion.8
  89.4 1.1 %collective-permute-start.22 = (f32[1,512]{1,0:T(1,128)S(1)}, f32[1,512]{1,0:T(1,128)S(1)}, u32[]{:S(2)}, u32[]{:S(2)}) collective-permute-start(f32[1,512]{1,0:T(1,128)S(1)} %bitcast.35), channel_id=1, source_target_pairs={{0,1},{1,0},{2,3},{3,2},{4,5},{5,4},{6,7},{7,6},{8,9},{9,8},{10,11... | collective-permute-start | bytes 6152 | tf_op jit(solution)/shard_map/ppermute | solution.py:285
  90.5 1.2 %fusion.6 = (f32[1,1,256,512]{3,2,1,0:T(8,128)}, f32[1,1,256,512]{3,2,1,0:T(8,128)}) fusion(f32[1,1,256,512]{3,2,1,0:T(8,128)S(1)} %copy-done.7, f32[1,1,128,512]{3,2,1,0:T(8,128)S(1)} %bitcast.34, f32[1,1,128,512]{3,2,1,0:T(8,128)S(1)} %bitcast.37, pred[]{:T(512)S(6)} %eq.9, f32[1,1,256,512]{3,2,1,0:T(8,128)S(1)} %copy-done.8), kind=kLoop, calls=%fused_computation.8 | loop fusion | flops 1310720 | bytes 2621441 | tf_op jit(solution)/shard_map/add | solution.py:31
  91.7 1.3 %collective-permute-done.22.refs_5_ = f32[1,512]{1,0:T(1,128)S(1)} collective-permute-done((f32[1,512]{1,0:T(1,128)S(1)}, f32[1,512]{1,0:T(1,128)S(1)}, u32[]{:S(2)}, u32[]{:S(2)}) %collective-permute-start.22) | collective-permute-done | bytes 2080 | tf_op jit(solution)/shard_map/ppermute | solution.py:285
  93.0 1.1 %shard_map.129 = (bf16[264,256]{1,0:T(8,128)(2,1)}, f32[264,512]{1,0:T(8,128)}) custom-call(f32[1,512]{1,0:T(1,128)S(1)} %broadcast_in_dim.2.refs_0_, f32[264,512]{1,0:T(8,128)S(1)} %shard_map.120.refs_4_.refs_1_, f32[264,512]{1,0:T(8,128)S(1)} %shard_map.124.refs_2_, f32[264,512]{1,0:T(8,128)S(1)} %collective-permute-done.14.refs_1_.refs_3_, ...), custom_call_target="tpu_custom_call" | custom-call | tf_op jit(solution)/shard_map/pallas_call | solution.py:97
  (45 shorter events, 0.6 us)
Async XLA Ops:
  0.6 0.9 copy-start.5
  1.6 10.6 %collective-permute-start.5 = (f32[264,128]{1,0:T(8,128)S(1)}, f32[264,128]{1,0:T(8,128)S(1)}, u32[]{:S(2)}, u32[]{:S(2)}) collective-permute-start(f32[264,128]{1,0:T(8,128)S(1)} %shard_map.112.refs_0_), channel_id=1, source_target_pairs={{0,16},{2,18},{4,20},{6,22},{8,24},{10,26},{12,28},{14,30},{16,0},... | collective-permute-start | bytes 405512 | tf_op jit(solution)/shard_map/ppermute | solution.py:270
  5.8 0.9 copy-start
  6.7 1.2 %copy-start.2 = (bf16[1,128,4224]{2,1,0:T(8,128)(2,1)S(1)}, bf16[1,128,4224]{2,1,0:T(8,128)(2,1)}, u32[]{:S(2)}) copy-start(bf16[1,128,4224]{2,1,0:T(8,128)(2,1)} %refs_1_.2) | copy-start | bytes 3244036
  9.0 12.6 %collective-permute-start.3 = (f32[776,128]{1,0:T(8,128)S(1)}, f32[776,128]{1,0:T(8,128)S(1)}, u32[]{:S(2)}, u32[]{:S(2)}) collective-permute-start(f32[776,128]{1,0:T(8,128)S(1)} %get-tuple-element.20), channel_id=1, source_target_pairs={{0,4},{2,6},{4,0},{6,2},{8,12},{10,14},{12,8},{14,10},{16,20},{18,... | collective-permute-start | bytes 1191944 | tf_op jit(solution)/shard_map/ppermute | solution.py:270
  12.2 9.4 %collective-permute-start.6 = (f32[2,264,128]{2,1,0:T(8,128)S(1)}, f32[2,264,128]{2,1,0:T(8,128)S(1)}, u32[]{:S(2)}, u32[]{:S(2)}) collective-permute-start(f32[2,264,128]{2,1,0:T(8,128)S(1)} %shard_map.113), channel_id=1, source_target_pairs={{0,8},{2,10},{4,12},{6,14},{8,0},{10,2},{12,4},{14,6},{16,24},{18,... | collective-permute-start | bytes 811016 | tf_op jit(solution)/shard_map/ppermute | solution.py:270
  13.0 8.6 %collective-permute-start.4 = (f32[264,128]{1,0:T(8,128)S(1)}, f32[264,128]{1,0:T(8,128)S(1)}, u32[]{:S(2)}, u32[]{:S(2)}) collective-permute-start(f32[264,128]{1,0:T(8,128)S(1)} %get-tuple-element.21), channel_id=1, source_target_pairs={{0,6},{2,4},{4,2},{6,0},{8,14},{10,12},{12,10},{14,8},{16,22},{18,... | collective-permute-start | bytes 405512 | tf_op jit(solution)/shard_map/ppermute | solution.py:270
  13.8 8.8 %collective-permute-start.2 = (f32[3,264,128]{2,1,0:T(8,128)S(1)}, f32[3,264,128]{2,1,0:T(8,128)S(1)}, u32[]{:S(2)}, u32[]{:S(2)}) collective-permute-start(f32[3,264,128]{2,1,0:T(8,128)S(1)} %get-tuple-element.19), channel_id=1, source_target_pairs={{0,2},{2,0},{4,6},{6,4},{8,10},{10,8},{12,14},{14,12},{16,18},{18,... | collective-permute-start | bytes 1216520 | tf_op jit(solution)/shard_map/ppermute | solution.py:270
  14.6 10.4 %collective-permute-start.1 = (f32[4,264,128]{2,1,0:T(8,128)S(1)}, f32[4,264,128]{2,1,0:T(8,128)S(1)}, u32[]{:S(2)}, u32[]{:S(2)}) collective-permute-start(f32[4,264,128]{2,1,0:T(8,128)S(1)} %get-tuple-element.17), channel_id=1, source_target_pairs={{0,2},{2,0},{4,6},{6,4},{8,10},{10,8},{12,14},{14,12},{16,18},{18,... | collective-permute-start | bytes 1622024 | tf_op jit(solution)/shard_map/ppermute | solution.py:270
  21.7 3.3 %collective-permute-start.8 = (f32[2,512,128]{2,1,0:T(8,128)S(1)}, f32[2,512,128]{2,1,0:T(8,128)S(1)}, u32[]{:S(2)}, u32[]{:S(2)}) collective-permute-start(f32[2,512,128]{2,1,0:T(8,128)S(1)} %shard_map.114.refs_4_), channel_id=1, source_target_pairs={{0,2},{2,0},{4,6},{6,4},{8,10},{10,8},{12,14},{14,12},{16,18},{18,... | collective-permute-start | bytes 1572872 | tf_op jit(solution)/shard_map/ppermute | solution.py:270
  22.6 2.4 %copy-start.1 = (bf16[1,128,512]{2,1,0:T(8,128)(2,1)S(1)}, bf16[1,128,512]{2,1,0:T(8,128)(2,1)}, u32[]{:S(2)}) copy-start(bf16[1,128,512]{2,1,0:T(8,128)(2,1)} %refs_4_.1) | copy-start | bytes 393220
  23.5 15.5 %collective-permute-start.7 = (f32[2,2,264,128]{3,2,1,0:T(8,128)}, f32[2,2,264,128]{3,2,1,0:T(8,128)}, u32[]{:S(2)}, u32[]{:S(2)}) collective-permute-start(f32[2,2,264,128]{3,2,1,0:T(8,128)} %shard_map.115), channel_id=1, source_target_pairs={{0,4},{2,6},{4,0},{6,2},{8,12},{10,14},{12,8},{14,10},{16,20},{18,... | collective-permute-start | bytes 1622024 | tf_op jit(solution)/shard_map/ppermute | solution.py:270
  25.3 16.8 %collective-permute-start.9 = (f32[264,512]{1,0:T(8,128)S(1)}, f32[264,512]{1,0:T(8,128)}, u32[]{:S(2)}, u32[]{:S(2)}) collective-permute-start(f32[264,512]{1,0:T(8,128)S(1)} %get-tuple-element.23.refs_2_.refs_1_), channel_id=1, source_target_pairs={{0,8},{2,10},{4,12},{6,14},{8,0},{10,2},{12,4},{14,6},{16,24},{18,... | collective-permute-start | bytes 1622024 | tf_op jit(solution)/shard_map/ppermute | solution.py:270
  27.0 17.0 %collective-permute-start = (f32[264,512]{1,0:T(8,128)}, f32[264,512]{1,0:T(8,128)}, u32[]{:S(2)}, u32[]{:S(2)}) collective-permute-start(f32[264,512]{1,0:T(8,128)} %bitcast.refs_0_), channel_id=1, source_target_pairs={{0,1},{1,0},{2,3},{3,2},{4,5},{5,4},{6,7},{7,6},{8,9},{9,8},{10,11... | collective-permute-start | bytes 1622024 | tf_op jit(solution)/shard_map/ppermute | solution.py:285
  28.5 21.0 %collective-permute-start.13 = (f32[3,264,128]{2,1,0:T(8,128)S(1)}, f32[3,264,128]{2,1,0:T(8,128)S(1)}, u32[]{:S(2)}, u32[]{:S(2)}) collective-permute-start(f32[3,264,128]{2,1,0:T(8,128)S(1)} %shard_map.117.refs_4_.refs_6_), channel_id=1, source_target_pairs={{0,1},{1,0},{2,3},{3,2},{4,5},{5,4},{6,7},{7,6},{8,9},{9,8},{10,11... | collective-permute-start | bytes 1216520 | tf_op jit(solution)/shard_map/ppermute | solution.py:285
  29.8 15.4 %collective-permute-start.10 = (f32[2,1,264,128]{3,2,1,0:T(8,128)}, f32[2,1,264,128]{3,2,1,0:T(8,128)}, u32[]{:S(2)}, u32[]{:S(2)}) collective-permute-start(f32[2,1,264,128]{3,2,1,0:T(8,128)} %shard_map.121), channel_id=1, source_target_pairs={{0,4},{2,6},{4,0},{6,2},{8,12},{10,14},{12,8},{14,10},{16,20},{18,... | collective-permute-start | bytes 811016 | tf_op jit(solution)/shard_map/ppermute | solution.py:270
  40.4 21.8 %collective-permute-start.11 = (f32[264,512]{1,0:T(8,128)S(1)}, f32[264,512]{1,0:T(8,128)S(1)}, u32[]{:S(2)}, u32[]{:S(2)}) collective-permute-start(f32[264,512]{1,0:T(8,128)S(1)} %get-tuple-element.25.refs_2_), channel_id=1, source_target_pairs={{0,8},{2,10},{4,12},{6,14},{8,0},{10,2},{12,4},{14,6},{16,24},{18,... | collective-permute-start | bytes 1622024 | tf_op jit(solution)/shard_map/ppermute | solution.py:270
  43.2 24.8 %collective-permute-start.12 = (f32[264,512]{1,0:T(8,128)S(1)}, f32[264,512]{1,0:T(8,128)S(1)}, u32[]{:S(2)}, u32[]{:S(2)}) collective-permute-start(f32[264,512]{1,0:T(8,128)S(1)} %shard_map.119.refs_2_), channel_id=1, source_target_pairs={{0,16},{2,18},{4,20},{6,22},{8,24},{10,26},{12,28},{14,30},{16,0},... | collective-permute-start | bytes 1622024 | tf_op jit(solution)/shard_map/ppermute | solution.py:270
  45.2 4.3 %copy-start.6 = (bf16[264,256]{1,0:T(8,128)(2,1)S(1)}, bf16[264,256]{1,0:T(8,128)(2,1)}, u32[]{:S(2)}) copy-start(bf16[264,256]{1,0:T(8,128)(2,1)} %refs_5_.1) | copy-start | bytes 405508
  50.9 18.8 %collective-permute-start.15 = (f32[64,512]{1,0:T(8,128)S(1)}, f32[64,512]{1,0:T(8,128)S(1)}, u32[]{:S(2)}, u32[]{:S(2)}) collective-permute-start(f32[64,512]{1,0:T(8,128)S(1)} %get-tuple-element.35), channel_id=1, source_target_pairs={{0,6},{2,4},{4,2},{6,0},{8,14},{10,12},{12,10},{14,8},{16,22},{18,... | collective-permute-start | bytes 393224 | tf_op jit(solution)/shard_map/ppermute | solution.py:270
  51.0 18.7 %collective-permute-start.16 = (f32[64,512]{1,0:T(8,128)S(1)}, f32[64,512]{1,0:T(8,128)S(1)}, u32[]{:S(2)}, u32[]{:S(2)}) collective-permute-start(f32[64,512]{1,0:T(8,128)S(1)} %get-tuple-element.34), channel_id=1, source_target_pairs={{0,4},{2,6},{4,0},{6,2},{8,12},{10,14},{12,8},{14,10},{16,20},{18,... | collective-permute-start | bytes 393224 | tf_op jit(solution)/shard_map/ppermute | solution.py:270
  52.3 17.4 %collective-permute-start.17 = (f32[64,512]{1,0:T(8,128)S(1)}, f32[64,512]{1,0:T(8,128)S(1)}, u32[]{:S(2)}, u32[]{:S(2)}) collective-permute-start(f32[64,512]{1,0:T(8,128)S(1)} %get-tuple-element.32), channel_id=1, source_target_pairs={{0,2},{2,0},{4,6},{6,4},{8,10},{10,8},{12,14},{14,12},{16,18},{18,... | collective-permute-start | bytes 393224 | tf_op jit(solution)/shard_map/ppermute | solution.py:270
  68.1 19.2 %collective-permute-start.14 = (f32[264,512]{1,0:T(8,128)S(1)}, f32[264,512]{1,0:T(8,128)S(1)}, u32[]{:S(2)}, u32[]{:S(2)}) collective-permute-start(f32[264,512]{1,0:T(8,128)S(1)} %shard_map.124.refs_2_), channel_id=1, source_target_pairs={{0,1},{1,0},{2,3},{3,2},{4,5},{5,4},{6,7},{7,6},{8,9},{9,8},{10,11... | collective-permute-start | bytes 1622024 | tf_op jit(solution)/shard_map/ppermute | solution.py:285
  69.7 6.1 %collective-permute-start.18 = (f32[64,512]{1,0:T(8,128)S(1)}, f32[64,512]{1,0:T(8,128)S(1)}, u32[]{:S(2)}, u32[]{:S(2)}) collective-permute-start(f32[64,512]{1,0:T(8,128)S(1)} %shard_map.125.refs_0_), channel_id=1, source_target_pairs={{0,8},{2,10},{4,12},{6,14},{8,0},{10,2},{12,4},{14,6},{16,24},{18,... | collective-permute-start | bytes 393224 | tf_op jit(solution)/shard_map/ppermute | solution.py:270
  75.8 13.1 %copy-start.7 = (f32[1,1,256,512]{3,2,1,0:T(8,128)S(1)}, f32[1,1,256,512]{3,2,1,0:T(8,128)}, u32[]{:S(2)}) copy-start(f32[1,1,256,512]{3,2,1,0:T(8,128)} %param.12) | copy-start | bytes 1572868
  75.8 13.1 %copy-start.8 = (f32[1,1,256,512]{3,2,1,0:T(8,128)S(1)}, f32[1,1,256,512]{3,2,1,0:T(8,128)}, u32[]{:S(2)}) copy-start(f32[1,1,256,512]{3,2,1,0:T(8,128)} %param.11) | copy-start | bytes 1572868
  75.8 6.3 %collective-permute-start.19 = (f32[64,512]{1,0:T(8,128)S(1)}, f32[64,512]{1,0:T(8,128)S(1)}, u32[]{:S(2)}, u32[]{:S(2)}) collective-permute-start(f32[64,512]{1,0:T(8,128)S(1)} %shard_map.126.refs_0_), channel_id=1, source_target_pairs={{0,16},{2,18},{4,20},{6,22},{8,24},{10,26},{12,28},{14,30},{16,0},... | collective-permute-start | bytes 393224 | tf_op jit(solution)/shard_map/ppermute | solution.py:270
  82.2 5.0 %collective-permute-start.20 = (f32[64,512]{1,0:T(8,128)S(1)}, f32[64,512]{1,0:T(8,128)S(1)}, u32[]{:S(2)}, u32[]{:S(2)}) collective-permute-start(f32[64,512]{1,0:T(8,128)S(1)} %shard_map.127), channel_id=1, source_target_pairs={{0,4},{2,6},{4,0},{6,2},{8,12},{10,14},{12,8},{14,10},{16,20},{18,... | collective-permute-start | bytes 393224 | tf_op jit(solution)/shard_map/ppermute | solution.py:270
  87.3 1.6 %collective-permute-start.21 = (f32[128,512]{1,0:T(8,128)S(1)}, f32[128,512]{1,0:T(8,128)S(1)}, u32[]{:S(2)}, u32[]{:S(2)}) collective-permute-start(f32[128,512]{1,0:T(8,128)S(1)} %shard_map.128), channel_id=1, source_target_pairs={{0,2},{2,0},{4,6},{6,4},{8,10},{10,8},{12,14},{14,12},{16,18},{18,... | collective-permute-start | bytes 786440 | tf_op jit(solution)/shard_map/ppermute | solution.py:270
  89.4 3.6 %collective-permute-start.22 = (f32[1,512]{1,0:T(1,128)S(1)}, f32[1,512]{1,0:T(1,128)S(1)}, u32[]{:S(2)}, u32[]{:S(2)}) collective-permute-start(f32[1,512]{1,0:T(1,128)S(1)} %bitcast.35), channel_id=1, source_target_pairs={{0,1},{1,0},{2,3},{3,2},{4,5},{5,4},{6,7},{7,6},{8,9},{9,8},{10,11... | collective-permute-start | bytes 6152 | tf_op jit(solution)/shard_map/ppermute | solution.py:285
  90.5 2.5 %copy-start.3 = (f32[264,512]{1,0:T(8,128)S(1)}, f32[264,512]{1,0:T(8,128)}, u32[]{:S(2)}) copy-start(f32[264,512]{1,0:T(8,128)} %refs_6_.1) | copy-start | bytes 1622020
  90.5 2.5 %copy-start.4 = (f32[264,512]{1,0:T(8,128)S(1)}, f32[264,512]{1,0:T(8,128)}, u32[]{:S(2)}) copy-start(f32[264,512]{1,0:T(8,128)} %refs_7_.1) | copy-start | bytes 1622020

commit v5 on v4

--- a/solution.py
+++ b/solution.py
@@ -186,11 +186,20 @@
     out[...] = jnp.dot(a, grads[...], preferred_element_type=F32)
 
 
-def product_kernel(k, here, core_a, crossed, grads, *outs):
-    for i, out in enumerate(outs):
-        pieces = (here[k + i], core_a[k + i], crossed[0, i], crossed[1, i])
-        a = jnp.concatenate([piece.astype(BF16) for piece in pieces], axis=1)
-        out[...] = jnp.dot(a, grads[...], preferred_element_type=F32)
+def later_product(k, i, here, core_a, crossed, grads):
+    pieces = (here[k], core_a[k], crossed[0, i], crossed[1, i])
+    a = jnp.concatenate([piece.astype(BF16) for piece in pieces], axis=1)
+    return jnp.dot(a, grads[...], preferred_element_type=F32)
+
+
+def product_kernel(k, i, here, core_a, crossed, grads, out):
+    out[...] = later_product(k, i, here, core_a, crossed, grads)
+
+
+def product_and_sum_kernel(here, core_a, crossed, grads, got, out, out_sum):
+    product = later_product(2, 1, here, core_a, crossed, grads)
+    out[...] = product
+    out_sum[...] = product + got[...]
 
 
 def sum_kernel(*refs):
@@ -346,20 +355,28 @@
     )
     proj_others = to_island(proj_stack)
 
-    def multiply(k, count, crossed, after):
-        return run(
-            functools.partial(product_kernel, k),
-            [((rows, cols), F32)] * count,
-            [here, from_core, crossed, grads],
-            after=after,
-        )
-
-    product1, product2 = multiply(1, 2, crossed12, [proj_stack])
+    row_block = ((rows, cols), F32)
+    (product1,) = run(
+        functools.partial(product_kernel, 1, 0),
+        [row_block],
+        [here, from_core, crossed12, grads],
+        after=[proj_stack],
+    )
     got1 = to_place(product1, 1)
-    sum2 = total(product2, got0, after=[product1])
+    product2, sum2 = run(
+        product_and_sum_kernel,
+        [row_block, row_block],
+        [here, from_core, crossed12, grads, got0],
+        after=[product1],
+    )
     got2 = to_place(sum2, 2)
     inner_sum = total(inner_weights[0], to_island(inner_weights[0]), after=[sum2])
-    (product3,) = multiply(3, 1, crossed3, [inner_sum])
+    (product3,) = run(
+        functools.partial(product_kernel, 3, 0),
+        [row_block],
+        [here, from_core, crossed3, grads],
+        after=[inner_sum],
+    )
 
     (partial,) = run(
         lift_kernel,
@@ -395,15 +412,16 @@
         to_side(quarter_of(number ^ 1)),
         to_core(quarter_of(number ^ 2)),
     ]
+    partial = total(*terms)
+    partial_next = to_place(partial, 1)
     grad_rows = total(product3, got1, got2, after=[partial])
-    partial = total(*terms, after=[got1, got2])
-    partial_next = to_place(partial, 1)
     grad_other = to_island(grad_rows)
-    partial = total(partial, partial_next)
+    partial = total(partial, partial_next, after=[got1, got2])
     partial_next = to_place(partial, 2)
     partial = total(partial, partial_next)
-    partial = total(double(partial, side, to_side), after=[grad_other])
-    projected = double(partial, core, to_core)
+    partial = double(partial, side, to_side)
+    token = to_core(grad_other[: rank // 4])
+    projected = total(double(partial, core, to_core), after=[token])
 
     new_first, new_second, scale = moments_and_scale(
         projected, first_moment[0, 0], second_moment[0, 0]

time: 94.5 us -> 88.3 us (0.934)
  waiting for transfers between devices: 53.4 us -> 47.8 us
    ppermute x19 -> x20, waiting for transfers between devices: 49.1 us -> 41 us  [move(): return lax.ppermute(value, 'fsdp', pairs)]
    ppermute x4, waiting for transfers between devices: 4.31 us -> 6.75 us  [to_island(): return lax.ppermute(value, 'island', [(0, 1), (1, 0)])]
    add x1 -> x0, other arithmetic: 1.17 us -> none  [moments_and_scale(): second_decay * second + (1.0 - second_decay) * projected * projected]
    pallas_call x19, Pallas kernels: 10.8 us -> 9.87 us  [run(): pl.pallas_call(body, out_shape=[jax.ShapeDtypeStruct(shape, kind) for sha...]
    ppermute x19 -> x20, starting transfers between devices: 19.3 us -> 19.4 us  [move(): return lax.ppermute(value, 'fsdp', pairs)]
  transfers between devices with their start and end apart: 23 -> 24, of which waited for: 11 -> 14; matrix products, arithmetic and copies ran while one was open for 2% -> 0% of each run, Pallas kernels for 10% -> 10%
where the time goes in v5:
time: 88.3 us; the launch traced here: 88 us
  waiting for transfers between devices  47.8 us (54%)
  starting transfers between devices  24.7 us (28%)
  Pallas kernels  9.87 us (11%)
  local copies, waits for them, and re-layouts  3.23 us (4%)
  other arithmetic  1.51 us (2%)
  between operations  0.91 us (1%)
    ppermute x20, waiting for transfers between devices, move(): return lax.ppermute(value, 'fsdp', pairs)  41 us
    ppermute x20, starting transfers between devices, move(): return lax.ppermute(value, 'fsdp', pairs)  19.4 us
    pallas_call x19, Pallas kernels, run(): pl.pallas_call(body, out_shape=[jax.ShapeDtypeStruct(shape, kind) for sha...  9.87 us
    ppermute x4, waiting for transfers between devices, to_island(): return lax.ppermute(value, 'island', [(0, 1), (1, 0)])  6.75 us
    ppermute x4, starting transfers between devices, to_island(): return lax.ppermute(value, 'island', [(0, 1), (1, 0)])  5.26 us
    unnamed x18, local copies, waits for them, and re-layouts  3.08 us
  transfers between devices with their start and end apart: 24, of which 14 were waited for; matrix products, arithmetic and copies ran while one was open for 0% of the time, Pallas kernels for 10%

profile of v5, /device:TPU:0, one launch (start us, length us, event | category | flops | bytes accessed | tf_op | source)
XLA Modules:
  0.0 88.0 jit_solution(9563354989323428690)
XLA Ops:
  0.7 0.9 %copy-done.5 = bf16[264,256]{1,0:T(8,128)(2,1)S(1)} copy-done((bf16[264,256]{1,0:T(8,128)(2,1)S(1)}, bf16[264,256]{1,0:T(8,128)(2,1)}, u32[]{:S(2)}) %copy-start.5) | copy-done | bytes 135192
  1.6 4.1 %collective-permute-start.5 = (f32[264,128]{1,0:T(8,128)S(1)}, f32[264,128]{1,0:T(8,128)S(1)}, u32[]{:S(2)}, u32[]{:S(2)}) collective-permute-start(f32[264,128]{1,0:T(8,128)S(1)} %shard_map.112.refs_0_), channel_id=1, source_target_pairs={{0,16},{2,18},{4,20},{6,22},{8,24},{10,26},{12,28},{14,30},{16,0},... | collective-permute-start | bytes 405512 | tf_op jit(solution)/shard_map/ppermute | solution.py:279
  5.8 0.9 %copy-done = bf16[1,128,512]{2,1,0:T(8,128)(2,1)S(1)} copy-done((bf16[1,128,512]{2,1,0:T(8,128)(2,1)S(1)}, bf16[1,128,512]{2,1,0:T(8,128)(2,1)}, u32[]{:S(2)}) %copy-start) | copy-done | bytes 131096
  6.7 1.2 %copy-done.2 = bf16[1,128,4224]{2,1,0:T(8,128)(2,1)S(1)} copy-done((bf16[1,128,4224]{2,1,0:T(8,128)(2,1)S(1)}, bf16[1,128,4224]{2,1,0:T(8,128)(2,1)}, u32[]{:S(2)}) %copy-start.2) | copy-done | bytes 1081368
  7.9 1.1 %shard_map.111 = (f32[776,128]{1,0:T(8,128)S(1)}, f32[264,128]{1,0:T(8,128)S(1)}, f32[3,264,128]{2,1,0:T(8,128)S(1)}, f32[4,264,128]{2,1,0:T(8,128)S(1)}, f32[4,...) custom-call(s32[6]{0:T(128)S(1)} %stack.27.refs_0_, bf16[1,128,4224]{2,1,0:T(8,128)(2,1)S(1)} %copy-done.2, ...), custom_call_target="tpu_custom_call" | custom-call | tf_op jit(solution)/shard_map/pallas_call | solution.py:97
  9.0 1.6 %collective-permute-start.3 = (f32[776,128]{1,0:T(8,128)S(1)}, f32[776,128]{1,0:T(8,128)S(1)}, u32[]{:S(2)}, u32[]{:S(2)}) collective-permute-start(f32[776,128]{1,0:T(8,128)S(1)} %get-tuple-element.20), channel_id=1, source_target_pairs={{0,4},{2,6},{4,0},{6,2},{8,12},{10,14},{12,8},{14,10},{16,20},{18,... | collective-permute-start | bytes 1191944 | tf_op jit(solution)/shard_map/ppermute | solution.py:279
  10.5 1.6 %collective-permute-done.5.refs_1_.refs_0_ = f32[264,128]{1,0:T(8,128)S(1)} collective-permute-done((f32[264,128]{1,0:T(8,128)S(1)}, f32[264,128]{1,0:T(8,128)S(1)}, u32[]{:S(2)}, u32[]{:S(2)}) %collective-permute-start.5) | collective-permute-done | bytes 135200 | tf_op jit(solution)/shard_map/ppermute | solution.py:279
  12.2 0.8 collective-permute-start.6
  13.0 0.8 collective-permute-start.4
  13.8 0.8 collective-permute-start.2
  14.6 7.0 %collective-permute-done.4.refs_2_.refs_3_ = f32[264,128]{1,0:T(8,128)S(1)} collective-permute-done((f32[264,128]{1,0:T(8,128)S(1)}, f32[264,128]{1,0:T(8,128)S(1)}, u32[]{:S(2)}, u32[]{:S(2)}) %collective-permute-start.4) | collective-permute-done | bytes 135200 | tf_op jit(solution)/shard_map/ppermute | solution.py:279
  21.7 0.9 collective-permute-start.8
  22.6 0.8 shard_map.115
  23.5 1.5 %collective-permute-start.7 = (f32[2,2,264,128]{3,2,1,0:T(8,128)}, f32[2,2,264,128]{3,2,1,0:T(8,128)S(1)}, u32[]{:S(2)}, u32[]{:S(2)}) collective-permute-start(f32[2,2,264,128]{3,2,1,0:T(8,128)} %shard_map.115), channel_id=1, source_target_pairs={{0,4},{2,6},{4,0},{6,2},{8,12},{10,14},{12,8},{14,10},{16,20},{18,... | collective-permute-start | bytes 1622024 | tf_op jit(solution)/shard_map/ppermute | solution.py:279
  25.0 0.3 shard_map.116
  25.3 1.6 %collective-permute-start.9 = (f32[264,512]{1,0:T(8,128)S(1)}, f32[264,512]{1,0:T(8,128)}, u32[]{:S(2)}, u32[]{:S(2)}) collective-permute-start(f32[264,512]{1,0:T(8,128)S(1)} %get-tuple-element.23.refs_2_.refs_1_), channel_id=1, source_target_pairs={{0,8},{2,10},{4,12},{6,14},{8,0},{10,2},{12,4},{14,6},{16,24},{18,... | collective-permute-start | bytes 1622024 | tf_op jit(solution)/shard_map/ppermute | solution.py:279
  27.0 1.5 %collective-permute-start = (f32[264,512]{1,0:T(8,128)}, f32[264,512]{1,0:T(8,128)}, u32[]{:S(2)}, u32[]{:S(2)}) collective-permute-start(f32[264,512]{1,0:T(8,128)} %bitcast.refs_0_), channel_id=1, source_target_pairs={{0,1},{1,0},{2,3},{3,2},{4,5},{5,4},{6,7},{7,6},{8,9},{9,8},{10,11... | collective-permute-start | bytes 1622024 | tf_op jit(solution)/shard_map/ppermute | solution.py:294
  28.5 0.6 collective-permute-start.13
  29.1 0.7 shard_map.121
  29.8 0.6 collective-permute-start.10
  30.4 8.4 %collective-permute-done.7.refs_2_ = f32[2,2,264,128]{3,2,1,0:T(8,128)S(1)} collective-permute-done((f32[2,2,264,128]{3,2,1,0:T(8,128)}, f32[2,2,264,128]{3,2,1,0:T(8,128)S(1)}, u32[]{:S(2)}, u32[]{:S(2)}) %collective-permute-start.7) | collective-permute-done | bytes 540704 | tf_op jit(solution)/shard_map/ppermute | solution.py:279
  38.8 0.3 shard_map.118.refs_5_.refs_2_
  39.1 1.6 %collective-permute-start.11 = (f32[264,512]{1,0:T(8,128)S(1)}, f32[264,512]{1,0:T(8,128)S(1)}, u32[]{:S(2)}, u32[]{:S(2)}) collective-permute-start(f32[264,512]{1,0:T(8,128)S(1)} %shard_map.118.refs_5_.refs_2_), channel_id=1, source_target_pairs={{0,8},{2,10},{4,12},{6,14},{8,0},{10,2},{12,4},{14,6},{16,24},{18,... | collective-permute-start | bytes 1622024 | tf_op jit(solution)/shard_map/ppermute | solution.py:279
  40.8 1.4 %shard_map.119 = (f32[264,512]{1,0:T(8,128)S(1)}, f32[264,512]{1,0:T(8,128)S(1)}) custom-call(f32[4,264,128]{2,1,0:T(8,128)S(1)} %get-tuple-element.16.refs_0_, f32[4,264,128]{2,1,0:T(8,128)S(1)} %collective-permute-done.1.refs_1_, f32[2,2,264,128]{3,2,1,0:T(8,128)S(1)} %collective-permute-done.7.refs_2_, bf16[512,512]{1,0:T(8,128)(2,1)S(1)} %get-tuple-element.22.refs_3_, ...), custom_call_target="tpu_custom_call" | custom-call | tf_op jit(solution)/shard_map/pallas_call | solution.py:97
  42.1 0.8 collective-permute-start.12
  42.9 1.3 %shard_map.120.refs_4_.refs_1_ = f32[264,512]{1,0:T(8,128)S(1)} custom-call(f32[264,512]{1,0:T(8,128)} %bitcast.refs_0_, f32[264,512]{1,0:T(8,128)} %collective-permute-done.refs_1_, f32[264,512]{1,0:T(8,128)S(1)} %get-tuple-element.24.refs_2_), custom_call_target="tpu_custom_call" | custom-call | tf_op jit(solution)/shard_map/pallas_call | solution.py:97
  44.2 1.3 %shard_map.122.refs_4_.refs_0_ = f32[264,512]{1,0:T(8,128)S(1)} custom-call(f32[4,264,128]{2,1,0:T(8,128)S(1)} %get-tuple-element.16.refs_0_, f32[4,264,128]{2,1,0:T(8,128)S(1)} %collective-permute-done.1.refs_1_, f32[2,1,264,128]{3,2,1,0:T(8,128)} %collective-permute-done.10.refs_2_, bf16[512,512]{1,0:T(8,128)(2,1)S(1)} %get-tuple-element.22.refs_3_, ...), custom_call_target="tpu_custom_call" | custom-call | tf_op jit(solution)/shard_map/pallas_call | solution.py:97
  45.5 4.0 %collective-permute-done.13.refs_7_ = f32[3,264,128]{2,1,0:T(8,128)S(1)} collective-permute-done((f32[3,264,128]{2,1,0:T(8,128)S(1)}, f32[3,264,128]{2,1,0:T(8,128)S(1)}, u32[]{:S(2)}, u32[]{:S(2)}) %collective-permute-start.13) | collective-permute-done | bytes 405536 | tf_op jit(solution)/shard_map/ppermute | solution.py:294
  49.5 1.3 %shard_map.123 = f32[256,512]{1,0:T(8,128)S(1)} custom-call(f32[1,512]{1,0:T(1,128)S(1)} %broadcast_in_dim.11.refs_0_, f32[264,512]{1,0:T(8,128)S(1)} %get-tuple-element.23.refs_2_.refs_1_, f32[264,512]{1,0:T(8,128)S(1)} %shard_map.118.refs_5_.refs_2_, f32[264,512]{1,0:T(8,128)S(1)} %get-tuple-element.25.refs_3_, f32[264,512]{1,0:T(8,128)S(1)} %shard_map.122.refs_4_.refs_0_, ...), custom_call_target="tpu_custom_call" | custom-call | tf_op jit(solution)/shard_map/pallas_call | solution.py:97
  51.0 1.2 %collective-permute-start.15 = (f32[64,512]{1,0:T(8,128)S(1)}, f32[64,512]{1,0:T(8,128)S(1)}, u32[]{:S(2)}, u32[]{:S(2)}) collective-permute-start(f32[64,512]{1,0:T(8,128)S(1)} %get-tuple-element.34), channel_id=1, source_target_pairs={{0,4},{2,6},{4,0},{6,2},{8,12},{10,14},{12,8},{14,10},{16,20},{18,... | collective-permute-start | bytes 393224 | tf_op jit(solution)/shard_map/ppermute | solution.py:279
  52.3 0.6 collective-permute-start.16
  52.9 3.8 %collective-permute-done.14.refs_1_ = f32[64,512]{1,0:T(8,128)S(1)} collective-permute-done((f32[64,512]{1,0:T(8,128)S(1)}, f32[64,512]{1,0:T(8,128)S(1)}, u32[]{:S(2)}, u32[]{:S(2)}) %collective-permute-start.14) | collective-permute-done | bytes 131104 | tf_op jit(solution)/shard_map/ppermute | solution.py:279
  56.7 2.4 %collective-permute-done.15.refs_2_ = f32[64,512]{1,0:T(8,128)S(1)} collective-permute-done((f32[64,512]{1,0:T(8,128)S(1)}, f32[64,512]{1,0:T(8,128)S(1)}, u32[]{:S(2)}, u32[]{:S(2)}) %collective-permute-start.15) | collective-permute-done | bytes 131104 | tf_op jit(solution)/shard_map/ppermute | solution.py:279
  59.1 0.5 collective-permute-start.18
  59.7 1.1 %collective-permute-done.11.refs_1_.refs_2_ = f32[264,512]{1,0:T(8,128)S(1)} collective-permute-done((f32[264,512]{1,0:T(8,128)S(1)}, f32[264,512]{1,0:T(8,128)S(1)}, u32[]{:S(2)}, u32[]{:S(2)}) %collective-permute-start.11) | collective-permute-done | bytes 540704 | tf_op jit(solution)/shard_map/ppermute | solution.py:279
  60.8 6.7 %collective-permute-done.18.refs_1_ = f32[64,512]{1,0:T(8,128)S(1)} collective-permute-done((f32[64,512]{1,0:T(8,128)S(1)}, f32[64,512]{1,0:T(8,128)S(1)}, u32[]{:S(2)}, u32[]{:S(2)}) %collective-permute-start.18) | collective-permute-done | bytes 131104 | tf_op jit(solution)/shard_map/ppermute | solution.py:279
  67.5 0.4 collective-permute-start.19
  67.9 1.6 %collective-permute-start.17 = (f32[264,512]{1,0:T(8,128)S(1)}, f32[264,512]{1,0:T(8,128)S(1)}, u32[]{:S(2)}, u32[]{:S(2)}) collective-permute-start(f32[264,512]{1,0:T(8,128)S(1)} %shard_map.125.refs_2_), channel_id=1, source_target_pairs={{0,1},{1,0},{2,3},{3,2},{4,5},{5,4},{6,7},{7,6},{8,9},{9,8},{10,11... | collective-permute-start | bytes 1622024 | tf_op jit(solution)/shard_map/ppermute | solution.py:294
  69.5 5.0 %collective-permute-done.19.refs_1_ = f32[64,512]{1,0:T(8,128)S(1)} collective-permute-done((f32[64,512]{1,0:T(8,128)S(1)}, f32[64,512]{1,0:T(8,128)S(1)}, u32[]{:S(2)}, u32[]{:S(2)}) %collective-permute-start.19) | collective-permute-done | bytes 131104 | tf_op jit(solution)/shard_map/ppermute | solution.py:279
  74.5 1.4 %collective-permute-start.20 = (f32[64,512]{1,0:T(8,128)S(1)}, f32[64,512]{1,0:T(8,128)S(1)}, u32[]{:S(2)}, u32[]{:S(2)}) collective-permute-start(f32[64,512]{1,0:T(8,128)S(1)} %shard_map.127), channel_id=1, source_target_pairs={{0,4},{2,6},{4,0},{6,2},{8,12},{10,14},{12,8},{14,10},{16,20},{18,... | collective-permute-start | bytes 393224 | tf_op jit(solution)/shard_map/ppermute | solution.py:279
  75.9 3.7 %collective-permute-done.20 = f32[64,512]{1,0:T(8,128)S(1)} collective-permute-done((f32[64,512]{1,0:T(8,128)S(1)}, f32[64,512]{1,0:T(8,128)S(1)}, u32[]{:S(2)}, u32[]{:S(2)}) %collective-permute-start.20) | collective-permute-done | bytes 131104 | tf_op jit(solution)/shard_map/ppermute | solution.py:279
  79.7 0.7 collective-permute-done.17.refs_3_
  80.5 0.7 collective-permute-done.21
  81.3 0.5 collective-permute-done.22.refs_1_
  81.8 1.4 %multiply_reduce_fusion.1 = (f32[512]{0:T(512)S(1)}, f32[512]{0:T(512)S(1)}, f32[1,1,256,512]{3,2,1,0:T(8,128)}, f32[1,1,256,512]{3,2,1,0:T(8,128)}) fusion(f32[256,512]{1,0:T(8,128)S(1)} %shard_map.128, f32[1,1,256,512]{3,2,1,0:T(8,128)S(1)} %copy-done.7, f32[1,1,256,512]{3,2,1,0:T(8,128)S(1)} %copy-done.8), kind=kLoop, calls=%fused_computation.5 | loop fusion | flops 1965056 | bytes 2625536 | tf_op jit(solution)/shard_map/reduce_sum | solution.py:33
  83.2 1.6 %collective-permute-start.23 = (f32[1,512]{1,0:T(1,128)S(1)}, f32[1,512]{1,0:T(1,128)S(1)}, u32[]{:S(2)}, u32[]{:S(2)}) collective-permute-start(f32[1,512]{1,0:T(1,128)S(1)} %bitcast.36), channel_id=1, source_target_pairs={{0,1},{1,0},{2,3},{3,2},{4,5},{5,4},{6,7},{7,6},{8,9},{9,8},{10,11... | collective-permute-start | bytes 6152 | tf_op jit(solution)/shard_map/ppermute | solution.py:294
  84.8 2.1 %collective-permute-done.23.refs_5_ = f32[1,512]{1,0:T(1,128)S(1)} collective-permute-done((f32[1,512]{1,0:T(1,128)S(1)}, f32[1,512]{1,0:T(1,128)S(1)}, u32[]{:S(2)}, u32[]{:S(2)}) %collective-permute-start.23) | collective-permute-done | bytes 2080 | tf_op jit(solution)/shard_map/ppermute | solution.py:294
  86.9 1.1 %shard_map.129 = (bf16[264,256]{1,0:T(8,128)(2,1)}, f32[264,512]{1,0:T(8,128)}) custom-call(f32[1,512]{1,0:T(1,128)S(1)} %broadcast_in_dim.11.refs_0_, f32[264,512]{1,0:T(8,128)S(1)} %shard_map.120.refs_4_.refs_1_, f32[264,512]{1,0:T(8,128)S(1)} %shard_map.125.refs_2_, f32[264,512]{1,0:T(8,128)S(1)} %collective-permute-done.17.refs_3_, ...), custom_call_target="tpu_custom_call" | custom-call | tf_op jit(solution)/shard_map/pallas_call | solution.py:97
  (48 shorter events, 0.9 us)
Async XLA Ops:
  0.6 0.9 %copy-start.5 = (bf16[264,256]{1,0:T(8,128)(2,1)S(1)}, bf16[264,256]{1,0:T(8,128)(2,1)}, u32[]{:S(2)}) copy-start(bf16[264,256]{1,0:T(8,128)(2,1)} %refs_5_.1) | copy-start | bytes 405508
  1.6 10.6 %collective-permute-start.5 = (f32[264,128]{1,0:T(8,128)S(1)}, f32[264,128]{1,0:T(8,128)S(1)}, u32[]{:S(2)}, u32[]{:S(2)}) collective-permute-start(f32[264,128]{1,0:T(8,128)S(1)} %shard_map.112.refs_0_), channel_id=1, source_target_pairs={{0,16},{2,18},{4,20},{6,22},{8,24},{10,26},{12,28},{14,30},{16,0},... | collective-permute-start | bytes 405512 | tf_op jit(solution)/shard_map/ppermute | solution.py:279
  5.8 0.9 %copy-start = (bf16[1,128,512]{2,1,0:T(8,128)(2,1)S(1)}, bf16[1,128,512]{2,1,0:T(8,128)(2,1)}, u32[]{:S(2)}) copy-start(bf16[1,128,512]{2,1,0:T(8,128)(2,1)} %refs_4_.1) | copy-start | bytes 393220
  6.7 1.2 %copy-start.2 = (bf16[1,128,4224]{2,1,0:T(8,128)(2,1)S(1)}, bf16[1,128,4224]{2,1,0:T(8,128)(2,1)}, u32[]{:S(2)}) copy-start(bf16[1,128,4224]{2,1,0:T(8,128)(2,1)} %refs_1_.2) | copy-start | bytes 3244036
  9.0 12.6 %collective-permute-start.3 = (f32[776,128]{1,0:T(8,128)S(1)}, f32[776,128]{1,0:T(8,128)S(1)}, u32[]{:S(2)}, u32[]{:S(2)}) collective-permute-start(f32[776,128]{1,0:T(8,128)S(1)} %get-tuple-element.20), channel_id=1, source_target_pairs={{0,4},{2,6},{4,0},{6,2},{8,12},{10,14},{12,8},{14,10},{16,20},{18,... | collective-permute-start | bytes 1191944 | tf_op jit(solution)/shard_map/ppermute | solution.py:279
  12.2 9.4 %collective-permute-start.6 = (f32[2,264,128]{2,1,0:T(8,128)S(1)}, f32[2,264,128]{2,1,0:T(8,128)S(1)}, u32[]{:S(2)}, u32[]{:S(2)}) collective-permute-start(f32[2,264,128]{2,1,0:T(8,128)S(1)} %shard_map.113), channel_id=1, source_target_pairs={{0,8},{2,10},{4,12},{6,14},{8,0},{10,2},{12,4},{14,6},{16,24},{18,... | collective-permute-start | bytes 811016 | tf_op jit(solution)/shard_map/ppermute | solution.py:279
  13.0 8.6 %collective-permute-start.4 = (f32[264,128]{1,0:T(8,128)S(1)}, f32[264,128]{1,0:T(8,128)S(1)}, u32[]{:S(2)}, u32[]{:S(2)}) collective-permute-start(f32[264,128]{1,0:T(8,128)S(1)} %get-tuple-element.21), channel_id=1, source_target_pairs={{0,6},{2,4},{4,2},{6,0},{8,14},{10,12},{12,10},{14,8},{16,22},{18,... | collective-permute-start | bytes 405512 | tf_op jit(solution)/shard_map/ppermute | solution.py:279
  13.8 8.8 %collective-permute-start.2 = (f32[3,264,128]{2,1,0:T(8,128)S(1)}, f32[3,264,128]{2,1,0:T(8,128)S(1)}, u32[]{:S(2)}, u32[]{:S(2)}) collective-permute-start(f32[3,264,128]{2,1,0:T(8,128)S(1)} %get-tuple-element.19), channel_id=1, source_target_pairs={{0,2},{2,0},{4,6},{6,4},{8,10},{10,8},{12,14},{14,12},{16,18},{18,... | collective-permute-start | bytes 1216520 | tf_op jit(solution)/shard_map/ppermute | solution.py:279
  14.6 10.4 %collective-permute-start.1 = (f32[4,264,128]{2,1,0:T(8,128)S(1)}, f32[4,264,128]{2,1,0:T(8,128)S(1)}, u32[]{:S(2)}, u32[]{:S(2)}) collective-permute-start(f32[4,264,128]{2,1,0:T(8,128)S(1)} %get-tuple-element.17), channel_id=1, source_target_pairs={{0,2},{2,0},{4,6},{6,4},{8,10},{10,8},{12,14},{14,12},{16,18},{18,... | collective-permute-start | bytes 1622024 | tf_op jit(solution)/shard_map/ppermute | solution.py:279
  21.7 3.3 %collective-permute-start.8 = (f32[2,512,128]{2,1,0:T(8,128)S(1)}, f32[2,512,128]{2,1,0:T(8,128)S(1)}, u32[]{:S(2)}, u32[]{:S(2)}) collective-permute-start(f32[2,512,128]{2,1,0:T(8,128)S(1)} %shard_map.114.refs_4_), channel_id=1, source_target_pairs={{0,2},{2,0},{4,6},{6,4},{8,10},{10,8},{12,14},{14,12},{16,18},{18,... | collective-permute-start | bytes 1572872 | tf_op jit(solution)/shard_map/ppermute | solution.py:279
  22.6 2.4 %copy-start.1 = (bf16[1,128,512]{2,1,0:T(8,128)(2,1)S(1)}, bf16[1,128,512]{2,1,0:T(8,128)(2,1)}, u32[]{:S(2)}) copy-start(bf16[1,128,512]{2,1,0:T(8,128)(2,1)} %refs_4_.1) | copy-start | bytes 393220
  23.5 15.3 %collective-permute-start.7 = (f32[2,2,264,128]{3,2,1,0:T(8,128)}, f32[2,2,264,128]{3,2,1,0:T(8,128)S(1)}, u32[]{:S(2)}, u32[]{:S(2)}) collective-permute-start(f32[2,2,264,128]{3,2,1,0:T(8,128)} %shard_map.115), channel_id=1, source_target_pairs={{0,4},{2,6},{4,0},{6,2},{8,12},{10,14},{12,8},{14,10},{16,20},{18,... | collective-permute-start | bytes 1622024 | tf_op jit(solution)/shard_map/ppermute | solution.py:279
  25.3 15.5 %collective-permute-start.9 = (f32[264,512]{1,0:T(8,128)S(1)}, f32[264,512]{1,0:T(8,128)}, u32[]{:S(2)}, u32[]{:S(2)}) collective-permute-start(f32[264,512]{1,0:T(8,128)S(1)} %get-tuple-element.23.refs_2_.refs_1_), channel_id=1, source_target_pairs={{0,8},{2,10},{4,12},{6,14},{8,0},{10,2},{12,4},{14,6},{16,24},{18,... | collective-permute-start | bytes 1622024 | tf_op jit(solution)/shard_map/ppermute | solution.py:279
  27.0 15.9 %collective-permute-start = (f32[264,512]{1,0:T(8,128)}, f32[264,512]{1,0:T(8,128)}, u32[]{:S(2)}, u32[]{:S(2)}) collective-permute-start(f32[264,512]{1,0:T(8,128)} %bitcast.refs_0_), channel_id=1, source_target_pairs={{0,1},{1,0},{2,3},{3,2},{4,5},{5,4},{6,7},{7,6},{8,9},{9,8},{10,11... | collective-permute-start | bytes 1622024 | tf_op jit(solution)/shard_map/ppermute | solution.py:294
  28.5 21.0 %collective-permute-start.13 = (f32[3,264,128]{2,1,0:T(8,128)S(1)}, f32[3,264,128]{2,1,0:T(8,128)S(1)}, u32[]{:S(2)}, u32[]{:S(2)}) collective-permute-start(f32[3,264,128]{2,1,0:T(8,128)S(1)} %shard_map.117.refs_4_.refs_6_), channel_id=1, source_target_pairs={{0,1},{1,0},{2,3},{3,2},{4,5},{5,4},{6,7},{7,6},{8,9},{9,8},{10,11... | collective-permute-start | bytes 1216520 | tf_op jit(solution)/shard_map/ppermute | solution.py:294
  29.8 14.4 %collective-permute-start.10 = (f32[2,1,264,128]{3,2,1,0:T(8,128)}, f32[2,1,264,128]{3,2,1,0:T(8,128)}, u32[]{:S(2)}, u32[]{:S(2)}) collective-permute-start(f32[2,1,264,128]{3,2,1,0:T(8,128)} %shard_map.121), channel_id=1, source_target_pairs={{0,4},{2,6},{4,0},{6,2},{8,12},{10,14},{12,8},{14,10},{16,20},{18,... | collective-permute-start | bytes 811016 | tf_op jit(solution)/shard_map/ppermute | solution.py:279
  39.1 21.6 %collective-permute-start.11 = (f32[264,512]{1,0:T(8,128)S(1)}, f32[264,512]{1,0:T(8,128)S(1)}, u32[]{:S(2)}, u32[]{:S(2)}) collective-permute-start(f32[264,512]{1,0:T(8,128)S(1)} %shard_map.118.refs_5_.refs_2_), channel_id=1, source_target_pairs={{0,8},{2,10},{4,12},{6,14},{8,0},{10,2},{12,4},{14,6},{16,24},{18,... | collective-permute-start | bytes 1622024 | tf_op jit(solution)/shard_map/ppermute | solution.py:279
  42.1 25.3 %collective-permute-start.12 = (f32[264,512]{1,0:T(8,128)S(1)}, f32[264,512]{1,0:T(8,128)S(1)}, u32[]{:S(2)}, u32[]{:S(2)}) collective-permute-start(f32[264,512]{1,0:T(8,128)S(1)} %get-tuple-element.24.refs_2_), channel_id=1, source_target_pairs={{0,16},{2,18},{4,20},{6,22},{8,24},{10,26},{12,28},{14,30},{16,0},... | collective-permute-start | bytes 1622024 | tf_op jit(solution)/shard_map/ppermute | solution.py:279
  44.2 5.3 %copy-start.6 = (bf16[264,256]{1,0:T(8,128)(2,1)S(1)}, bf16[264,256]{1,0:T(8,128)(2,1)}, u32[]{:S(2)}) copy-start(bf16[264,256]{1,0:T(8,128)(2,1)} %refs_5_.1) | copy-start | bytes 405508
  50.9 5.9 %collective-permute-start.14 = (f32[64,512]{1,0:T(8,128)S(1)}, f32[64,512]{1,0:T(8,128)S(1)}, u32[]{:S(2)}, u32[]{:S(2)}) collective-permute-start(f32[64,512]{1,0:T(8,128)S(1)} %get-tuple-element.35), channel_id=1, source_target_pairs={{0,6},{2,4},{4,2},{6,0},{8,14},{10,12},{12,10},{14,8},{16,22},{18,... | collective-permute-start | bytes 393224 | tf_op jit(solution)/shard_map/ppermute | solution.py:279
  51.0 8.1 %collective-permute-start.15 = (f32[64,512]{1,0:T(8,128)S(1)}, f32[64,512]{1,0:T(8,128)S(1)}, u32[]{:S(2)}, u32[]{:S(2)}) collective-permute-start(f32[64,512]{1,0:T(8,128)S(1)} %get-tuple-element.34), channel_id=1, source_target_pairs={{0,4},{2,6},{4,0},{6,2},{8,12},{10,14},{12,8},{14,10},{16,20},{18,... | collective-permute-start | bytes 393224 | tf_op jit(solution)/shard_map/ppermute | solution.py:279
  52.3 6.8 %collective-permute-start.16 = (f32[64,512]{1,0:T(8,128)S(1)}, f32[64,512]{1,0:T(8,128)S(1)}, u32[]{:S(2)}, u32[]{:S(2)}) collective-permute-start(f32[64,512]{1,0:T(8,128)S(1)} %get-tuple-element.32), channel_id=1, source_target_pairs={{0,2},{2,0},{4,6},{6,4},{8,10},{10,8},{12,14},{14,12},{16,18},{18,... | collective-permute-start | bytes 393224 | tf_op jit(solution)/shard_map/ppermute | solution.py:279
  59.1 8.3 %collective-permute-start.18 = (f32[64,512]{1,0:T(8,128)S(1)}, f32[64,512]{1,0:T(8,128)S(1)}, u32[]{:S(2)}, u32[]{:S(2)}) collective-permute-start(f32[64,512]{1,0:T(8,128)S(1)} %shard_map.124.refs_3_.refs_0_), channel_id=1, source_target_pairs={{0,8},{2,10},{4,12},{6,14},{8,0},{10,2},{12,4},{14,6},{16,24},{18,... | collective-permute-start | bytes 393224 | tf_op jit(solution)/shard_map/ppermute | solution.py:279
  67.5 7.0 %collective-permute-start.19 = (f32[64,512]{1,0:T(8,128)S(1)}, f32[64,512]{1,0:T(8,128)S(1)}, u32[]{:S(2)}, u32[]{:S(2)}) collective-permute-start(f32[64,512]{1,0:T(8,128)S(1)} %shard_map.126.refs_0_), channel_id=1, source_target_pairs={{0,16},{2,18},{4,20},{6,22},{8,24},{10,26},{12,28},{14,30},{16,0},... | collective-permute-start | bytes 393224 | tf_op jit(solution)/shard_map/ppermute | solution.py:279
  67.9 12.4 %collective-permute-start.17 = (f32[264,512]{1,0:T(8,128)S(1)}, f32[264,512]{1,0:T(8,128)S(1)}, u32[]{:S(2)}, u32[]{:S(2)}) collective-permute-start(f32[264,512]{1,0:T(8,128)S(1)} %shard_map.125.refs_2_), channel_id=1, source_target_pairs={{0,1},{1,0},{2,3},{3,2},{4,5},{5,4},{6,7},{7,6},{8,9},{9,8},{10,11... | collective-permute-start | bytes 1622024 | tf_op jit(solution)/shard_map/ppermute | solution.py:294
  74.5 5.0 %collective-permute-start.20 = (f32[64,512]{1,0:T(8,128)S(1)}, f32[64,512]{1,0:T(8,128)S(1)}, u32[]{:S(2)}, u32[]{:S(2)}) collective-permute-start(f32[64,512]{1,0:T(8,128)S(1)} %shard_map.127), channel_id=1, source_target_pairs={{0,4},{2,6},{4,0},{6,2},{8,12},{10,14},{12,8},{14,10},{16,20},{18,... | collective-permute-start | bytes 393224 | tf_op jit(solution)/shard_map/ppermute | solution.py:279
  79.6 1.6 %collective-permute-start.21 = (f32[128,512]{1,0:T(8,128)S(1)}, f32[128,512]{1,0:T(8,128)S(1)}, u32[]{:S(2)}, u32[]{:S(2)}) collective-permute-start(f32[128,512]{1,0:T(8,128)S(1)} %maximum_select_fusion.1), channel_id=1, source_target_pairs={{0,2},{2,0},{4,6},{6,4},{8,10},{10,8},{12,14},{14,12},{16,18},{18,... | collective-permute-start | bytes 786440 | tf_op jit(solution)/shard_map/ppermute | solution.py:279
  80.4 1.4 %collective-permute-start.22 = (f32[64,512]{1,0:T(8,128)S(1)}, f32[64,512]{1,0:T(8,128)S(1)}, u32[]{:S(2)}, u32[]{:S(2)}) collective-permute-start(f32[64,512]{1,0:T(8,128)S(1)} %slice.63), channel_id=1, source_target_pairs={{0,2},{2,0},{4,6},{6,4},{8,10},{10,8},{12,14},{14,12},{16,18},{18,... | collective-permute-start | bytes 393224 | tf_op jit(solution)/shard_map/ppermute | solution.py:279
  80.4 1.4 %copy-start.7 = (f32[1,1,256,512]{3,2,1,0:T(8,128)S(1)}, f32[1,1,256,512]{3,2,1,0:T(8,128)}, u32[]{:S(2)}) copy-start(f32[1,1,256,512]{3,2,1,0:T(8,128)} %param.11) | copy-start | bytes 1572868
  80.4 1.4 %copy-start.8 = (f32[1,1,256,512]{3,2,1,0:T(8,128)S(1)}, f32[1,1,256,512]{3,2,1,0:T(8,128)}, u32[]{:S(2)}) copy-start(f32[1,1,256,512]{3,2,1,0:T(8,128)} %param.12) | copy-start | bytes 1572868
  81.8 5.0 %copy-start.3 = (f32[264,512]{1,0:T(8,128)S(1)}, f32[264,512]{1,0:T(8,128)}, u32[]{:S(2)}) copy-start(f32[264,512]{1,0:T(8,128)} %refs_6_.1) | copy-start | bytes 1622020
  81.8 5.0 %copy-start.4 = (f32[264,512]{1,0:T(8,128)S(1)}, f32[264,512]{1,0:T(8,128)}, u32[]{:S(2)}) copy-start(f32[264,512]{1,0:T(8,128)} %refs_7_.1) | copy-start | bytes 1622020
  83.2 3.6 %collective-permute-start.23 = (f32[1,512]{1,0:T(1,128)S(1)}, f32[1,512]{1,0:T(1,128)S(1)}, u32[]{:S(2)}, u32[]{:S(2)}) collective-permute-start(f32[1,512]{1,0:T(1,128)S(1)} %bitcast.36), channel_id=1, source_target_pairs={{0,1},{1,0},{2,3},{3,2},{4,5},{5,4},{6,7},{7,6},{8,9},{9,8},{10,11... | collective-permute-start | bytes 6152 | tf_op jit(solution)/shard_map/ppermute | solution.py:294

commit v6 on v5

--- a/solution.py
+++ b/solution.py
@@ -79,7 +79,7 @@
     return (weights_block, new_momentum, new_first[None, None], new_second[None, None])
 
 
-VMEM_BYTES = 32 * 1024 * 1024
+VMEM_BYTES = 16 * 1024 * 1024
 
 
 def whole_block(shape):
@@ -234,6 +234,10 @@
     out[half:, :] = jnp.where(first, totals[1], totals[0])
 
 
+def scale_kernel(projected, first, second, out):
+    _, _, out[...] = moments_and_scale(projected[...], first[...], second[...])
+
+
 def outer_kernel(
     flag, inner_sum, grad, grad_other, scale, scale_other, weights, momentum, out, momentum_out
 ):
@@ -421,9 +425,15 @@
     partial = total(partial, partial_next)
     partial = double(partial, side, to_side)
     token = to_core(grad_other[: rank // 4])
-    projected = total(double(partial, core, to_core), after=[token])
-
-    new_first, new_second, scale = moments_and_scale(
+    projected = double(partial, core, to_core)
+    (scale,) = run(
+        scale_kernel,
+        [((1, cols), F32)],
+        [projected, first_moment[0, 0], second_moment[0, 0]],
+        after=[token],
+    )
+
+    new_first, new_second, _ = moments_and_scale(
         projected, first_moment[0, 0], second_moment[0, 0]
     )
     scale_other = to_island(scale)

time: 88.3 us -> 87.6 us (level)
  waiting for transfers between devices: 47.8 us -> 46.6 us
    reduce_sum x1 -> x0, other arithmetic: 1.35 us -> none  [moments_and_scale(): jnp.mean(adapted * adapted, axis=0, keepdims=True)]
    add x0 -> x1, other arithmetic: none -> 1.18 us  [moments_and_scale(): second_decay * second + (1.0 - second_decay) * projected * projected]
    ppermute x4, waiting for transfers between devices: 6.75 us -> 5.59 us  [to_island(): return lax.ppermute(value, 'island', [(0, 1), (1, 0)])]
  transfers between devices with their start and end apart: 24 -> 24, of which waited for: 14 -> 14; matrix products, arithmetic and copies ran while one was open for 0% -> 2% of each run, Pallas kernels for 10% -> 10%
where the time goes in v6:
time: 87.6 us; the launch traced here: 87.3 us
  waiting for transfers between devices  46.6 us (53%)
  starting transfers between devices  24.7 us (28%)
  Pallas kernels  10.6 us (12%)
  local copies, waits for them, and re-layouts  3.23 us (4%)
  other arithmetic  1.33 us (2%)
  between operations  0.88 us (1%)
    ppermute x20, waiting for transfers between devices, move(): return lax.ppermute(value, 'fsdp', pairs)  41 us
    ppermute x20, starting transfers between devices, move(): return lax.ppermute(value, 'fsdp', pairs)  19.4 us
    pallas_call x19, Pallas kernels, run(): pl.pallas_call(body, out_shape=[jax.ShapeDtypeStruct(shape, kind) for sha...  10.6 us
    ppermute x4, waiting for transfers between devices, to_island(): return lax.ppermute(value, 'island', [(0, 1), (1, 0)])  5.59 us
    ppermute x4, starting transfers between devices, to_island(): return lax.ppermute(value, 'island', [(0, 1), (1, 0)])  5.26 us
    unnamed x18, local copies, waits for them, and re-layouts  3.08 us
  transfers between devices with their start and end apart: 24, of which 14 were waited for; matrix products, arithmetic and copies ran while one was open for 2% of the time, Pallas kernels for 10%

profile of v6, /device:TPU:0, one launch (start us, length us, event | category | flops | bytes accessed | tf_op | source)
XLA Modules:
  0.0 87.3 jit_solution(1150276446856447470)
XLA Ops:
  0.7 0.9 %copy-done.7 = bf16[264,256]{1,0:T(8,128)(2,1)S(1)} copy-done((bf16[264,256]{1,0:T(8,128)(2,1)S(1)}, bf16[264,256]{1,0:T(8,128)(2,1)}, u32[]{:S(2)}) %copy-start.7) | copy-done | bytes 135192
  1.6 4.1 %collective-permute-start.5 = (f32[264,128]{1,0:T(8,128)S(1)}, f32[264,128]{1,0:T(8,128)S(1)}, u32[]{:S(2)}, u32[]{:S(2)}) collective-permute-start(f32[264,128]{1,0:T(8,128)S(1)} %shard_map.112.refs_0_), channel_id=1, source_target_pairs={{0,16},{2,18},{4,20},{6,22},{8,24},{10,26},{12,28},{14,30},{16,0},... | collective-permute-start | bytes 405512 | tf_op jit(solution)/shard_map/ppermute | solution.py:283
  5.8 0.9 %copy-done.2 = bf16[1,128,512]{2,1,0:T(8,128)(2,1)S(1)} copy-done((bf16[1,128,512]{2,1,0:T(8,128)(2,1)S(1)}, bf16[1,128,512]{2,1,0:T(8,128)(2,1)}, u32[]{:S(2)}) %copy-start.2) | copy-done | bytes 131096
  6.7 1.2 %copy-done.4 = bf16[1,128,4224]{2,1,0:T(8,128)(2,1)S(1)} copy-done((bf16[1,128,4224]{2,1,0:T(8,128)(2,1)S(1)}, bf16[1,128,4224]{2,1,0:T(8,128)(2,1)}, u32[]{:S(2)}) %copy-start.4) | copy-done | bytes 1081368
  7.9 1.1 %shard_map.111 = (f32[776,128]{1,0:T(8,128)S(1)}, f32[264,128]{1,0:T(8,128)S(1)}, f32[3,264,128]{2,1,0:T(8,128)S(1)}, f32[4,264,128]{2,1,0:T(8,128)S(1)}, f32[4,...) custom-call(s32[6]{0:T(128)S(1)} %stack.27.refs_0_, bf16[1,128,4224]{2,1,0:T(8,128)(2,1)S(1)} %copy-done.4, ...), custom_call_target="tpu_custom_call" | custom-call | tf_op jit(solution)/shard_map/pallas_call | solution.py:97
  9.0 1.6 %collective-permute-start.3 = (f32[776,128]{1,0:T(8,128)S(1)}, f32[776,128]{1,0:T(8,128)S(1)}, u32[]{:S(2)}, u32[]{:S(2)}) collective-permute-start(f32[776,128]{1,0:T(8,128)S(1)} %get-tuple-element.20), channel_id=1, source_target_pairs={{0,4},{2,6},{4,0},{6,2},{8,12},{10,14},{12,8},{14,10},{16,20},{18,... | collective-permute-start | bytes 1191944 | tf_op jit(solution)/shard_map/ppermute | solution.py:283
  10.5 1.6 %collective-permute-done.5.refs_1_.refs_0_ = f32[264,128]{1,0:T(8,128)S(1)} collective-permute-done((f32[264,128]{1,0:T(8,128)S(1)}, f32[264,128]{1,0:T(8,128)S(1)}, u32[]{:S(2)}, u32[]{:S(2)}) %collective-permute-start.5) | collective-permute-done | bytes 135200 | tf_op jit(solution)/shard_map/ppermute | solution.py:283
  12.2 0.8 collective-permute-start.6
  13.0 0.8 collective-permute-start.4
  13.8 0.8 collective-permute-start.2
  14.6 7.0 %collective-permute-done.4.refs_2_.refs_3_ = f32[264,128]{1,0:T(8,128)S(1)} collective-permute-done((f32[264,128]{1,0:T(8,128)S(1)}, f32[264,128]{1,0:T(8,128)S(1)}, u32[]{:S(2)}, u32[]{:S(2)}) %collective-permute-start.4) | collective-permute-done | bytes 135200 | tf_op jit(solution)/shard_map/ppermute | solution.py:283
  21.7 0.9 %collective-permute-start.8 = (f32[2,512,128]{2,1,0:T(8,128)S(1)}, f32[2,512,128]{2,1,0:T(8,128)S(1)}, u32[]{:S(2)}, u32[]{:S(2)}) collective-permute-start(f32[2,512,128]{2,1,0:T(8,128)S(1)} %shard_map.114.refs_4_), channel_id=1, source_target_pairs={{0,2},{2,0},{4,6},{6,4},{8,10},{10,8},{12,14},{14,12},{16,18},{18,... | collective-permute-start | bytes 1572872 | tf_op jit(solution)/shard_map/ppermute | solution.py:283
  22.6 0.8 shard_map.115
  23.5 1.5 %collective-permute-start.7 = (f32[2,2,264,128]{3,2,1,0:T(8,128)}, f32[2,2,264,128]{3,2,1,0:T(8,128)S(1)}, u32[]{:S(2)}, u32[]{:S(2)}) collective-permute-start(f32[2,2,264,128]{3,2,1,0:T(8,128)} %shard_map.115), channel_id=1, source_target_pairs={{0,4},{2,6},{4,0},{6,2},{8,12},{10,14},{12,8},{14,10},{16,20},{18,... | collective-permute-start | bytes 1622024 | tf_op jit(solution)/shard_map/ppermute | solution.py:283
  25.0 0.3 shard_map.116
  25.3 1.6 %collective-permute-start.9 = (f32[264,512]{1,0:T(8,128)S(1)}, f32[264,512]{1,0:T(8,128)}, u32[]{:S(2)}, u32[]{:S(2)}) collective-permute-start(f32[264,512]{1,0:T(8,128)S(1)} %get-tuple-element.23.refs_2_.refs_1_), channel_id=1, source_target_pairs={{0,8},{2,10},{4,12},{6,14},{8,0},{10,2},{12,4},{14,6},{16,24},{18,... | collective-permute-start | bytes 1622024 | tf_op jit(solution)/shard_map/ppermute | solution.py:283
  27.0 1.5 %collective-permute-start = (f32[264,512]{1,0:T(8,128)}, f32[264,512]{1,0:T(8,128)}, u32[]{:S(2)}, u32[]{:S(2)}) collective-permute-start(f32[264,512]{1,0:T(8,128)} %bitcast.refs_0_), channel_id=1, source_target_pairs={{0,1},{1,0},{2,3},{3,2},{4,5},{5,4},{6,7},{7,6},{8,9},{9,8},{10,11... | collective-permute-start | bytes 1622024 | tf_op jit(solution)/shard_map/ppermute | solution.py:298
  28.5 0.6 collective-permute-start.13
  29.1 0.7 shard_map.121
  29.8 0.6 collective-permute-start.10
  30.4 8.4 %collective-permute-done.7.refs_2_ = f32[2,2,264,128]{3,2,1,0:T(8,128)S(1)} collective-permute-done((f32[2,2,264,128]{3,2,1,0:T(8,128)}, f32[2,2,264,128]{3,2,1,0:T(8,128)S(1)}, u32[]{:S(2)}, u32[]{:S(2)}) %collective-permute-start.7) | collective-permute-done | bytes 540704 | tf_op jit(solution)/shard_map/ppermute | solution.py:283
  39.1 1.6 %collective-permute-start.11 = (f32[264,512]{1,0:T(8,128)S(1)}, f32[264,512]{1,0:T(8,128)S(1)}, u32[]{:S(2)}, u32[]{:S(2)}) collective-permute-start(f32[264,512]{1,0:T(8,128)S(1)} %shard_map.118.refs_5_.refs_2_), channel_id=1, source_target_pairs={{0,8},{2,10},{4,12},{6,14},{8,0},{10,2},{12,4},{14,6},{16,24},{18,... | collective-permute-start | bytes 1622024 | tf_op jit(solution)/shard_map/ppermute | solution.py:283
  40.8 1.4 %shard_map.119 = (f32[264,512]{1,0:T(8,128)S(1)}, f32[264,512]{1,0:T(8,128)S(1)}) custom-call(f32[4,264,128]{2,1,0:T(8,128)S(1)} %get-tuple-element.16.refs_0_, f32[4,264,128]{2,1,0:T(8,128)S(1)} %collective-permute-done.1.refs_1_, f32[2,2,264,128]{3,2,1,0:T(8,128)S(1)} %collective-permute-done.7.refs_2_, bf16[512,512]{1,0:T(8,128)(2,1)S(1)} %get-tuple-element.22.refs_3_, ...), custom_call_target="tpu_custom_call" | custom-call | tf_op jit(solution)/shard_map/pallas_call | solution.py:97
  42.1 0.8 collective-permute-start.12
  42.9 1.3 %shard_map.120.refs_4_.refs_1_ = f32[264,512]{1,0:T(8,128)S(1)} custom-call(f32[264,512]{1,0:T(8,128)} %bitcast.refs_0_, f32[264,512]{1,0:T(8,128)} %collective-permute-done.refs_1_, f32[264,512]{1,0:T(8,128)S(1)} %get-tuple-element.24.refs_2_), custom_call_target="tpu_custom_call" | custom-call | tf_op jit(solution)/shard_map/pallas_call | solution.py:97
  44.2 1.3 %shard_map.122.refs_4_.refs_0_ = f32[264,512]{1,0:T(8,128)S(1)} custom-call(f32[4,264,128]{2,1,0:T(8,128)S(1)} %get-tuple-element.16.refs_0_, f32[4,264,128]{2,1,0:T(8,128)S(1)} %collective-permute-done.1.refs_1_, f32[2,1,264,128]{3,2,1,0:T(8,128)} %collective-permute-done.10.refs_2_, bf16[512,512]{1,0:T(8,128)(2,1)S(1)} %get-tuple-element.22.refs_3_, ...), custom_call_target="tpu_custom_call" | custom-call | tf_op jit(solution)/shard_map/pallas_call | solution.py:97
  45.5 4.0 %collective-permute-done.13.refs_7_ = f32[3,264,128]{2,1,0:T(8,128)S(1)} collective-permute-done((f32[3,264,128]{2,1,0:T(8,128)S(1)}, f32[3,264,128]{2,1,0:T(8,128)S(1)}, u32[]{:S(2)}, u32[]{:S(2)}) %collective-permute-start.13) | collective-permute-done | bytes 405536 | tf_op jit(solution)/shard_map/ppermute | solution.py:298
  49.5 1.3 %shard_map.123 = f32[256,512]{1,0:T(8,128)S(1)} custom-call(f32[1,512]{1,0:T(1,128)S(1)} %broadcast_in_dim.2.refs_0_, f32[264,512]{1,0:T(8,128)S(1)} %get-tuple-element.23.refs_2_.refs_1_, f32[264,512]{1,0:T(8,128)S(1)} %shard_map.118.refs_5_.refs_2_, f32[264,512]{1,0:T(8,128)S(1)} %get-tuple-element.25.refs_3_, f32[264,512]{1,0:T(8,128)S(1)} %shard_map.122.refs_4_.refs_0_, ...), custom_call_target="tpu_custom_call" | custom-call | tf_op jit(solution)/shard_map/pallas_call | solution.py:97
  51.0 1.2 %collective-permute-start.15 = (f32[64,512]{1,0:T(8,128)S(1)}, f32[64,512]{1,0:T(8,128)S(1)}, u32[]{:S(2)}, u32[]{:S(2)}) collective-permute-start(f32[64,512]{1,0:T(8,128)S(1)} %get-tuple-element.32), channel_id=1, source_target_pairs={{0,4},{2,6},{4,0},{6,2},{8,12},{10,14},{12,8},{14,10},{16,20},{18,... | collective-permute-start | bytes 393224 | tf_op jit(solution)/shard_map/ppermute | solution.py:283
  52.3 0.6 collective-permute-start.16
  52.9 3.8 %collective-permute-done.14.refs_1_ = f32[64,512]{1,0:T(8,128)S(1)} collective-permute-done((f32[64,512]{1,0:T(8,128)S(1)}, f32[64,512]{1,0:T(8,128)S(1)}, u32[]{:S(2)}, u32[]{:S(2)}) %collective-permute-start.14) | collective-permute-done | bytes 131104 | tf_op jit(solution)/shard_map/ppermute | solution.py:283
  56.7 2.4 %collective-permute-done.15.refs_2_ = f32[64,512]{1,0:T(8,128)S(1)} collective-permute-done((f32[64,512]{1,0:T(8,128)S(1)}, f32[64,512]{1,0:T(8,128)S(1)}, u32[]{:S(2)}, u32[]{:S(2)}) %collective-permute-start.15) | collective-permute-done | bytes 131104 | tf_op jit(solution)/shard_map/ppermute | solution.py:283
  59.1 0.5 collective-permute-start.18
  59.7 1.1 %collective-permute-done.11.refs_1_.refs_2_ = f32[264,512]{1,0:T(8,128)S(1)} collective-permute-done((f32[264,512]{1,0:T(8,128)S(1)}, f32[264,512]{1,0:T(8,128)S(1)}, u32[]{:S(2)}, u32[]{:S(2)}) %collective-permute-start.11) | collective-permute-done | bytes 540704 | tf_op jit(solution)/shard_map/ppermute | solution.py:283
  60.8 6.7 %collective-permute-done.18.refs_1_ = f32[64,512]{1,0:T(8,128)S(1)} collective-permute-done((f32[64,512]{1,0:T(8,128)S(1)}, f32[64,512]{1,0:T(8,128)S(1)}, u32[]{:S(2)}, u32[]{:S(2)}) %collective-permute-start.18) | collective-permute-done | bytes 131104 | tf_op jit(solution)/shard_map/ppermute | solution.py:283
  67.5 0.4 collective-permute-start.19
  68.0 1.6 %collective-permute-start.17 = (f32[264,512]{1,0:T(8,128)S(1)}, f32[264,512]{1,0:T(8,128)S(1)}, u32[]{:S(2)}, u32[]{:S(2)}) collective-permute-start(f32[264,512]{1,0:T(8,128)S(1)} %shard_map.125.refs_2_), channel_id=1, source_target_pairs={{0,1},{1,0},{2,3},{3,2},{4,5},{5,4},{6,7},{7,6},{8,9},{9,8},{10,11... | collective-permute-start | bytes 1622024 | tf_op jit(solution)/shard_map/ppermute | solution.py:298
  69.5 5.0 %collective-permute-done.19.refs_1_ = f32[64,512]{1,0:T(8,128)S(1)} collective-permute-done((f32[64,512]{1,0:T(8,128)S(1)}, f32[64,512]{1,0:T(8,128)S(1)}, u32[]{:S(2)}, u32[]{:S(2)}) %collective-permute-start.19) | collective-permute-done | bytes 131104 | tf_op jit(solution)/shard_map/ppermute | solution.py:283
  74.5 1.4 %collective-permute-start.20 = (f32[64,512]{1,0:T(8,128)S(1)}, f32[64,512]{1,0:T(8,128)S(1)}, u32[]{:S(2)}, u32[]{:S(2)}) collective-permute-start(f32[64,512]{1,0:T(8,128)S(1)} %shard_map.127), channel_id=1, source_target_pairs={{0,4},{2,6},{4,0},{6,2},{8,12},{10,14},{12,8},{14,10},{16,20},{18,... | collective-permute-start | bytes 393224 | tf_op jit(solution)/shard_map/ppermute | solution.py:283
  75.9 3.7 %collective-permute-done.20 = f32[64,512]{1,0:T(8,128)S(1)} collective-permute-done((f32[64,512]{1,0:T(8,128)S(1)}, f32[64,512]{1,0:T(8,128)S(1)}, u32[]{:S(2)}, u32[]{:S(2)}) %collective-permute-start.20) | collective-permute-done | bytes 131104 | tf_op jit(solution)/shard_map/ppermute | solution.py:283
  79.7 0.7 collective-permute-done.17.refs_3_
  80.5 0.7 collective-permute-done.21
  81.3 0.5 collective-permute-done.22.refs_3_
  81.8 0.7 shard_map.128.refs_4_
  82.5 1.6 %collective-permute-start.23 = (f32[1,512]{1,0:T(1,128)S(1)}, f32[1,512]{1,0:T(1,128)S(1)}, u32[]{:S(2)}, u32[]{:S(2)}) collective-permute-start(f32[1,512]{1,0:T(1,128)S(1)} %shard_map.128.refs_4_), channel_id=1, source_target_pairs={{0,1},{1,0},{2,3},{3,2},{4,5},{5,4},{6,7},{7,6},{8,9},{9,8},{10,11... | collective-permute-start | bytes 6152 | tf_op jit(solution)/shard_map/ppermute | solution.py:298
  84.1 1.2 %fusion = (f32[1,1,256,512]{3,2,1,0:T(8,128)}, f32[1,1,256,512]{3,2,1,0:T(8,128)}) fusion(f32[1,1,256,512]{3,2,1,0:T(8,128)S(1)} %copy-done.1, f32[1,1,128,512]{3,2,1,0:T(8,128)S(1)} %bitcast.25, f32[1,1,128,512]{3,2,1,0:T(8,128)S(1)} %bitcast.26, pred[]{:T(512)S(6)} %eq.9, f32[1,1,256,512]{3,2,1,0:T(8,128)S(1)} %copy-done), kind=kLoop, calls=%fused_computation.1 | loop fusion | flops 1310720 | bytes 2621441 | tf_op jit(solution)/shard_map/add | solution.py:31
  85.3 0.9 %collective-permute-done.23.refs_5_ = f32[1,512]{1,0:T(1,128)S(1)} collective-permute-done((f32[1,512]{1,0:T(1,128)S(1)}, f32[1,512]{1,0:T(1,128)S(1)}, u32[]{:S(2)}, u32[]{:S(2)}) %collective-permute-start.23) | collective-permute-done | bytes 2080 | tf_op jit(solution)/shard_map/ppermute | solution.py:298
  86.2 1.1 %shard_map.129 = (bf16[264,256]{1,0:T(8,128)(2,1)}, f32[264,512]{1,0:T(8,128)}) custom-call(f32[1,512]{1,0:T(1,128)S(1)} %broadcast_in_dim.2.refs_0_, f32[264,512]{1,0:T(8,128)S(1)} %shard_map.120.refs_4_.refs_1_, f32[264,512]{1,0:T(8,128)S(1)} %shard_map.125.refs_2_, f32[264,512]{1,0:T(8,128)S(1)} %collective-permute-done.17.refs_3_, ...), custom_call_target="tpu_custom_call" | custom-call | tf_op jit(solution)/shard_map/pallas_call | solution.py:97
  (47 shorter events, 1.2 us)
Async XLA Ops:
  0.6 0.9 %copy-start.7 = (bf16[264,256]{1,0:T(8,128)(2,1)S(1)}, bf16[264,256]{1,0:T(8,128)(2,1)}, u32[]{:S(2)}) copy-start(bf16[264,256]{1,0:T(8,128)(2,1)} %refs_5_.1) | copy-start | bytes 405508
  1.6 10.6 %collective-permute-start.5 = (f32[264,128]{1,0:T(8,128)S(1)}, f32[264,128]{1,0:T(8,128)S(1)}, u32[]{:S(2)}, u32[]{:S(2)}) collective-permute-start(f32[264,128]{1,0:T(8,128)S(1)} %shard_map.112.refs_0_), channel_id=1, source_target_pairs={{0,16},{2,18},{4,20},{6,22},{8,24},{10,26},{12,28},{14,30},{16,0},... | collective-permute-start | bytes 405512 | tf_op jit(solution)/shard_map/ppermute | solution.py:283
  5.8 0.9 %copy-start.2 = (bf16[1,128,512]{2,1,0:T(8,128)(2,1)S(1)}, bf16[1,128,512]{2,1,0:T(8,128)(2,1)}, u32[]{:S(2)}) copy-start(bf16[1,128,512]{2,1,0:T(8,128)(2,1)} %refs_4_.1) | copy-start | bytes 393220
  6.7 1.2 %copy-start.4 = (bf16[1,128,4224]{2,1,0:T(8,128)(2,1)S(1)}, bf16[1,128,4224]{2,1,0:T(8,128)(2,1)}, u32[]{:S(2)}) copy-start(bf16[1,128,4224]{2,1,0:T(8,128)(2,1)} %refs_1_.2) | copy-start | bytes 3244036
  9.0 12.6 %collective-permute-start.3 = (f32[776,128]{1,0:T(8,128)S(1)}, f32[776,128]{1,0:T(8,128)S(1)}, u32[]{:S(2)}, u32[]{:S(2)}) collective-permute-start(f32[776,128]{1,0:T(8,128)S(1)} %get-tuple-element.20), channel_id=1, source_target_pairs={{0,4},{2,6},{4,0},{6,2},{8,12},{10,14},{12,8},{14,10},{16,20},{18,... | collective-permute-start | bytes 1191944 | tf_op jit(solution)/shard_map/ppermute | solution.py:283
  12.2 9.4 %collective-permute-start.6 = (f32[2,264,128]{2,1,0:T(8,128)S(1)}, f32[2,264,128]{2,1,0:T(8,128)S(1)}, u32[]{:S(2)}, u32[]{:S(2)}) collective-permute-start(f32[2,264,128]{2,1,0:T(8,128)S(1)} %shard_map.113), channel_id=1, source_target_pairs={{0,8},{2,10},{4,12},{6,14},{8,0},{10,2},{12,4},{14,6},{16,24},{18,... | collective-permute-start | bytes 811016 | tf_op jit(solution)/shard_map/ppermute | solution.py:283
  13.0 8.6 %collective-permute-start.4 = (f32[264,128]{1,0:T(8,128)S(1)}, f32[264,128]{1,0:T(8,128)S(1)}, u32[]{:S(2)}, u32[]{:S(2)}) collective-permute-start(f32[264,128]{1,0:T(8,128)S(1)} %get-tuple-element.21), channel_id=1, source_target_pairs={{0,6},{2,4},{4,2},{6,0},{8,14},{10,12},{12,10},{14,8},{16,22},{18,... | collective-permute-start | bytes 405512 | tf_op jit(solution)/shard_map/ppermute | solution.py:283
  13.8 8.8 %collective-permute-start.2 = (f32[3,264,128]{2,1,0:T(8,128)S(1)}, f32[3,264,128]{2,1,0:T(8,128)S(1)}, u32[]{:S(2)}, u32[]{:S(2)}) collective-permute-start(f32[3,264,128]{2,1,0:T(8,128)S(1)} %get-tuple-element.19), channel_id=1, source_target_pairs={{0,2},{2,0},{4,6},{6,4},{8,10},{10,8},{12,14},{14,12},{16,18},{18,... | collective-permute-start | bytes 1216520 | tf_op jit(solution)/shard_map/ppermute | solution.py:283
  14.6 10.4 %collective-permute-start.1 = (f32[4,264,128]{2,1,0:T(8,128)S(1)}, f32[4,264,128]{2,1,0:T(8,128)S(1)}, u32[]{:S(2)}, u32[]{:S(2)}) collective-permute-start(f32[4,264,128]{2,1,0:T(8,128)S(1)} %get-tuple-element.17), channel_id=1, source_target_pairs={{0,2},{2,0},{4,6},{6,4},{8,10},{10,8},{12,14},{14,12},{16,18},{18,... | collective-permute-start | bytes 1622024 | tf_op jit(solution)/shard_map/ppermute | solution.py:283
  21.7 3.3 %collective-permute-start.8 = (f32[2,512,128]{2,1,0:T(8,128)S(1)}, f32[2,512,128]{2,1,0:T(8,128)S(1)}, u32[]{:S(2)}, u32[]{:S(2)}) collective-permute-start(f32[2,512,128]{2,1,0:T(8,128)S(1)} %shard_map.114.refs_4_), channel_id=1, source_target_pairs={{0,2},{2,0},{4,6},{6,4},{8,10},{10,8},{12,14},{14,12},{16,18},{18,... | collective-permute-start | bytes 1572872 | tf_op jit(solution)/shard_map/ppermute | solution.py:283
  22.6 2.4 %copy-start.3 = (bf16[1,128,512]{2,1,0:T(8,128)(2,1)S(1)}, bf16[1,128,512]{2,1,0:T(8,128)(2,1)}, u32[]{:S(2)}) copy-start(bf16[1,128,512]{2,1,0:T(8,128)(2,1)} %refs_4_.1) | copy-start | bytes 393220
  23.5 15.3 %collective-permute-start.7 = (f32[2,2,264,128]{3,2,1,0:T(8,128)}, f32[2,2,264,128]{3,2,1,0:T(8,128)S(1)}, u32[]{:S(2)}, u32[]{:S(2)}) collective-permute-start(f32[2,2,264,128]{3,2,1,0:T(8,128)} %shard_map.115), channel_id=1, source_target_pairs={{0,4},{2,6},{4,0},{6,2},{8,12},{10,14},{12,8},{14,10},{16,20},{18,... | collective-permute-start | bytes 1622024 | tf_op jit(solution)/shard_map/ppermute | solution.py:283
  25.3 15.5 %collective-permute-start.9 = (f32[264,512]{1,0:T(8,128)S(1)}, f32[264,512]{1,0:T(8,128)}, u32[]{:S(2)}, u32[]{:S(2)}) collective-permute-start(f32[264,512]{1,0:T(8,128)S(1)} %get-tuple-element.23.refs_2_.refs_1_), channel_id=1, source_target_pairs={{0,8},{2,10},{4,12},{6,14},{8,0},{10,2},{12,4},{14,6},{16,24},{18,... | collective-permute-start | bytes 1622024 | tf_op jit(solution)/shard_map/ppermute | solution.py:283
  27.0 15.9 %collective-permute-start = (f32[264,512]{1,0:T(8,128)}, f32[264,512]{1,0:T(8,128)}, u32[]{:S(2)}, u32[]{:S(2)}) collective-permute-start(f32[264,512]{1,0:T(8,128)} %bitcast.refs_0_), channel_id=1, source_target_pairs={{0,1},{1,0},{2,3},{3,2},{4,5},{5,4},{6,7},{7,6},{8,9},{9,8},{10,11... | collective-permute-start | bytes 1622024 | tf_op jit(solution)/shard_map/ppermute | solution.py:298
  28.5 21.0 %collective-permute-start.13 = (f32[3,264,128]{2,1,0:T(8,128)S(1)}, f32[3,264,128]{2,1,0:T(8,128)S(1)}, u32[]{:S(2)}, u32[]{:S(2)}) collective-permute-start(f32[3,264,128]{2,1,0:T(8,128)S(1)} %shard_map.117.refs_4_.refs_6_), channel_id=1, source_target_pairs={{0,1},{1,0},{2,3},{3,2},{4,5},{5,4},{6,7},{7,6},{8,9},{9,8},{10,11... | collective-permute-start | bytes 1216520 | tf_op jit(solution)/shard_map/ppermute | solution.py:298
  29.8 14.4 %collective-permute-start.10 = (f32[2,1,264,128]{3,2,1,0:T(8,128)}, f32[2,1,264,128]{3,2,1,0:T(8,128)}, u32[]{:S(2)}, u32[]{:S(2)}) collective-permute-start(f32[2,1,264,128]{3,2,1,0:T(8,128)} %shard_map.121), channel_id=1, source_target_pairs={{0,4},{2,6},{4,0},{6,2},{8,12},{10,14},{12,8},{14,10},{16,20},{18,... | collective-permute-start | bytes 811016 | tf_op jit(solution)/shard_map/ppermute | solution.py:283
  39.1 21.6 %collective-permute-start.11 = (f32[264,512]{1,0:T(8,128)S(1)}, f32[264,512]{1,0:T(8,128)S(1)}, u32[]{:S(2)}, u32[]{:S(2)}) collective-permute-start(f32[264,512]{1,0:T(8,128)S(1)} %shard_map.118.refs_5_.refs_2_), channel_id=1, source_target_pairs={{0,8},{2,10},{4,12},{6,14},{8,0},{10,2},{12,4},{14,6},{16,24},{18,... | collective-permute-start | bytes 1622024 | tf_op jit(solution)/shard_map/ppermute | solution.py:283
  42.1 25.3 %collective-permute-start.12 = (f32[264,512]{1,0:T(8,128)S(1)}, f32[264,512]{1,0:T(8,128)S(1)}, u32[]{:S(2)}, u32[]{:S(2)}) collective-permute-start(f32[264,512]{1,0:T(8,128)S(1)} %get-tuple-element.24.refs_2_), channel_id=1, source_target_pairs={{0,16},{2,18},{4,20},{6,22},{8,24},{10,26},{12,28},{14,30},{16,0},... | collective-permute-start | bytes 1622024 | tf_op jit(solution)/shard_map/ppermute | solution.py:283
  44.2 5.3 %copy-start.8 = (bf16[264,256]{1,0:T(8,128)(2,1)S(1)}, bf16[264,256]{1,0:T(8,128)(2,1)}, u32[]{:S(2)}) copy-start(bf16[264,256]{1,0:T(8,128)(2,1)} %refs_5_.1) | copy-start | bytes 405508
  50.9 5.9 %collective-permute-start.14 = (f32[64,512]{1,0:T(8,128)S(1)}, f32[64,512]{1,0:T(8,128)S(1)}, u32[]{:S(2)}, u32[]{:S(2)}) collective-permute-start(f32[64,512]{1,0:T(8,128)S(1)} %get-tuple-element.33), channel_id=1, source_target_pairs={{0,6},{2,4},{4,2},{6,0},{8,14},{10,12},{12,10},{14,8},{16,22},{18,... | collective-permute-start | bytes 393224 | tf_op jit(solution)/shard_map/ppermute | solution.py:283
  51.0 8.1 %collective-permute-start.15 = (f32[64,512]{1,0:T(8,128)S(1)}, f32[64,512]{1,0:T(8,128)S(1)}, u32[]{:S(2)}, u32[]{:S(2)}) collective-permute-start(f32[64,512]{1,0:T(8,128)S(1)} %get-tuple-element.32), channel_id=1, source_target_pairs={{0,4},{2,6},{4,0},{6,2},{8,12},{10,14},{12,8},{14,10},{16,20},{18,... | collective-permute-start | bytes 393224 | tf_op jit(solution)/shard_map/ppermute | solution.py:283
  52.3 6.8 %collective-permute-start.16 = (f32[64,512]{1,0:T(8,128)S(1)}, f32[64,512]{1,0:T(8,128)S(1)}, u32[]{:S(2)}, u32[]{:S(2)}) collective-permute-start(f32[64,512]{1,0:T(8,128)S(1)} %get-tuple-element.30), channel_id=1, source_target_pairs={{0,2},{2,0},{4,6},{6,4},{8,10},{10,8},{12,14},{14,12},{16,18},{18,... | collective-permute-start | bytes 393224 | tf_op jit(solution)/shard_map/ppermute | solution.py:283
  59.1 8.3 %collective-permute-start.18 = (f32[64,512]{1,0:T(8,128)S(1)}, f32[64,512]{1,0:T(8,128)S(1)}, u32[]{:S(2)}, u32[]{:S(2)}) collective-permute-start(f32[64,512]{1,0:T(8,128)S(1)} %shard_map.124.refs_3_.refs_0_), channel_id=1, source_target_pairs={{0,8},{2,10},{4,12},{6,14},{8,0},{10,2},{12,4},{14,6},{16,24},{18,... | collective-permute-start | bytes 393224 | tf_op jit(solution)/shard_map/ppermute | solution.py:283
  67.5 7.0 %collective-permute-start.19 = (f32[64,512]{1,0:T(8,128)S(1)}, f32[64,512]{1,0:T(8,128)S(1)}, u32[]{:S(2)}, u32[]{:S(2)}) collective-permute-start(f32[64,512]{1,0:T(8,128)S(1)} %shard_map.126.refs_0_), channel_id=1, source_target_pairs={{0,16},{2,18},{4,20},{6,22},{8,24},{10,26},{12,28},{14,30},{16,0},... | collective-permute-start | bytes 393224 | tf_op jit(solution)/shard_map/ppermute | solution.py:283
  67.9 13.9 %copy-start = (f32[1,1,256,512]{3,2,1,0:T(8,128)S(1)}, f32[1,1,256,512]{3,2,1,0:T(8,128)}, u32[]{:S(2)}) copy-start(f32[1,1,256,512]{3,2,1,0:T(8,128)} %param.11) | copy-start | bytes 1572868
  67.9 13.9 %copy-start.1 = (f32[1,1,256,512]{3,2,1,0:T(8,128)S(1)}, f32[1,1,256,512]{3,2,1,0:T(8,128)}, u32[]{:S(2)}) copy-start(f32[1,1,256,512]{3,2,1,0:T(8,128)} %param.12) | copy-start | bytes 1572868
  68.0 12.4 %collective-permute-start.17 = (f32[264,512]{1,0:T(8,128)S(1)}, f32[264,512]{1,0:T(8,128)S(1)}, u32[]{:S(2)}, u32[]{:S(2)}) collective-permute-start(f32[264,512]{1,0:T(8,128)S(1)} %shard_map.125.refs_2_), channel_id=1, source_target_pairs={{0,1},{1,0},{2,3},{3,2},{4,5},{5,4},{6,7},{7,6},{8,9},{9,8},{10,11... | collective-permute-start | bytes 1622024 | tf_op jit(solution)/shard_map/ppermute | solution.py:298
  74.5 5.0 %collective-permute-start.20 = (f32[64,512]{1,0:T(8,128)S(1)}, f32[64,512]{1,0:T(8,128)S(1)}, u32[]{:S(2)}, u32[]{:S(2)}) collective-permute-start(f32[64,512]{1,0:T(8,128)S(1)} %shard_map.127), channel_id=1, source_target_pairs={{0,4},{2,6},{4,0},{6,2},{8,12},{10,14},{12,8},{14,10},{16,20},{18,... | collective-permute-start | bytes 393224 | tf_op jit(solution)/shard_map/ppermute | solution.py:283
  79.6 1.6 %collective-permute-start.21 = (f32[128,512]{1,0:T(8,128)S(1)}, f32[128,512]{1,0:T(8,128)S(1)}, u32[]{:S(2)}, u32[]{:S(2)}) collective-permute-start(f32[128,512]{1,0:T(8,128)S(1)} %maximum_select_fusion.2), channel_id=1, source_target_pairs={{0,2},{2,0},{4,6},{6,4},{8,10},{10,8},{12,14},{14,12},{16,18},{18,... | collective-permute-start | bytes 786440 | tf_op jit(solution)/shard_map/ppermute | solution.py:283
  80.4 1.4 %collective-permute-start.22 = (f32[64,512]{1,0:T(8,128)S(1)}, f32[64,512]{1,0:T(8,128)S(1)}, u32[]{:S(2)}, u32[]{:S(2)}) collective-permute-start(f32[64,512]{1,0:T(8,128)S(1)} %slice.63), channel_id=1, source_target_pairs={{0,2},{2,0},{4,6},{6,4},{8,10},{10,8},{12,14},{14,12},{16,18},{18,... | collective-permute-start | bytes 393224 | tf_op jit(solution)/shard_map/ppermute | solution.py:283
  82.5 3.7 %collective-permute-start.23 = (f32[1,512]{1,0:T(1,128)S(1)}, f32[1,512]{1,0:T(1,128)S(1)}, u32[]{:S(2)}, u32[]{:S(2)}) collective-permute-start(f32[1,512]{1,0:T(1,128)S(1)} %shard_map.128.refs_4_), channel_id=1, source_target_pairs={{0,1},{1,0},{2,3},{3,2},{4,5},{5,4},{6,7},{7,6},{8,9},{9,8},{10,11... | collective-permute-start | bytes 6152 | tf_op jit(solution)/shard_map/ppermute | solution.py:298
  84.1 2.1 %copy-start.5 = (f32[264,512]{1,0:T(8,128)S(1)}, f32[264,512]{1,0:T(8,128)}, u32[]{:S(2)}) copy-start(f32[264,512]{1,0:T(8,128)} %refs_6_.1) | copy-start | bytes 1622020
  84.1 2.1 %copy-start.6 = (f32[264,512]{1,0:T(8,128)S(1)}, f32[264,512]{1,0:T(8,128)}, u32[]{:S(2)}) copy-start(f32[264,512]{1,0:T(8,128)} %refs_7_.1) | copy-start | bytes 1622020

commit v7 on v6

--- a/solution.py
+++ b/solution.py
@@ -424,7 +424,7 @@
     partial_next = to_place(partial, 2)
     partial = total(partial, partial_next)
     partial = double(partial, side, to_side)
-    token = to_core(grad_other[: rank // 4])
+    token = to_core(grad_other[: rank // 16])
     projected = double(partial, core, to_core)
     (scale,) = run(
         scale_kernel,

time: 87.6 us -> 87.4 us (level)
  no operation moved by 1% of the time
where the time goes in v7:
time: 87.4 us; the launch traced here: 87.1 us
  waiting for transfers between devices  46.5 us (53%)
  starting transfers between devices  24.6 us (28%)
  Pallas kernels  10.6 us (12%)
  local copies, waits for them, and re-layouts  3.22 us (4%)
  other arithmetic  1.33 us (2%)
    ppermute x20, waiting for transfers between devices, move(): return lax.ppermute(value, 'fsdp', pairs)  40.9 us
    ppermute x20, starting transfers between devices, move(): return lax.ppermute(value, 'fsdp', pairs)  19.4 us
    pallas_call x19, Pallas kernels, run(): pl.pallas_call(body, out_shape=[jax.ShapeDtypeStruct(shape, kind) for sha...  10.6 us
    ppermute x4, waiting for transfers between devices, to_island(): return lax.ppermute(value, 'island', [(0, 1), (1, 0)])  5.58 us
    ppermute x4, starting transfers between devices, to_island(): return lax.ppermute(value, 'island', [(0, 1), (1, 0)])  5.26 us
    unnamed x18, local copies, waits for them, and re-layouts  3.08 us
  transfers between devices with their start and end apart: 24, of which 14 were waited for; matrix products, arithmetic and copies ran while one was open for 2% of the time, Pallas kernels for 10%

profile of v7, /device:TPU:0, one launch (start us, length us, event | category | flops | bytes accessed | tf_op | source)
XLA Modules:
  0.0 87.1 jit_solution(15100706162855827525)
XLA Ops:
  0.7 0.9 %copy-done.7 = bf16[264,256]{1,0:T(8,128)(2,1)S(1)} copy-done((bf16[264,256]{1,0:T(8,128)(2,1)S(1)}, bf16[264,256]{1,0:T(8,128)(2,1)}, u32[]{:S(2)}) %copy-start.7) | copy-done | bytes 135192
  1.6 4.1 %collective-permute-start.5 = (f32[264,128]{1,0:T(8,128)S(1)}, f32[264,128]{1,0:T(8,128)S(1)}, u32[]{:S(2)}, u32[]{:S(2)}) collective-permute-start(f32[264,128]{1,0:T(8,128)S(1)} %shard_map.112.refs_0_), channel_id=1, source_target_pairs={{0,16},{2,18},{4,20},{6,22},{8,24},{10,26},{12,28},{14,30},{16,0},... | collective-permute-start | bytes 405512 | tf_op jit(solution)/shard_map/ppermute | solution.py:283
  5.8 0.9 %copy-done.2 = bf16[1,128,512]{2,1,0:T(8,128)(2,1)S(1)} copy-done((bf16[1,128,512]{2,1,0:T(8,128)(2,1)S(1)}, bf16[1,128,512]{2,1,0:T(8,128)(2,1)}, u32[]{:S(2)}) %copy-start.2) | copy-done | bytes 131096
  6.7 1.2 %copy-done.4 = bf16[1,128,4224]{2,1,0:T(8,128)(2,1)S(1)} copy-done((bf16[1,128,4224]{2,1,0:T(8,128)(2,1)S(1)}, bf16[1,128,4224]{2,1,0:T(8,128)(2,1)}, u32[]{:S(2)}) %copy-start.4) | copy-done | bytes 1081368
  7.9 1.1 %shard_map.111 = (f32[776,128]{1,0:T(8,128)S(1)}, f32[264,128]{1,0:T(8,128)S(1)}, f32[3,264,128]{2,1,0:T(8,128)S(1)}, f32[4,264,128]{2,1,0:T(8,128)S(1)}, f32[4,...) custom-call(s32[6]{0:T(128)S(1)} %stack.27.refs_0_, bf16[1,128,4224]{2,1,0:T(8,128)(2,1)S(1)} %copy-done.4, ...), custom_call_target="tpu_custom_call" | custom-call | tf_op jit(solution)/shard_map/pallas_call | solution.py:97
  9.0 1.6 %collective-permute-start.3 = (f32[776,128]{1,0:T(8,128)S(1)}, f32[776,128]{1,0:T(8,128)S(1)}, u32[]{:S(2)}, u32[]{:S(2)}) collective-permute-start(f32[776,128]{1,0:T(8,128)S(1)} %get-tuple-element.20), channel_id=1, source_target_pairs={{0,4},{2,6},{4,0},{6,2},{8,12},{10,14},{12,8},{14,10},{16,20},{18,... | collective-permute-start | bytes 1191944 | tf_op jit(solution)/shard_map/ppermute | solution.py:283
  10.5 1.6 %collective-permute-done.5.refs_1_.refs_0_ = f32[264,128]{1,0:T(8,128)S(1)} collective-permute-done((f32[264,128]{1,0:T(8,128)S(1)}, f32[264,128]{1,0:T(8,128)S(1)}, u32[]{:S(2)}, u32[]{:S(2)}) %collective-permute-start.5) | collective-permute-done | bytes 135200 | tf_op jit(solution)/shard_map/ppermute | solution.py:283
  12.2 0.8 collective-permute-start.6
  13.0 0.8 collective-permute-start.4
  13.8 0.8 collective-permute-start.2
  14.6 7.0 %collective-permute-done.4.refs_2_.refs_3_ = f32[264,128]{1,0:T(8,128)S(1)} collective-permute-done((f32[264,128]{1,0:T(8,128)S(1)}, f32[264,128]{1,0:T(8,128)S(1)}, u32[]{:S(2)}, u32[]{:S(2)}) %collective-permute-start.4) | collective-permute-done | bytes 135200 | tf_op jit(solution)/shard_map/ppermute | solution.py:283
  21.7 0.9 %collective-permute-start.8 = (f32[2,512,128]{2,1,0:T(8,128)S(1)}, f32[2,512,128]{2,1,0:T(8,128)S(1)}, u32[]{:S(2)}, u32[]{:S(2)}) collective-permute-start(f32[2,512,128]{2,1,0:T(8,128)S(1)} %shard_map.114.refs_4_), channel_id=1, source_target_pairs={{0,2},{2,0},{4,6},{6,4},{8,10},{10,8},{12,14},{14,12},{16,18},{18,... | collective-permute-start | bytes 1572872 | tf_op jit(solution)/shard_map/ppermute | solution.py:283
  22.6 0.8 shard_map.115
  23.5 1.5 %collective-permute-start.7 = (f32[2,2,264,128]{3,2,1,0:T(8,128)}, f32[2,2,264,128]{3,2,1,0:T(8,128)S(1)}, u32[]{:S(2)}, u32[]{:S(2)}) collective-permute-start(f32[2,2,264,128]{3,2,1,0:T(8,128)} %shard_map.115), channel_id=1, source_target_pairs={{0,4},{2,6},{4,0},{6,2},{8,12},{10,14},{12,8},{14,10},{16,20},{18,... | collective-permute-start | bytes 1622024 | tf_op jit(solution)/shard_map/ppermute | solution.py:283
  25.0 0.3 shard_map.116
  25.3 1.6 %collective-permute-start.9 = (f32[264,512]{1,0:T(8,128)S(1)}, f32[264,512]{1,0:T(8,128)}, u32[]{:S(2)}, u32[]{:S(2)}) collective-permute-start(f32[264,512]{1,0:T(8,128)S(1)} %get-tuple-element.23.refs_2_.refs_1_), channel_id=1, source_target_pairs={{0,8},{2,10},{4,12},{6,14},{8,0},{10,2},{12,4},{14,6},{16,24},{18,... | collective-permute-start | bytes 1622024 | tf_op jit(solution)/shard_map/ppermute | solution.py:283
  27.0 1.5 %collective-permute-start = (f32[264,512]{1,0:T(8,128)}, f32[264,512]{1,0:T(8,128)}, u32[]{:S(2)}, u32[]{:S(2)}) collective-permute-start(f32[264,512]{1,0:T(8,128)} %bitcast.refs_0_), channel_id=1, source_target_pairs={{0,1},{1,0},{2,3},{3,2},{4,5},{5,4},{6,7},{7,6},{8,9},{9,8},{10,11... | collective-permute-start | bytes 1622024 | tf_op jit(solution)/shard_map/ppermute | solution.py:298
  28.5 0.6 collective-permute-start.13
  29.1 0.7 shard_map.121
  29.8 0.6 collective-permute-start.10
  30.4 8.4 %collective-permute-done.7.refs_2_ = f32[2,2,264,128]{3,2,1,0:T(8,128)S(1)} collective-permute-done((f32[2,2,264,128]{3,2,1,0:T(8,128)}, f32[2,2,264,128]{3,2,1,0:T(8,128)S(1)}, u32[]{:S(2)}, u32[]{:S(2)}) %collective-permute-start.7) | collective-permute-done | bytes 540704 | tf_op jit(solution)/shard_map/ppermute | solution.py:283
  39.1 1.6 %collective-permute-start.11 = (f32[264,512]{1,0:T(8,128)S(1)}, f32[264,512]{1,0:T(8,128)S(1)}, u32[]{:S(2)}, u32[]{:S(2)}) collective-permute-start(f32[264,512]{1,0:T(8,128)S(1)} %shard_map.118.refs_5_.refs_2_), channel_id=1, source_target_pairs={{0,8},{2,10},{4,12},{6,14},{8,0},{10,2},{12,4},{14,6},{16,24},{18,... | collective-permute-start | bytes 1622024 | tf_op jit(solution)/shard_map/ppermute | solution.py:283
  40.8 1.4 %shard_map.119 = (f32[264,512]{1,0:T(8,128)S(1)}, f32[264,512]{1,0:T(8,128)S(1)}) custom-call(f32[4,264,128]{2,1,0:T(8,128)S(1)} %get-tuple-element.16.refs_0_, f32[4,264,128]{2,1,0:T(8,128)S(1)} %collective-permute-done.1.refs_1_, f32[2,2,264,128]{3,2,1,0:T(8,128)S(1)} %collective-permute-done.7.refs_2_, bf16[512,512]{1,0:T(8,128)(2,1)S(1)} %get-tuple-element.22.refs_3_, ...), custom_call_target="tpu_custom_call" | custom-call | tf_op jit(solution)/shard_map/pallas_call | solution.py:97
  42.1 0.8 collective-permute-start.12
  42.9 1.3 %shard_map.120.refs_4_.refs_1_ = f32[264,512]{1,0:T(8,128)S(1)} custom-call(f32[264,512]{1,0:T(8,128)} %bitcast.refs_0_, f32[264,512]{1,0:T(8,128)} %collective-permute-done.refs_1_, f32[264,512]{1,0:T(8,128)S(1)} %get-tuple-element.24.refs_2_), custom_call_target="tpu_custom_call" | custom-call | tf_op jit(solution)/shard_map/pallas_call | solution.py:97
  44.2 1.3 %shard_map.122.refs_4_.refs_0_ = f32[264,512]{1,0:T(8,128)S(1)} custom-call(f32[4,264,128]{2,1,0:T(8,128)S(1)} %get-tuple-element.16.refs_0_, f32[4,264,128]{2,1,0:T(8,128)S(1)} %collective-permute-done.1.refs_1_, f32[2,1,264,128]{3,2,1,0:T(8,128)} %collective-permute-done.10.refs_2_, bf16[512,512]{1,0:T(8,128)(2,1)S(1)} %get-tuple-element.22.refs_3_, ...), custom_call_target="tpu_custom_call" | custom-call | tf_op jit(solution)/shard_map/pallas_call | solution.py:97
  45.5 4.0 %collective-permute-done.13.refs_7_ = f32[3,264,128]{2,1,0:T(8,128)S(1)} collective-permute-done((f32[3,264,128]{2,1,0:T(8,128)S(1)}, f32[3,264,128]{2,1,0:T(8,128)S(1)}, u32[]{:S(2)}, u32[]{:S(2)}) %collective-permute-start.13) | collective-permute-done | bytes 405536 | tf_op jit(solution)/shard_map/ppermute | solution.py:298
  49.5 1.3 %shard_map.123 = f32[256,512]{1,0:T(8,128)S(1)} custom-call(f32[1,512]{1,0:T(1,128)S(1)} %broadcast_in_dim.2.refs_0_, f32[264,512]{1,0:T(8,128)S(1)} %get-tuple-element.23.refs_2_.refs_1_, f32[264,512]{1,0:T(8,128)S(1)} %shard_map.118.refs_5_.refs_2_, f32[264,512]{1,0:T(8,128)S(1)} %get-tuple-element.25.refs_3_, f32[264,512]{1,0:T(8,128)S(1)} %shard_map.122.refs_4_.refs_0_, ...), custom_call_target="tpu_custom_call" | custom-call | tf_op jit(solution)/shard_map/pallas_call | solution.py:97
  51.0 1.2 %collective-permute-start.15 = (f32[64,512]{1,0:T(8,128)S(1)}, f32[64,512]{1,0:T(8,128)S(1)}, u32[]{:S(2)}, u32[]{:S(2)}) collective-permute-start(f32[64,512]{1,0:T(8,128)S(1)} %get-tuple-element.32), channel_id=1, source_target_pairs={{0,4},{2,6},{4,0},{6,2},{8,12},{10,14},{12,8},{14,10},{16,20},{18,... | collective-permute-start | bytes 393224 | tf_op jit(solution)/shard_map/ppermute | solution.py:283
  52.3 0.6 collective-permute-start.16
  52.9 3.8 %collective-permute-done.14.refs_1_ = f32[64,512]{1,0:T(8,128)S(1)} collective-permute-done((f32[64,512]{1,0:T(8,128)S(1)}, f32[64,512]{1,0:T(8,128)S(1)}, u32[]{:S(2)}, u32[]{:S(2)}) %collective-permute-start.14) | collective-permute-done | bytes 131104 | tf_op jit(solution)/shard_map/ppermute | solution.py:283
  56.7 2.4 %collective-permute-done.15.refs_2_ = f32[64,512]{1,0:T(8,128)S(1)} collective-permute-done((f32[64,512]{1,0:T(8,128)S(1)}, f32[64,512]{1,0:T(8,128)S(1)}, u32[]{:S(2)}, u32[]{:S(2)}) %collective-permute-start.15) | collective-permute-done | bytes 131104 | tf_op jit(solution)/shard_map/ppermute | solution.py:283
  59.1 0.5 collective-permute-start.18
  59.7 1.1 %collective-permute-done.11.refs_1_.refs_2_ = f32[264,512]{1,0:T(8,128)S(1)} collective-permute-done((f32[264,512]{1,0:T(8,128)S(1)}, f32[264,512]{1,0:T(8,128)S(1)}, u32[]{:S(2)}, u32[]{:S(2)}) %collective-permute-start.11) | collective-permute-done | bytes 540704 | tf_op jit(solution)/shard_map/ppermute | solution.py:283
  60.8 6.7 %collective-permute-done.18.refs_1_ = f32[64,512]{1,0:T(8,128)S(1)} collective-permute-done((f32[64,512]{1,0:T(8,128)S(1)}, f32[64,512]{1,0:T(8,128)S(1)}, u32[]{:S(2)}, u32[]{:S(2)}) %collective-permute-start.18) | collective-permute-done | bytes 131104 | tf_op jit(solution)/shard_map/ppermute | solution.py:283
  67.5 0.4 collective-permute-start.19
  68.0 1.6 %collective-permute-start.17 = (f32[264,512]{1,0:T(8,128)S(1)}, f32[264,512]{1,0:T(8,128)S(1)}, u32[]{:S(2)}, u32[]{:S(2)}) collective-permute-start(f32[264,512]{1,0:T(8,128)S(1)} %shard_map.125.refs_2_), channel_id=1, source_target_pairs={{0,1},{1,0},{2,3},{3,2},{4,5},{5,4},{6,7},{7,6},{8,9},{9,8},{10,11... | collective-permute-start | bytes 1622024 | tf_op jit(solution)/shard_map/ppermute | solution.py:298
  69.5 5.0 %collective-permute-done.19.refs_1_ = f32[64,512]{1,0:T(8,128)S(1)} collective-permute-done((f32[64,512]{1,0:T(8,128)S(1)}, f32[64,512]{1,0:T(8,128)S(1)}, u32[]{:S(2)}, u32[]{:S(2)}) %collective-permute-start.19) | collective-permute-done | bytes 131104 | tf_op jit(solution)/shard_map/ppermute | solution.py:283
  74.5 1.4 %collective-permute-start.20 = (f32[64,512]{1,0:T(8,128)S(1)}, f32[64,512]{1,0:T(8,128)S(1)}, u32[]{:S(2)}, u32[]{:S(2)}) collective-permute-start(f32[64,512]{1,0:T(8,128)S(1)} %shard_map.127), channel_id=1, source_target_pairs={{0,4},{2,6},{4,0},{6,2},{8,12},{10,14},{12,8},{14,10},{16,20},{18,... | collective-permute-start | bytes 393224 | tf_op jit(solution)/shard_map/ppermute | solution.py:283
  75.9 3.7 %collective-permute-done.20 = f32[64,512]{1,0:T(8,128)S(1)} collective-permute-done((f32[64,512]{1,0:T(8,128)S(1)}, f32[64,512]{1,0:T(8,128)S(1)}, u32[]{:S(2)}, u32[]{:S(2)}) %collective-permute-start.20) | collective-permute-done | bytes 131104 | tf_op jit(solution)/shard_map/ppermute | solution.py:283
  79.7 0.7 collective-permute-done.17.refs_3_
  80.4 0.8 collective-permute-done.21
  81.3 0.3 collective-permute-done.22.refs_3_
  81.6 0.7 shard_map.128.refs_4_
  82.3 1.6 %collective-permute-start.23 = (f32[1,512]{1,0:T(1,128)S(1)}, f32[1,512]{1,0:T(1,128)S(1)}, u32[]{:S(2)}, u32[]{:S(2)}) collective-permute-start(f32[1,512]{1,0:T(1,128)S(1)} %shard_map.128.refs_4_), channel_id=1, source_target_pairs={{0,1},{1,0},{2,3},{3,2},{4,5},{5,4},{6,7},{7,6},{8,9},{9,8},{10,11... | collective-permute-start | bytes 6152 | tf_op jit(solution)/shard_map/ppermute | solution.py:298
  83.9 1.2 %fusion = (f32[1,1,256,512]{3,2,1,0:T(8,128)}, f32[1,1,256,512]{3,2,1,0:T(8,128)}) fusion(f32[1,1,256,512]{3,2,1,0:T(8,128)S(1)} %copy-done.1, f32[1,1,128,512]{3,2,1,0:T(8,128)S(1)} %bitcast.25, f32[1,1,128,512]{3,2,1,0:T(8,128)S(1)} %bitcast.26, pred[]{:T(512)S(6)} %eq.9, f32[1,1,256,512]{3,2,1,0:T(8,128)S(1)} %copy-done), kind=kLoop, calls=%fused_computation.1 | loop fusion | flops 1310720 | bytes 2621441 | tf_op jit(solution)/shard_map/add | solution.py:31
  85.1 0.9 %collective-permute-done.23.refs_5_ = f32[1,512]{1,0:T(1,128)S(1)} collective-permute-done((f32[1,512]{1,0:T(1,128)S(1)}, f32[1,512]{1,0:T(1,128)S(1)}, u32[]{:S(2)}, u32[]{:S(2)}) %collective-permute-start.23) | collective-permute-done | bytes 2080 | tf_op jit(solution)/shard_map/ppermute | solution.py:298
  86.0 1.1 %shard_map.129 = (bf16[264,256]{1,0:T(8,128)(2,1)}, f32[264,512]{1,0:T(8,128)}) custom-call(f32[1,512]{1,0:T(1,128)S(1)} %broadcast_in_dim.2.refs_0_, f32[264,512]{1,0:T(8,128)S(1)} %shard_map.120.refs_4_.refs_1_, f32[264,512]{1,0:T(8,128)S(1)} %shard_map.125.refs_2_, f32[264,512]{1,0:T(8,128)S(1)} %collective-permute-done.17.refs_3_, ...), custom_call_target="tpu_custom_call" | custom-call | tf_op jit(solution)/shard_map/pallas_call | solution.py:97
  (47 shorter events, 1.1 us)
Async XLA Ops:
  0.6 0.9 %copy-start.7 = (bf16[264,256]{1,0:T(8,128)(2,1)S(1)}, bf16[264,256]{1,0:T(8,128)(2,1)}, u32[]{:S(2)}) copy-start(bf16[264,256]{1,0:T(8,128)(2,1)} %refs_5_.1) | copy-start | bytes 405508
  1.6 10.6 %collective-permute-start.5 = (f32[264,128]{1,0:T(8,128)S(1)}, f32[264,128]{1,0:T(8,128)S(1)}, u32[]{:S(2)}, u32[]{:S(2)}) collective-permute-start(f32[264,128]{1,0:T(8,128)S(1)} %shard_map.112.refs_0_), channel_id=1, source_target_pairs={{0,16},{2,18},{4,20},{6,22},{8,24},{10,26},{12,28},{14,30},{16,0},... | collective-permute-start | bytes 405512 | tf_op jit(solution)/shard_map/ppermute | solution.py:283
  5.8 0.9 %copy-start.2 = (bf16[1,128,512]{2,1,0:T(8,128)(2,1)S(1)}, bf16[1,128,512]{2,1,0:T(8,128)(2,1)}, u32[]{:S(2)}) copy-start(bf16[1,128,512]{2,1,0:T(8,128)(2,1)} %refs_4_.1) | copy-start | bytes 393220
  6.7 1.2 %copy-start.4 = (bf16[1,128,4224]{2,1,0:T(8,128)(2,1)S(1)}, bf16[1,128,4224]{2,1,0:T(8,128)(2,1)}, u32[]{:S(2)}) copy-start(bf16[1,128,4224]{2,1,0:T(8,128)(2,1)} %refs_1_.2) | copy-start | bytes 3244036
  9.0 12.6 %collective-permute-start.3 = (f32[776,128]{1,0:T(8,128)S(1)}, f32[776,128]{1,0:T(8,128)S(1)}, u32[]{:S(2)}, u32[]{:S(2)}) collective-permute-start(f32[776,128]{1,0:T(8,128)S(1)} %get-tuple-element.20), channel_id=1, source_target_pairs={{0,4},{2,6},{4,0},{6,2},{8,12},{10,14},{12,8},{14,10},{16,20},{18,... | collective-permute-start | bytes 1191944 | tf_op jit(solution)/shard_map/ppermute | solution.py:283
  12.2 9.4 %collective-permute-start.6 = (f32[2,264,128]{2,1,0:T(8,128)S(1)}, f32[2,264,128]{2,1,0:T(8,128)S(1)}, u32[]{:S(2)}, u32[]{:S(2)}) collective-permute-start(f32[2,264,128]{2,1,0:T(8,128)S(1)} %shard_map.113), channel_id=1, source_target_pairs={{0,8},{2,10},{4,12},{6,14},{8,0},{10,2},{12,4},{14,6},{16,24},{18,... | collective-permute-start | bytes 811016 | tf_op jit(solution)/shard_map/ppermute | solution.py:283
  13.0 8.6 %collective-permute-start.4 = (f32[264,128]{1,0:T(8,128)S(1)}, f32[264,128]{1,0:T(8,128)S(1)}, u32[]{:S(2)}, u32[]{:S(2)}) collective-permute-start(f32[264,128]{1,0:T(8,128)S(1)} %get-tuple-element.21), channel_id=1, source_target_pairs={{0,6},{2,4},{4,2},{6,0},{8,14},{10,12},{12,10},{14,8},{16,22},{18,... | collective-permute-start | bytes 405512 | tf_op jit(solution)/shard_map/ppermute | solution.py:283
  13.8 8.8 %collective-permute-start.2 = (f32[3,264,128]{2,1,0:T(8,128)S(1)}, f32[3,264,128]{2,1,0:T(8,128)S(1)}, u32[]{:S(2)}, u32[]{:S(2)}) collective-permute-start(f32[3,264,128]{2,1,0:T(8,128)S(1)} %get-tuple-element.19), channel_id=1, source_target_pairs={{0,2},{2,0},{4,6},{6,4},{8,10},{10,8},{12,14},{14,12},{16,18},{18,... | collective-permute-start | bytes 1216520 | tf_op jit(solution)/shard_map/ppermute | solution.py:283
  14.6 10.4 %collective-permute-start.1 = (f32[4,264,128]{2,1,0:T(8,128)S(1)}, f32[4,264,128]{2,1,0:T(8,128)S(1)}, u32[]{:S(2)}, u32[]{:S(2)}) collective-permute-start(f32[4,264,128]{2,1,0:T(8,128)S(1)} %get-tuple-element.17), channel_id=1, source_target_pairs={{0,2},{2,0},{4,6},{6,4},{8,10},{10,8},{12,14},{14,12},{16,18},{18,... | collective-permute-start | bytes 1622024 | tf_op jit(solution)/shard_map/ppermute | solution.py:283
  21.7 3.3 %collective-permute-start.8 = (f32[2,512,128]{2,1,0:T(8,128)S(1)}, f32[2,512,128]{2,1,0:T(8,128)S(1)}, u32[]{:S(2)}, u32[]{:S(2)}) collective-permute-start(f32[2,512,128]{2,1,0:T(8,128)S(1)} %shard_map.114.refs_4_), channel_id=1, source_target_pairs={{0,2},{2,0},{4,6},{6,4},{8,10},{10,8},{12,14},{14,12},{16,18},{18,... | collective-permute-start | bytes 1572872 | tf_op jit(solution)/shard_map/ppermute | solution.py:283
  22.6 2.4 %copy-start.3 = (bf16[1,128,512]{2,1,0:T(8,128)(2,1)S(1)}, bf16[1,128,512]{2,1,0:T(8,128)(2,1)}, u32[]{:S(2)}) copy-start(bf16[1,128,512]{2,1,0:T(8,128)(2,1)} %refs_4_.1) | copy-start | bytes 393220
  23.5 15.3 %collective-permute-start.7 = (f32[2,2,264,128]{3,2,1,0:T(8,128)}, f32[2,2,264,128]{3,2,1,0:T(8,128)S(1)}, u32[]{:S(2)}, u32[]{:S(2)}) collective-permute-start(f32[2,2,264,128]{3,2,1,0:T(8,128)} %shard_map.115), channel_id=1, source_target_pairs={{0,4},{2,6},{4,0},{6,2},{8,12},{10,14},{12,8},{14,10},{16,20},{18,... | collective-permute-start | bytes 1622024 | tf_op jit(solution)/shard_map/ppermute | solution.py:283
  25.3 15.5 %collective-permute-start.9 = (f32[264,512]{1,0:T(8,128)S(1)}, f32[264,512]{1,0:T(8,128)}, u32[]{:S(2)}, u32[]{:S(2)}) collective-permute-start(f32[264,512]{1,0:T(8,128)S(1)} %get-tuple-element.23.refs_2_.refs_1_), channel_id=1, source_target_pairs={{0,8},{2,10},{4,12},{6,14},{8,0},{10,2},{12,4},{14,6},{16,24},{18,... | collective-permute-start | bytes 1622024 | tf_op jit(solution)/shard_map/ppermute | solution.py:283
  27.0 15.9 %collective-permute-start = (f32[264,512]{1,0:T(8,128)}, f32[264,512]{1,0:T(8,128)}, u32[]{:S(2)}, u32[]{:S(2)}) collective-permute-start(f32[264,512]{1,0:T(8,128)} %bitcast.refs_0_), channel_id=1, source_target_pairs={{0,1},{1,0},{2,3},{3,2},{4,5},{5,4},{6,7},{7,6},{8,9},{9,8},{10,11... | collective-permute-start | bytes 1622024 | tf_op jit(solution)/shard_map/ppermute | solution.py:298
  28.5 21.0 %collective-permute-start.13 = (f32[3,264,128]{2,1,0:T(8,128)S(1)}, f32[3,264,128]{2,1,0:T(8,128)S(1)}, u32[]{:S(2)}, u32[]{:S(2)}) collective-permute-start(f32[3,264,128]{2,1,0:T(8,128)S(1)} %shard_map.117.refs_4_.refs_6_), channel_id=1, source_target_pairs={{0,1},{1,0},{2,3},{3,2},{4,5},{5,4},{6,7},{7,6},{8,9},{9,8},{10,11... | collective-permute-start | bytes 1216520 | tf_op jit(solution)/shard_map/ppermute | solution.py:298
  29.8 14.4 %collective-permute-start.10 = (f32[2,1,264,128]{3,2,1,0:T(8,128)}, f32[2,1,264,128]{3,2,1,0:T(8,128)}, u32[]{:S(2)}, u32[]{:S(2)}) collective-permute-start(f32[2,1,264,128]{3,2,1,0:T(8,128)} %shard_map.121), channel_id=1, source_target_pairs={{0,4},{2,6},{4,0},{6,2},{8,12},{10,14},{12,8},{14,10},{16,20},{18,... | collective-permute-start | bytes 811016 | tf_op jit(solution)/shard_map/ppermute | solution.py:283
  39.1 21.6 %collective-permute-start.11 = (f32[264,512]{1,0:T(8,128)S(1)}, f32[264,512]{1,0:T(8,128)S(1)}, u32[]{:S(2)}, u32[]{:S(2)}) collective-permute-start(f32[264,512]{1,0:T(8,128)S(1)} %shard_map.118.refs_5_.refs_2_), channel_id=1, source_target_pairs={{0,8},{2,10},{4,12},{6,14},{8,0},{10,2},{12,4},{14,6},{16,24},{18,... | collective-permute-start | bytes 1622024 | tf_op jit(solution)/shard_map/ppermute | solution.py:283
  42.1 25.3 %collective-permute-start.12 = (f32[264,512]{1,0:T(8,128)S(1)}, f32[264,512]{1,0:T(8,128)S(1)}, u32[]{:S(2)}, u32[]{:S(2)}) collective-permute-start(f32[264,512]{1,0:T(8,128)S(1)} %get-tuple-element.24.refs_2_), channel_id=1, source_target_pairs={{0,16},{2,18},{4,20},{6,22},{8,24},{10,26},{12,28},{14,30},{16,0},... | collective-permute-start | bytes 1622024 | tf_op jit(solution)/shard_map/ppermute | solution.py:283
  44.2 5.3 %copy-start.8 = (bf16[264,256]{1,0:T(8,128)(2,1)S(1)}, bf16[264,256]{1,0:T(8,128)(2,1)}, u32[]{:S(2)}) copy-start(bf16[264,256]{1,0:T(8,128)(2,1)} %refs_5_.1) | copy-start | bytes 405508
  50.9 5.9 %collective-permute-start.14 = (f32[64,512]{1,0:T(8,128)S(1)}, f32[64,512]{1,0:T(8,128)S(1)}, u32[]{:S(2)}, u32[]{:S(2)}) collective-permute-start(f32[64,512]{1,0:T(8,128)S(1)} %get-tuple-element.33), channel_id=1, source_target_pairs={{0,6},{2,4},{4,2},{6,0},{8,14},{10,12},{12,10},{14,8},{16,22},{18,... | collective-permute-start | bytes 393224 | tf_op jit(solution)/shard_map/ppermute | solution.py:283
  51.0 8.1 %collective-permute-start.15 = (f32[64,512]{1,0:T(8,128)S(1)}, f32[64,512]{1,0:T(8,128)S(1)}, u32[]{:S(2)}, u32[]{:S(2)}) collective-permute-start(f32[64,512]{1,0:T(8,128)S(1)} %get-tuple-element.32), channel_id=1, source_target_pairs={{0,4},{2,6},{4,0},{6,2},{8,12},{10,14},{12,8},{14,10},{16,20},{18,... | collective-permute-start | bytes 393224 | tf_op jit(solution)/shard_map/ppermute | solution.py:283
  52.3 6.8 %collective-permute-start.16 = (f32[64,512]{1,0:T(8,128)S(1)}, f32[64,512]{1,0:T(8,128)S(1)}, u32[]{:S(2)}, u32[]{:S(2)}) collective-permute-start(f32[64,512]{1,0:T(8,128)S(1)} %get-tuple-element.30), channel_id=1, source_target_pairs={{0,2},{2,0},{4,6},{6,4},{8,10},{10,8},{12,14},{14,12},{16,18},{18,... | collective-permute-start | bytes 393224 | tf_op jit(solution)/shard_map/ppermute | solution.py:283
  59.1 8.3 %collective-permute-start.18 = (f32[64,512]{1,0:T(8,128)S(1)}, f32[64,512]{1,0:T(8,128)S(1)}, u32[]{:S(2)}, u32[]{:S(2)}) collective-permute-start(f32[64,512]{1,0:T(8,128)S(1)} %shard_map.124.refs_3_.refs_0_), channel_id=1, source_target_pairs={{0,8},{2,10},{4,12},{6,14},{8,0},{10,2},{12,4},{14,6},{16,24},{18,... | collective-permute-start | bytes 393224 | tf_op jit(solution)/shard_map/ppermute | solution.py:283
  67.5 7.0 %collective-permute-start.19 = (f32[64,512]{1,0:T(8,128)S(1)}, f32[64,512]{1,0:T(8,128)S(1)}, u32[]{:S(2)}, u32[]{:S(2)}) collective-permute-start(f32[64,512]{1,0:T(8,128)S(1)} %shard_map.126.refs_0_), channel_id=1, source_target_pairs={{0,16},{2,18},{4,20},{6,22},{8,24},{10,26},{12,28},{14,30},{16,0},... | collective-permute-start | bytes 393224 | tf_op jit(solution)/shard_map/ppermute | solution.py:283
  67.9 13.7 %copy-start = (f32[1,1,256,512]{3,2,1,0:T(8,128)S(1)}, f32[1,1,256,512]{3,2,1,0:T(8,128)}, u32[]{:S(2)}) copy-start(f32[1,1,256,512]{3,2,1,0:T(8,128)} %param.11) | copy-start | bytes 1572868
  67.9 13.6 %copy-start.1 = (f32[1,1,256,512]{3,2,1,0:T(8,128)S(1)}, f32[1,1,256,512]{3,2,1,0:T(8,128)}, u32[]{:S(2)}) copy-start(f32[1,1,256,512]{3,2,1,0:T(8,128)} %param.12) | copy-start | bytes 1572868
  68.0 12.4 %collective-permute-start.17 = (f32[264,512]{1,0:T(8,128)S(1)}, f32[264,512]{1,0:T(8,128)S(1)}, u32[]{:S(2)}, u32[]{:S(2)}) collective-permute-start(f32[264,512]{1,0:T(8,128)S(1)} %shard_map.125.refs_2_), channel_id=1, source_target_pairs={{0,1},{1,0},{2,3},{3,2},{4,5},{5,4},{6,7},{7,6},{8,9},{9,8},{10,11... | collective-permute-start | bytes 1622024 | tf_op jit(solution)/shard_map/ppermute | solution.py:298
  74.5 5.0 %collective-permute-start.20 = (f32[64,512]{1,0:T(8,128)S(1)}, f32[64,512]{1,0:T(8,128)S(1)}, u32[]{:S(2)}, u32[]{:S(2)}) collective-permute-start(f32[64,512]{1,0:T(8,128)S(1)} %shard_map.127), channel_id=1, source_target_pairs={{0,4},{2,6},{4,0},{6,2},{8,12},{10,14},{12,8},{14,10},{16,20},{18,... | collective-permute-start | bytes 393224 | tf_op jit(solution)/shard_map/ppermute | solution.py:283
  79.6 1.6 %collective-permute-start.21 = (f32[128,512]{1,0:T(8,128)S(1)}, f32[128,512]{1,0:T(8,128)S(1)}, u32[]{:S(2)}, u32[]{:S(2)}) collective-permute-start(f32[128,512]{1,0:T(8,128)S(1)} %maximum_select_fusion.2), channel_id=1, source_target_pairs={{0,2},{2,0},{4,6},{6,4},{8,10},{10,8},{12,14},{14,12},{16,18},{18,... | collective-permute-start | bytes 786440 | tf_op jit(solution)/shard_map/ppermute | solution.py:283
  80.4 1.2 %collective-permute-start.22 = (f32[16,512]{1,0:T(8,128)S(1)}, f32[16,512]{1,0:T(8,128)S(1)}, u32[]{:S(2)}, u32[]{:S(2)}) collective-permute-start(f32[16,512]{1,0:T(8,128)S(1)} %slice.63), channel_id=1, source_target_pairs={{0,2},{2,0},{4,6},{6,4},{8,10},{10,8},{12,14},{14,12},{16,18},{18,... | collective-permute-start | bytes 98312 | tf_op jit(solution)/shard_map/ppermute | solution.py:283
  82.3 3.7 %collective-permute-start.23 = (f32[1,512]{1,0:T(1,128)S(1)}, f32[1,512]{1,0:T(1,128)S(1)}, u32[]{:S(2)}, u32[]{:S(2)}) collective-permute-start(f32[1,512]{1,0:T(1,128)S(1)} %shard_map.128.refs_4_), channel_id=1, source_target_pairs={{0,1},{1,0},{2,3},{3,2},{4,5},{5,4},{6,7},{7,6},{8,9},{9,8},{10,11... | collective-permute-start | bytes 6152 | tf_op jit(solution)/shard_map/ppermute | solution.py:298
  83.9 2.1 %copy-start.5 = (f32[264,512]{1,0:T(8,128)S(1)}, f32[264,512]{1,0:T(8,128)}, u32[]{:S(2)}) copy-start(f32[264,512]{1,0:T(8,128)} %refs_6_.1) | copy-start | bytes 1622020
  83.9 2.1 %copy-start.6 = (f32[264,512]{1,0:T(8,128)S(1)}, f32[264,512]{1,0:T(8,128)}, u32[]{:S(2)}) copy-start(f32[264,512]{1,0:T(8,128)} %refs_7_.1) | copy-start | bytes 1622020
